TPU v7x, 512 devices: a whole 4x8x8 slice. The times are simulated.
512 devices in a mesh: pair: 64 (over y, x, core), panel: 8 (over z).
Axes of the slice: x: 4, y: 8, z: 8, core: 2. Of those that a mesh axis runs over, the one named last changes fastest.
Arguments:
- amplitudes: bfloat16 [1536, 8, 4096], P(('pair', 'panel')), may hold values from -6 to 6
- integrals: bfloat16 [3, 16384, 4096], P(None, 'pair', 'panel'), may hold values from -0.0546875 to 0.0546875
- residual_in: bfloat16 [1536, 16384], P(('pair', 'panel')), may hold values from -6 to 6
- kept_tiles: int32 [4, 3], replicated, may hold values from 0 to 7, as said below
Outputs:
- residual_out: bfloat16 [1536, 16384], P(('pair', 'panel'))
Inputs may be any that keep to these rules, and one draw needn't show every extreme that they name: `kept_tiles`: each row names 3 different cd tile pairs; the first row names cd tile pairs 0 and 7.
All inputs are finite; a program needn't handle non-finite values.
Results may differ from a plain program's by a relative error of at most 0.0042.
Values may be sent and summed in bfloat16 or wider, within the bound.
No kernel may reach another device: no remote copies, remote signals or barrier semaphores. Data moves between devices by JAX's collectives and lax.ppermute only.
A program may use at most 128 MiB of HBM per device.

v0:
```python
import jax
import jax.numpy as jnp
from jax import lax
from jax.sharding import PartitionSpec as P


def shards(amplitudes, integrals, residual_in, kept_tiles):
    pair_count = lax.axis_size("pair")
    per_tile = pair_count // kept_tiles.shape[0]
    keep_count = kept_tiles.shape[1]
    width = amplitudes.shape[2]
    group_rows = amplitudes.shape[0] * pair_count
    peer_tiles = kept_tiles[jnp.arange(pair_count) // per_tile]
    outgoing = jnp.take(amplitudes, peer_tiles, axis=1)
    incoming = lax.all_to_all(outgoing, "pair", split_axis=1, concat_axis=0, tiled=True)
    incoming = incoming.reshape(group_rows, keep_count, width)
    total = jnp.einsum(
        "mkc,kac->ma",
        incoming,
        lax.all_gather(integrals, "panel", axis=2, tiled=True),
        preferred_element_type=jnp.float32,
    )
    ladder = total.astype(jnp.bfloat16)
    returned = lax.all_to_all(ladder, "pair", split_axis=0, concat_axis=1, tiled=True)
    return (residual_in.astype(jnp.float32) + returned.astype(jnp.float32)).astype(jnp.bfloat16)


def solution(mesh):
    in_specs = (
        P(("pair", "panel"), None, None),
        P(None, "pair", "panel"),
        P(("pair", "panel"), None),
        P(),
    )
    out_specs = P(("pair", "panel"), None)
    return jax.shard_map(shards, mesh=mesh, in_specs=in_specs, out_specs=out_specs, check_vma=False)
```

profile of v0, /device:TPU:1, one launch (start us, length us, event | category | flops | bytes accessed | tf_op | source)
XLA Modules:
  0.0 241.3 jit_solution(13925093936344972353)
XLA Ops:
  6.5 0.0 copy-start
  6.5 0.0 all-gather.2.cloned.1.call-start
  6.5 0.7 all-gather.2.cloned.1.call-update
  7.3 1.3 gather_fusion
  8.6 0.1 reshape.82
  8.7 0.0 copy-done
  8.7 21.1 %gather_fusion.1 = bf16[192,3,4096]{2,0,1:T(8,128)(2,1)} fusion(bf16[3,8,4096]{2,1,0:T(8,128)(2,1)S(1)} %copy-done, s32[1024]{0:T(1024)S(1)} %pad_clamp_fusion), kind=kCustom, calls=%fused_computation.1 | custom fusion | bytes 9437952 | tf_op jit(solution)/shard_map/jit(_take)/gather | solution.py:14
  29.8 10.0 %reshape.85 = bf16[64,3,3,4096]{3,1,0,2:T(4,128)(2,1)} reshape(bf16[192,3,4096]{2,0,1:T(8,128)(2,1)} %gather_fusion.1) | data formatting | bytes 9437184 | tf_op jit(solution)/shard_map/jit(_take)/gather | solution.py:14
  39.8 8.4 %select_bitcast_fusion = bf16[3,64,3,4096]{3,2,1,0:T(4,128)(2,1)} fusion(bf16[64,3,3,4096]{3,1,0,2:T(4,128)(2,1)} %reshape.85, pred[64,3]{1,0:T(8,128)(4,1)S(1)} %compare_and_fusion), kind=kLoop, calls=%fused_computation.2 | loop fusion | flops 2359296 | bytes 9437376 | tf_op jit(solution)/shard_map/jit(_take)/select_n | solution.py:14
  48.3 5.9 %copy.9 = bf16[3,64,3,4096]{3,2,0,1:T(4,128)(2,1)S(1)} copy(bf16[3,64,3,4096]{3,2,1,0:T(4,128)(2,1)} %select_bitcast_fusion) | data formatting | bytes 9437184 | tf_op jit(solution)/shard_map/jit(_take)/select_n | solution.py:14
  54.2 151.1 %all_to_all.28 = bf16[3,64,3,4096]{3,2,0,1:T(4,128)(2,1)} all-to-all(bf16[3,64,3,4096]{3,2,0,1:T(4,128)(2,1)S(1)} %copy.9), channel_id=1, replica_groups=mesh['pair'=64,'panel'=8] {'pair'}, dimensions={1} | all-to-all | bytes 9437184 | tf_op jit(solution)/shard_map/all_to_all | solution.py:15
  205.3 0.0 all-gather.2.cloned.1.call-done
  205.3 0.0 copy-start.1
  205.3 10.5 %fusion.5 = bf16[192,256]{1,0:T(8,128)(2,1)S(1)} fusion(bf16[3,256,4096]{2,1,0:T(8,128)(2,1)} %all-gather.2.cloned.1.call-done, bf16[192,3,4096]{2,1,0:T(4,128)(2,1)} %bitcast.23), kind=kOutput, calls=%fused_computation.6 | convolution fusion | flops 1208008704 | bytes 11108352 | tf_op jit(solution)/shard_map/mkc,kac->ma/dot_general | solution.py:17
  215.7 0.1 all_to_all.24
  215.8 17.9 %all_to_all.29 = bf16[64,3,256]{2,1,0:T(4,128)(2,1)S(1)} all-to-all(bf16[64,3,256]{2,1,0:T(4,128)(2,1)S(1)} %all_to_all.24), channel_id=1, replica_groups=mesh['pair'=64,'panel'=8] {'pair'}, dimensions={0} | all-to-all | bytes 196608 | tf_op jit(solution)/shard_map/all_to_all | solution.py:24
  233.8 0.0 copy-done.1
  233.8 0.7 add_convert_fusion
  (6 shorter events, 0.1 us)
Async XLA Ops:
  6.5 2.2 copy-start
  6.5 198.7 %all-gather.2.cloned.1.call-start = ((), (), s32[]{:S(2)}) async-start(), calls=%async_computation.2 | async-start | bytes 7077888 | tf_op jit(solution)/shard_map/all_gather | solution.py:20
  205.3 28.5 %copy-start.1 = (bf16[3,16384]{1,0:T(4,128)(2,1)S(1)}, bf16[3,16384]{1,0:T(4,128)(2,1)}, u32[]{:S(2)}) copy-start(bf16[3,16384]{1,0:T(4,128)(2,1)} %param.6) | copy-start | bytes 294916
Sparse Core Ops, SparseCore 0:
  9.4 83.3 all-gather.1
where the time goes:
time: 242 us; the launch traced here: 241 us
  blocking collectives  169 us (70%)
  local copies, waits for them, and re-layouts  38.5 us (16%)
  between operations  13.5 us (6%)
  matrix products  10.5 us (4%)
  other arithmetic  9.23 us (4%)
    all_to_all x1, blocking collectives, shards(): lax.all_to_all(outgoing, 'pair', split_axis=1, concat_axis=0, tiled=True)  151 us
    gather x2, local copies, waits for them, and re-layouts, shards(): outgoing = jnp.take(amplitudes, peer_tiles, axis=1)  31.1 us
    all_to_all x1, blocking collectives, shards(): lax.all_to_all(ladder, 'pair', split_axis=0, concat_axis=1, tiled=True)  17.9 us
    dot_general x1, matrix products, shards(): jnp.einsum('mkc,kac->ma', incoming, lax.all_gather(integrals, 'panel', ax...  10.5 us
    select_n x2, other arithmetic, shards(): outgoing = jnp.take(amplitudes, peer_tiles, axis=1)  8.45 us
    select_n x2, local copies, waits for them, and re-layouts, shards(): outgoing = jnp.take(amplitudes, peer_tiles, axis=1)  6.04 us
  transfers between devices with their start and end apart: 1, of which 0 were waited for; matrix products, arithmetic and copies ran while one was open for 19% of the time, Pallas kernels for 0%

commit v1 on v0

v1 whole, which is shorter than its diff:
```python
import jax
import jax.numpy as jnp
from jax import lax
from jax.sharding import Mesh, PartitionSpec as P

Y, X, CORE, Z = 8, 4, 2, 8


def shards(amplitudes, integrals, residual_in, kept_tiles):
    rows, tiles, width = amplitudes.shape
    keep = kept_tiles.shape[1]
    share = width // Z
    panel = lax.all_gather(integrals, ("x", "c"), axis=1, tiled=True)
    pick = jax.nn.one_hot(kept_tiles, tiles, dtype=jnp.bfloat16)
    pick = jnp.repeat(pick, Y // kept_tiles.shape[0], axis=0)
    outgoing = jnp.einsum(
        "ykt,rtzc->yzrkc",
        pick,
        amplitudes.reshape(rows, tiles, Z, share),
        preferred_element_type=jnp.float32,
    ).astype(jnp.bfloat16)
    outgoing = outgoing.reshape(Y * Z, rows, keep * share)
    incoming = lax.all_to_all(outgoing, ("y", "z"), split_axis=0, concat_axis=0, tiled=True)
    incoming = incoming.reshape(Y * Z * rows, keep, share)
    partial = jnp.einsum("mkc,kac->ma", incoming, panel, preferred_element_type=jnp.float32)
    partial = partial.astype(jnp.bfloat16).reshape(Y * Z, rows, -1)
    returned = lax.all_to_all(partial, ("y", "z"), split_axis=0, concat_axis=0, tiled=True)
    returned = returned.reshape(Y, Z, rows, -1).astype(jnp.float32)
    ladder = jnp.sum(returned, axis=1).astype(jnp.bfloat16)
    ladder = jnp.transpose(ladder, (1, 0, 2)).reshape(residual_in.shape)
    return (residual_in.astype(jnp.float32) + ladder.astype(jnp.float32)).astype(jnp.bfloat16)


def solution(mesh):
    fine = Mesh(mesh.devices.reshape(Y, X, CORE, Z), ("y", "x", "c", "z"))
    owner = ("y", "x", "c", "z")
    in_specs = (
        P(owner, None, None),
        P(None, ("y", "x", "c"), "z"),
        P(owner, None),
        P(),
    )
    return jax.shard_map(
        shards, mesh=fine, in_specs=in_specs, out_specs=P(owner, None), check_vma=False
    )
```

time: 242 us -> 118 us (0.49)
  the two profiles are of different devices: /device:TPU:1 before, /device:TPU:16 now
where the time goes in v1:
time: 118 us
  blocking collectives  85.1 us (72%)
  between operations  13.5 us (11%)
  waiting for transfers between devices  9.41 us (8%)
  matrix products  5.27 us (4%)
  local copies, waits for them, and re-layouts  3.24 us (3%)
  other arithmetic  1.36 us (1%)
    all_to_all x1, blocking collectives, shards(): lax.all_to_all(partial, ('y', 'z'), split_axis=0, concat_axis=0, tiled=True)  43.9 us
    all_to_all x1, blocking collectives, shards(): lax.all_to_all(outgoing, ('y', 'z'), split_axis=0, concat_axis=0, tiled=T...  41.1 us
    all_gather x1, waiting for transfers between devices, shards(): panel = lax.all_gather(integrals, ('x', 'c'), axis=1, tiled=True)  8.7 us
    dot_general x1, matrix products, shards(): jnp.einsum('mkc,kac->ma', incoming, panel, preferred_element_type=jnp.flo...  4.98 us
  transfers between devices with their start and end apart: 1, of which 1 were waited for; matrix products, arithmetic and copies ran while one was open for 3% of the time, Pallas kernels for 0%

profile of v1, /device:TPU:16, one launch (start us, length us, event | category | flops | bytes accessed | tf_op | source)
XLA Modules:
  0.0 117.8 jit_solution(2962381361042000847)
XLA Ops:
  6.5 0.0 copy-start
  6.5 0.0 all-gather.2.cloned.1.call-start
  6.5 0.7 all-gather.2.cloned.1.call-update
  7.3 0.8 copy.10
  8.0 0.1 fusion.3
  8.1 0.0 copy-done
  8.1 0.3 fusion.1
  8.4 0.5 copy.15
  8.9 0.7 reshape.32
  9.7 41.1 %all_to_all.10 = bf16[64,3,1536]{2,1,0:T(4,128)(2,1)S(1)} all-to-all(bf16[64,3,1536]{2,1,0:T(4,128)(2,1)S(1)} %reshape.32), channel_id=1, replica_groups=mesh['y'=8,'x'=4,'c'=2,'z'=8] {'y','z'}, dimensions={0} | all-to-all | bytes 1179648 | tf_op jit(solution)/shard_map/all_to_all | solution.py:23
  50.8 0.7 reshape.25
  51.5 0.0 copy-start.1
  51.5 8.7 %all-gather.2.cloned.1.call-done = bf16[3,2048,512]{2,1,0:T(8,128)(2,1)} async-done(((bf16[3,256,512]{2,1,0:T(8,128)(2,1)}), bf16[3,2048,512]{2,1,0:T(8,128)(2,1)}) %all-gather.2.cloned.1.call-update) | async-done | bytes 6291472 | tf_op jit(solution)/shard_map/all_gather | solution.py:13
  60.2 5.0 %fusion = bf16[192,2048]{1,0:T(8,128)(2,1)S(1)} fusion(bf16[3,2048,512]{2,1,0:T(8,128)(2,1)} %all-gather.2.cloned.1.call-done, bf16[192,3,512]{2,1,0:T(4,128)(2,1)S(1)} %reshape.25), kind=kOutput, calls=%fused_computation.1 | convolution fusion | flops 1208352768 | bytes 7667712 | tf_op jit(solution)/shard_map/mkc,kac->ma/dot_general | solution.py:25
  65.2 0.5 reshape.26
  65.7 43.9 %all_to_all.11 = bf16[64,3,2048]{2,1,0:T(4,128)(2,1)S(1)} all-to-all(bf16[64,3,2048]{2,1,0:T(4,128)(2,1)S(1)} %reshape.26), channel_id=1, replica_groups=mesh['y'=8,'x'=4,'c'=2,'z'=8] {'y','z'}, dimensions={0} | all-to-all | bytes 1572864 | tf_op jit(solution)/shard_map/all_to_all | solution.py:27
  109.7 0.5 bitcast_reduce_fusion
  110.2 0.0 copy-done.1
  110.2 0.7 add_convert_fusion
  (2 shorter events, 0.0 us)
Async XLA Ops:
  6.5 1.6 %copy-start = (bf16[3,8,4096]{2,1,0:T(8,128)(2,1)S(1)}, bf16[3,8,4096]{2,1,0:T(8,128)(2,1)}, u32[]{:S(2)}) copy-start(bf16[3,8,4096]{2,1,0:T(8,128)(2,1)} %param.4) | copy-start | bytes 589828
  6.5 53.7 %all-gather.2.cloned.1.call-start = ((), (), s32[]{:S(2)}) async-start(), calls=%async_computation.2 | async-start | bytes 7077888 | tf_op jit(solution)/shard_map/all_gather | solution.py:13
  51.5 58.7 %copy-start.1 = (bf16[3,16384]{1,0:T(4,128)(2,1)S(1)}, bf16[3,16384]{1,0:T(4,128)(2,1)}, u32[]{:S(2)}) copy-start(bf16[3,16384]{1,0:T(4,128)(2,1)} %param.6) | copy-start | bytes 294916
Sparse Core Ops, SparseCore 0:
  9.5 50.6 all-gather.1

commit v2 on v1

v2 whole, which is shorter than its diff:
```python
import jax
import jax.numpy as jnp
from jax import lax
from jax.sharding import Mesh, PartitionSpec as P

Y, X, CORE, Z = 8, 4, 2, 8
LANES = 128
SWAP = ((0, 1), (1, 0))
UP = tuple((i, (i + 1) % X) for i in range(X))
DOWN = tuple((i, (i - 1) % X) for i in range(X))
ACROSS = tuple((i, (i + 2) % X) for i in range(X))


def shards(amplitudes, integrals, residual_in, kept_tiles):
    rows, tiles, width = amplitudes.shape
    keep = kept_tiles.shape[1]
    share = width // Z
    block = integrals.shape[1]
    x = lax.axis_index("x")
    core = lax.axis_index("c")

    below = lax.ppermute(integrals, "x", UP)
    above = lax.ppermute(integrals, "x", DOWN)
    far = lax.ppermute(integrals, "x", ACROSS)

    pick = jax.nn.one_hot(kept_tiles, tiles, dtype=jnp.bfloat16)
    pick = jnp.repeat(pick, Y // kept_tiles.shape[0], axis=0)
    outgoing = jnp.einsum(
        "ykt,rtzc->yzrkc",
        pick,
        amplitudes.reshape(rows, tiles, Z, share),
        preferred_element_type=jnp.float32,
    ).astype(jnp.bfloat16)
    outgoing = outgoing.reshape(Y * Z, rows * keep, share // LANES, LANES)
    mine = lax.all_to_all(outgoing, ("y", "z"), split_axis=0, concat_axis=0, tiled=True)
    mine = mine.reshape(Y * Z, rows, keep, share)
    theirs = lax.ppermute(mine, "c", SWAP)

    left = jnp.stack([mine, theirs], axis=2)

    def product(right):
        out = jnp.einsum(
            "drosc,sac->droa", left, right, preferred_element_type=jnp.float32
        )
        return out.astype(jnp.bfloat16)

    pieces = [product(p) for p in (integrals, above, far, below)]
    partial = jnp.concatenate(pieces, axis=-1)
    returned = lax.all_to_all(partial, ("y", "z"), split_axis=0, concat_axis=0, tiled=True)
    returned = returned.reshape(Y, Z, rows, CORE, X * block).astype(jnp.float32)
    ladder = jnp.sum(returned, axis=1).astype(jnp.bfloat16)
    ladder = ladder.reshape(Y, rows, CORE, X, block)
    own = ladder[:, :, 0]
    other = lax.ppermute(ladder[:, :, 1], "c", SWAP)
    low = jnp.where(core == 0, own, other)
    high = jnp.where(core == 0, other, own)
    both = jnp.stack([low, high], axis=3)
    both = jnp.roll(both, x, axis=2)
    both = jnp.transpose(both, (1, 0, 2, 3, 4)).reshape(residual_in.shape)
    return (residual_in.astype(jnp.float32) + both.astype(jnp.float32)).astype(jnp.bfloat16)


def solution(mesh):
    fine = Mesh(mesh.devices.reshape(Y, X, CORE, Z), ("y", "x", "c", "z"))
    owner = ("y", "x", "c", "z")
    in_specs = (
        P(owner, None, None),
        P(None, ("y", "x", "c"), "z"),
        P(owner, None),
        P(),
    )
    return jax.shard_map(
        shards, mesh=fine, in_specs=in_specs, out_specs=P(owner, None), check_vma=False
    )
```

time: 118 us -> 124 us (1.051)
  the two profiles are of different devices: /device:TPU:16 before, /device:TPU:1 now
where the time goes in v2:
time: 124 us; the launch traced here: 123 us
  blocking collectives  60.6 us (49%)
  waiting for transfers between devices  26.9 us (22%)
  starting transfers between devices  22 us (18%)
  matrix products  7.03 us (6%)
  local copies, waits for them, and re-layouts  3.9 us (3%)
  other arithmetic  1.81 us (1%)
    all_to_all x1, blocking collectives, shards(): lax.all_to_all(outgoing, ('y', 'z'), split_axis=0, concat_axis=0, tiled=T...  34.4 us
    all_to_all x1, blocking collectives, shards(): lax.all_to_all(partial, ('y', 'z'), split_axis=0, concat_axis=0, tiled=True)  26.2 us
    ppermute x1, waiting for transfers between devices, shards(): far = lax.ppermute(integrals, 'x', ACROSS)  16 us
    ppermute x1, waiting for transfers between devices, shards(): below = lax.ppermute(integrals, 'x', UP)  9.99 us
    dot_general x4, matrix products, product(): jnp.einsum('drosc,sac->droa', left, right, preferred_element_type=jnp.flo...  6.75 us
    ppermute x1, starting transfers between devices, shards(): theirs = lax.ppermute(mine, 'c', SWAP)  5.76 us
    ppermute x1, starting transfers between devices, shards(): other = lax.ppermute(ladder[:, :, 1], 'c', SWAP)  5.74 us
    ppermute x1, starting transfers between devices, shards(): far = lax.ppermute(integrals, 'x', ACROSS)  4.36 us
  transfers between devices with their start and end apart: 5, of which 3 were waited for; matrix products, arithmetic and copies ran while one was open for 4% of the time, Pallas kernels for 0%

profile of v2, /device:TPU:1, one launch (start us, length us, event | category | flops | bytes accessed | tf_op | source)
XLA Modules:
  0.0 122.5 jit_solution(10293121005933511363)
XLA Ops:
  0.0 0.0 copy-start
  0.0 0.8 copy.25
  0.8 0.1 fusion.12
  0.9 0.0 copy-done
  0.9 0.3 fusion
  1.2 0.5 copy.45
  1.7 0.5 reshape.39
  2.3 34.4 %all_to_all.10 = bf16[64,9,4,128]{3,2,1,0:T(4,128)(2,1)S(1)} all-to-all(bf16[64,9,4,128]{3,2,1,0:T(4,128)(2,1)S(1)} %reshape.39), channel_id=1, replica_groups=mesh['y'=8,'x'=4,'c'=2,'z'=8] {'y','z'}, dimensions={0} | all-to-all | bytes 1179648 | tf_op jit(solution)/shard_map/all_to_all | solution.py:35
  36.7 0.2 copy.28
  37.0 0.0 copy-start.2
  37.0 0.2 reshape.25
  37.2 5.8 %collective-permute-start = (bf16[64,3,3,512]{3,0,2,1:T(8,128)(2,1)S(1)}, bf16[64,3,3,512]{3,0,2,1:T(8,128)(2,1)}, u32[]{:S(2)}, u32[]{:S(2)}) collective-permute-start(bf16[64,3,3,512]{3,0,2,1:T(8,128)(2,1)S(1)} %reshape.25), channel_id=1, source_target_pairs={{0,8},{8,0},{1,9},{9,1},{2,10},{10,2},{3,11},{11,3},{4,12},{12,4},... | collective-permute-start | bytes 1769480 | tf_op jit(solution)/shard_map/ppermute | solution.py:37
  43.0 0.0 copy-done.2
  43.0 3.1 %collective-permute-start.3 = (bf16[3,256,512]{2,1,0:T(8,128)(2,1)S(1)}, bf16[3,256,512]{2,1,0:T(8,128)(2,1)}, u32[]{:S(2)}, u32[]{:S(2)}) collective-permute-start(bf16[3,256,512]{2,1,0:T(8,128)(2,1)S(1)} %copy-done.2), channel_id=1, source_target_pairs={{0,16},{16,32},{32,48},{48,0},{1,17},{17,33},{33,49},{49,1},{2,18}... | collective-permute-start | bytes 2359304 | tf_op jit(solution)/shard_map/ppermute | solution.py:22
  46.1 4.4 %collective-permute-start.2 = (bf16[3,256,512]{2,1,0:T(8,128)(2,1)S(1)}, bf16[3,256,512]{2,1,0:T(8,128)(2,1)}, u32[]{:S(2)}, u32[]{:S(2)}) collective-permute-start(bf16[3,256,512]{2,1,0:T(8,128)(2,1)S(1)} %copy-done.2), channel_id=1, source_target_pairs={{0,32},{16,48},{32,0},{48,16},{1,33},{17,49},{33,1},{49,17},{2,34}... | collective-permute-start | bytes 2359304 | tf_op jit(solution)/shard_map/ppermute | solution.py:24
  50.5 3.1 %collective-permute-start.1 = (bf16[3,256,512]{2,1,0:T(8,128)(2,1)S(1)}, bf16[3,256,512]{2,1,0:T(8,128)(2,1)S(1)}, u32[]{:S(2)}, u32[]{:S(2)}) collective-permute-start(bf16[3,256,512]{2,1,0:T(8,128)(2,1)S(1)} %copy-done.2), channel_id=1, source_target_pairs={{0,48},{16,0},{32,16},{48,32},{1,49},{17,1},{33,17},{49,33},{2,50}... | collective-permute-start | bytes 2359304 | tf_op jit(solution)/shard_map/ppermute | solution.py:23
  53.5 0.2 stack_reshape.3
  53.8 0.0 collective-permute-done
  53.8 1.6 %fusion.1 = bf16[64,3,2,256]{3,0,2,1:T(8,128)(2,1)S(1)} fusion(bf16[3,256,512]{2,1,0:T(8,128)(2,1)S(1)} %copy-done.2, bf16[64,3,1,3,512]{4,0,3,2,1:T(8,128)(2,1)} %bitcast.6, bf16[64,3,1,3,512]{4,0,3,2,1:T(8,128)(2,1)S(1)} %stack_reshape.3), kind=kOutput, calls=%fused_computation.7 | convolution fusion | flops 302678016 | bytes 2162688 | tf_op jit(solution)/shard_map/drosc,sac->droa/dot_general | solution.py:42
  55.4 10.0 %collective-permute-done.3 = bf16[3,256,512]{2,1,0:T(8,128)(2,1)} collective-permute-done((bf16[3,256,512]{2,1,0:T(8,128)(2,1)S(1)}, bf16[3,256,512]{2,1,0:T(8,128)(2,1)}, u32[]{:S(2)}, u32[]{:S(2)}) %collective-permute-start.3) | collective-permute-done | bytes 786464 | tf_op jit(solution)/shard_map/ppermute | solution.py:22
  65.3 1.8 %fusion.4 = bf16[64,3,2,256]{3,0,2,1:T(8,128)(2,1)S(1)} fusion(bf16[3,256,512]{2,1,0:T(8,128)(2,1)} %collective-permute-done.3, bf16[64,3,1,3,512]{4,0,3,2,1:T(8,128)(2,1)} %bitcast.6, bf16[64,3,1,3,512]{4,0,3,2,1:T(8,128)(2,1)S(1)} %stack_reshape.3), kind=kOutput, calls=%fused_computation.10 | convolution fusion | flops 302678016 | bytes 2162688 | tf_op jit(solution)/shard_map/drosc,sac->droa/dot_general | solution.py:42
  67.2 16.0 %collective-permute-done.2 = bf16[3,256,512]{2,1,0:T(8,128)(2,1)} collective-permute-done((bf16[3,256,512]{2,1,0:T(8,128)(2,1)S(1)}, bf16[3,256,512]{2,1,0:T(8,128)(2,1)}, u32[]{:S(2)}, u32[]{:S(2)}) %collective-permute-start.2) | collective-permute-done | bytes 786464 | tf_op jit(solution)/shard_map/ppermute | solution.py:24
  83.2 1.8 %fusion.3 = bf16[64,3,2,256]{3,0,2,1:T(8,128)(2,1)S(1)} fusion(bf16[3,256,512]{2,1,0:T(8,128)(2,1)} %collective-permute-done.2, bf16[64,3,1,3,512]{4,0,3,2,1:T(8,128)(2,1)} %bitcast.6, bf16[64,3,1,3,512]{4,0,3,2,1:T(8,128)(2,1)S(1)} %stack_reshape.3), kind=kOutput, calls=%fused_computation.9 | convolution fusion | flops 302678016 | bytes 2162688 | tf_op jit(solution)/shard_map/drosc,sac->droa/dot_general | solution.py:42
  85.0 0.0 collective-permute-done.1
  85.0 1.6 %fusion.2 = bf16[64,3,2,256]{3,0,2,1:T(8,128)(2,1)S(1)} fusion(bf16[3,256,512]{2,1,0:T(8,128)(2,1)S(1)} %collective-permute-done.1, bf16[64,3,1,3,512]{4,0,3,2,1:T(8,128)(2,1)} %bitcast.6, bf16[64,3,1,3,512]{4,0,3,2,1:T(8,128)(2,1)S(1)} %stack_reshape.3), kind=kOutput, calls=%fused_computation.8 | convolution fusion | flops 302678016 | bytes 2162688 | tf_op jit(solution)/shard_map/drosc,sac->droa/dot_general | solution.py:42
  86.6 0.1 pad_maximum_fusion.1
  86.7 0.8 copy.30
  87.5 26.2 %all_to_all.11 = bf16[64,3,2,1024]{3,2,1,0:T(2,128)(2,1)S(1)} all-to-all(bf16[64,3,2,1024]{3,2,1,0:T(2,128)(2,1)S(1)} %copy.30), channel_id=1, replica_groups=mesh['y'=8,'x'=4,'c'=2,'z'=8] {'y','z'}, dimensions={0} | all-to-all | bytes 1572864 | tf_op jit(solution)/shard_map/all_to_all | solution.py:49
  113.7 0.7 bitcast_reduce_fusion
  114.4 0.1 reshape.40
  114.5 0.0 copy-start.1
  114.6 5.7 %collective-permute-start.4 = (bf16[8,3,4,256]{3,2,0,1:T(4,128)(2,1)S(1)}, bf16[8,3,4,256]{3,2,0,1:T(4,128)(2,1)S(1)}, u32[]{:S(2)}, u32[]{:S(2)}) collective-permute-start(bf16[8,3,4,256]{3,2,0,1:T(4,128)(2,1)S(1)} %bitcast.75), channel_id=1, source_target_pairs={{0,8},{8,0},{1,9},{9,1},{2,10},{10,2},{3,11},{11,3},{4,12},{12,4},... | collective-permute-start | bytes 147464 | tf_op jit(solution)/shard_map/ppermute | solution.py:54
  120.3 0.8 collective-permute-done.4
  121.2 0.2 convert_bitcast_fusion
  121.4 0.2 copy.35
  121.6 0.2 reshape.28
  121.8 0.0 copy-done.1
  121.8 0.7 add_convert_fusion
  (4 shorter events, 0.1 us)
Async XLA Ops:
  0.0 0.9 copy-start
  37.0 6.0 %copy-start.2 = (bf16[3,256,512]{2,1,0:T(8,128)(2,1)S(1)}, bf16[3,256,512]{2,1,0:T(8,128)(2,1)}, u32[]{:S(2)}) copy-start(bf16[3,256,512]{2,1,0:T(8,128)(2,1)} %param.5) | copy-start | bytes 2359300
  37.2 16.6 %collective-permute-start = (bf16[64,3,3,512]{3,0,2,1:T(8,128)(2,1)S(1)}, bf16[64,3,3,512]{3,0,2,1:T(8,128)(2,1)}, u32[]{:S(2)}, u32[]{:S(2)}) collective-permute-start(bf16[64,3,3,512]{3,0,2,1:T(8,128)(2,1)S(1)} %reshape.25), channel_id=1, source_target_pairs={{0,8},{8,0},{1,9},{9,1},{2,10},{10,2},{3,11},{11,3},{4,12},{12,4},... | collective-permute-start | bytes 1769480 | tf_op jit(solution)/shard_map/ppermute | solution.py:37
  43.0 22.4 %collective-permute-start.3 = (bf16[3,256,512]{2,1,0:T(8,128)(2,1)S(1)}, bf16[3,256,512]{2,1,0:T(8,128)(2,1)}, u32[]{:S(2)}, u32[]{:S(2)}) collective-permute-start(bf16[3,256,512]{2,1,0:T(8,128)(2,1)S(1)} %copy-done.2), channel_id=1, source_target_pairs={{0,16},{16,32},{32,48},{48,0},{1,17},{17,33},{33,49},{49,1},{2,18}... | collective-permute-start | bytes 2359304 | tf_op jit(solution)/shard_map/ppermute | solution.py:22
  46.1 37.1 %collective-permute-start.2 = (bf16[3,256,512]{2,1,0:T(8,128)(2,1)S(1)}, bf16[3,256,512]{2,1,0:T(8,128)(2,1)}, u32[]{:S(2)}, u32[]{:S(2)}) collective-permute-start(bf16[3,256,512]{2,1,0:T(8,128)(2,1)S(1)} %copy-done.2), channel_id=1, source_target_pairs={{0,32},{16,48},{32,0},{48,16},{1,33},{17,49},{33,1},{49,17},{2,34}... | collective-permute-start | bytes 2359304 | tf_op jit(solution)/shard_map/ppermute | solution.py:24
  50.5 34.5 %collective-permute-start.1 = (bf16[3,256,512]{2,1,0:T(8,128)(2,1)S(1)}, bf16[3,256,512]{2,1,0:T(8,128)(2,1)S(1)}, u32[]{:S(2)}, u32[]{:S(2)}) collective-permute-start(bf16[3,256,512]{2,1,0:T(8,128)(2,1)S(1)} %copy-done.2), channel_id=1, source_target_pairs={{0,48},{16,0},{32,16},{48,32},{1,49},{17,1},{33,17},{49,33},{2,50}... | collective-permute-start | bytes 2359304 | tf_op jit(solution)/shard_map/ppermute | solution.py:23
  114.5 7.3 %copy-start.1 = (bf16[3,16384]{1,0:T(4,128)(2,1)S(1)}, bf16[3,16384]{1,0:T(4,128)(2,1)}, u32[]{:S(2)}) copy-start(bf16[3,16384]{1,0:T(4,128)(2,1)} %param.6) | copy-start | bytes 294916
  114.6 6.6 %collective-permute-start.4 = (bf16[8,3,4,256]{3,2,0,1:T(4,128)(2,1)S(1)}, bf16[8,3,4,256]{3,2,0,1:T(4,128)(2,1)S(1)}, u32[]{:S(2)}, u32[]{:S(2)}) collective-permute-start(bf16[8,3,4,256]{3,2,0,1:T(4,128)(2,1)S(1)} %bitcast.75), channel_id=1, source_target_pairs={{0,8},{8,0},{1,9},{9,1},{2,10},{10,2},{3,11},{11,3},{4,12},{12,4},... | collective-permute-start | bytes 147464 | tf_op jit(solution)/shard_map/ppermute | solution.py:54

commit v3 on v1

v3 whole, which is shorter than its diff:
```python
import jax
import jax.numpy as jnp
from jax import lax
from jax.experimental import pallas as pl
from jax.experimental.pallas import tpu as pltpu
from jax.sharding import Mesh, PartitionSpec as P

Y, X, CORE, Z = 8, 4, 2, 8
LANES = 128
SWAP = ((0, 1), (1, 0))
UP = tuple((i, (i + 1) % X) for i in range(X))
DOWN = tuple((i, (i - 1) % X) for i in range(X))
ACROSS = tuple((i, (i + 2) % X) for i in range(X))
VMEM = pl.BlockSpec(memory_space=pltpu.VMEM)
SMEM = pl.BlockSpec(memory_space=pltpu.SMEM)
GRANT = 32 * 1024 * 1024


def pick_kernel(kept_ref, amplitudes_ref, out_ref):
    tiles, keep = kept_ref.shape
    rows = amplitudes_ref.shape[0]
    repeat = Y // tiles
    for a in range(tiles):
        for k in range(keep):
            tile = kept_ref[a, k]
            for r in range(rows):
                piece = amplitudes_ref[r, tile]
                for i in range(repeat):
                    out_ref[a * repeat + i, :, r * keep + k] = piece


def pick(kept_tiles, amplitudes):
    rows, tiles, width = amplitudes.shape
    keep = kept_tiles.shape[1]
    split = amplitudes.reshape(rows, tiles, Z, width // Z // LANES, LANES)
    shape = (Y, Z, rows * keep, width // Z // LANES, LANES)
    return pl.pallas_call(
        pick_kernel,
        out_shape=jax.ShapeDtypeStruct(shape, amplitudes.dtype),
        in_specs=[SMEM, VMEM],
        out_specs=VMEM,
        cost_estimate=pl.CostEstimate(flops=10**11, bytes_accessed=10**6, transcendentals=0),
        compiler_params=pltpu.CompilerParams(vmem_limit_bytes=GRANT),
    )(kept_tiles, split)


def product_kernel(where_ref, left_ref, *refs):
    rights, out_ref = refs[:-1], refs[-1]
    peers, both, chunks, lanes = left_ref.shape
    halves, rows, _, columns = out_ref.shape
    keep, block, share = rights[0].shape
    left = [
        jnp.concatenate(
            [
                jnp.concatenate([left_ref[:, r * keep + k, c] for c in range(chunks)], axis=1)
                for r in range(rows)
            ],
            axis=0,
        )
        for k in range(keep)
    ]
    for j, right_ref in enumerate(rights):
        total = jnp.zeros((rows * peers, block), jnp.float32)
        for k in range(keep):
            total += lax.dot_general(
                left[k],
                right_ref[k],
                (((1,), (1,)), ((), ())),
                preferred_element_type=jnp.float32,
            )
        place = where_ref[j]
        per_half = columns // block
        start = pl.multiple_of(lax.rem(place, per_half) * block, block)
        out_ref[lax.div(place, per_half), :, :, pl.ds(start, block)] = total.astype(jnp.bfloat16).reshape(rows, peers, block)


def product(where, left, rights):
    peers = left.shape[0]
    rows = left.shape[1] // rights[0].shape[0]
    columns = sum(r.shape[1] for r in rights) // 2
    return pl.pallas_call(
        product_kernel,
        out_shape=jax.ShapeDtypeStruct((2, rows, peers, columns), jnp.bfloat16),
        in_specs=[SMEM] + [VMEM] * (1 + len(rights)),
        out_specs=VMEM,
        cost_estimate=pl.CostEstimate(flops=1000, bytes_accessed=1000, transcendentals=0),
        compiler_params=pltpu.CompilerParams(vmem_limit_bytes=GRANT),
    )(where, left, *rights)


def shards(amplitudes, integrals, residual_in, kept_tiles):
    rows, tiles, width = amplitudes.shape
    keep = kept_tiles.shape[1]
    share = width // Z
    x = lax.axis_index("x")
    core = lax.axis_index("c")

    below = lax.ppermute(integrals, "x", UP)
    above = lax.ppermute(integrals, "x", DOWN)
    far = lax.ppermute(integrals, "x", ACROSS)

    outgoing = pick(kept_tiles, amplitudes)
    outgoing = outgoing.reshape(Y * Z, rows * keep, share // LANES, LANES)
    mine = lax.all_to_all(outgoing, ("y", "z"), split_axis=0, concat_axis=0, tiled=True)

    ring = [integrals, above, far, below]
    rights = ring + [lax.ppermute(r, "c", SWAP) for r in ring]
    steps = jnp.arange(X)
    blocks = lax.rem(x + steps, X) * CORE
    where = jnp.concatenate([blocks + core, blocks + 1 - core])
    partial = product(where.astype(jnp.int32), mine, rights)
    partial = partial.transpose(2, 1, 0, 3)
    returned = lax.all_to_all(partial, ("y", "z"), split_axis=0, concat_axis=0, tiled=True)
    returned = returned.reshape(Y, Z, rows, -1).astype(jnp.float32)
    ladder = jnp.sum(returned, axis=1).astype(jnp.bfloat16)
    ladder = jnp.transpose(ladder, (1, 0, 2)).reshape(residual_in.shape)
    return (residual_in.astype(jnp.float32) + ladder.astype(jnp.float32)).astype(jnp.bfloat16)


def solution(mesh):
    fine = Mesh(mesh.devices.reshape(Y, X, CORE, Z), ("y", "x", "c", "z"))
    owner = ("y", "x", "c", "z")
    in_specs = (
        P(owner, None, None),
        P(None, ("y", "x", "c"), "z"),
        P(owner, None),
        P(),
    )
    return jax.shard_map(
        shards, mesh=fine, in_specs=in_specs, out_specs=P(owner, None), check_vma=False
    )
```

time: 118 us -> 98.4 us (0.83)
  the two profiles are of different devices: /device:TPU:16 before, /device:TPU:18 now
where the time goes in v3:
time: 98.4 us; the launch traced here: 97.9 us
  blocking collectives  39.2 us (40%)
  starting transfers between devices  35.4 us (36%)
  waiting for transfers between devices  11.7 us (12%)
  Pallas kernels  6.3 us (6%)
  local copies, waits for them, and re-layouts  3.89 us (4%)
  other arithmetic  1.35 us (1%)
    all_to_all x1, blocking collectives, shards(): lax.all_to_all(partial, ('y', 'z'), split_axis=0, concat_axis=0, tiled=True)  39.2 us
    all_to_all x1, starting transfers between devices, shards(): lax.all_to_all(outgoing, ('y', 'z'), split_axis=0, concat_axis=0, tiled=T...  16.6 us
    ppermute x4, starting transfers between devices, shards(): rights = ring + [lax.ppermute(r, 'c', SWAP) for r in ring]  8.17 us
    ppermute x1, waiting for transfers between devices, shards(): above = lax.ppermute(integrals, 'x', DOWN)  6.94 us
    pallas_call x1, Pallas kernels, product(): pl.pallas_call(product_kernel, out_shape=jax.ShapeDtypeStruct((2, rows, p...  4.76 us
    all_to_all x1, waiting for transfers between devices, shards(): lax.all_to_all(outgoing, ('y', 'z'), split_axis=0, concat_axis=0, tiled=T...  4.73 us
    ppermute x1, starting transfers between devices, shards(): above = lax.ppermute(integrals, 'x', DOWN)  4.06 us
    ppermute x1, starting transfers between devices, shards(): below = lax.ppermute(integrals, 'x', UP)  3.52 us
  transfers between devices with their start and end apart: 8, of which 2 were waited for; matrix products, arithmetic and copies ran while one was open for 1% of the time, Pallas kernels for 2%

profile of v3, /device:TPU:18, one launch (start us, length us, event | category | flops | bytes accessed | tf_op | source)
XLA Modules:
  0.0 97.9 jit_solution(9748188275125694817)
XLA Ops:
  0.0 0.0 copy-start.1
  0.0 3.5 %collective-permute-start.2 = (bf16[3,256,512]{2,1,0:T(8,128)(2,1)}, bf16[3,256,512]{2,1,0:T(8,128)(2,1)S(1)}, u32[]{:S(2)}, u32[]{:S(2)}) collective-permute-start(bf16[3,256,512]{2,1,0:T(8,128)(2,1)} %refs_0_.1), channel_id=1, source_target_pairs={{0,16},{16,32},{32,48},{48,0},{1,17},{17,33},{33,49},{49,1},{2,18}... | collective-permute-start | bytes 2359304 | tf_op jit(solution)/shard_map/ppermute | solution.py:98
  3.5 3.0 %collective-permute-start.1 = (bf16[3,256,512]{2,1,0:T(8,128)(2,1)}, bf16[3,256,512]{2,1,0:T(8,128)(2,1)S(1)}, u32[]{:S(2)}, u32[]{:S(2)}) collective-permute-start(bf16[3,256,512]{2,1,0:T(8,128)(2,1)} %refs_0_.1), channel_id=1, source_target_pairs={{0,32},{16,48},{32,0},{48,16},{1,33},{17,49},{33,1},{49,17},{2,34}... | collective-permute-start | bytes 2359304 | tf_op jit(solution)/shard_map/ppermute | solution.py:100
  6.6 4.1 %collective-permute-start = (bf16[3,256,512]{2,1,0:T(8,128)(2,1)}, bf16[3,256,512]{2,1,0:T(8,128)(2,1)}, u32[]{:S(2)}, u32[]{:S(2)}) collective-permute-start(bf16[3,256,512]{2,1,0:T(8,128)(2,1)} %refs_0_.1), channel_id=1, source_target_pairs={{0,48},{16,0},{32,16},{48,32},{1,49},{17,1},{33,17},{49,33},{2,50}... | collective-permute-start | bytes 2359304 | tf_op jit(solution)/shard_map/ppermute | solution.py:99
  10.6 1.0 %reshape.12.amplitudes_ref = bf16[3,8,8,4,128]{4,3,2,1,0:T(4,128)(2,1)S(1)} reshape(bf16[3,8,4096]{2,1,0:T(8,128)(2,1)} %param.4) | data formatting | bytes 393216 | tf_op jit(solution)/shard_map/reshape | solution.py:35
  11.7 0.0 copy-done.1
  11.7 1.5 %shard_map.46 = bf16[8,8,9,4,128]{4,3,2,1,0:T(4,128)(2,1)} custom-call(s32[4,3]{1,0:T(4,128)S(1)} %copy-done.1, bf16[3,8,8,4,128]{4,3,2,1,0:T(4,128)(2,1)S(1)} %reshape.12.amplitudes_ref), custom_call_target="tpu_custom_call" | custom-call | flops 99999997952 | bytes 1000000 | tf_op jit(solution)/shard_map/pallas_call | solution.py:37
  13.2 0.0 copy-start
  13.2 16.6 %all-to-all-start = ((bf16[64,9,4,128]{3,2,1,0:T(4,128)(2,1)}), bf16[64,9,4,128]{3,2,1,0:T(4,128)(2,1)S(1)}, u32[]{:S(2)}, u32[]{:S(2)}) async-start(bf16[64,9,4,128]{3,2,1,0:T(4,128)(2,1)} %bitcast), calls=%async_computation | async-start | bytes 1179648 | tf_op jit(solution)/shard_map/all_to_all | solution.py:104
  29.9 0.0 copy-done
  29.9 1.9 %collective-permute-start.3 = (bf16[3,256,512]{2,1,0:T(8,128)(2,1)S(1)}, bf16[3,256,512]{2,1,0:T(8,128)(2,1)}, u32[]{:S(2)}, u32[]{:S(2)}) collective-permute-start(bf16[3,256,512]{2,1,0:T(8,128)(2,1)S(1)} %copy-done), channel_id=1, source_target_pairs={{0,8},{8,0},{1,9},{9,1},{2,10},{10,2},{3,11},{11,3},{4,12},{12,4},... | collective-permute-start | bytes 2359304 | tf_op jit(solution)/shard_map/ppermute | solution.py:107
  31.8 0.0 collective-permute-done.2.refs_3_
  31.8 2.4 %collective-permute-start.6 = (bf16[3,256,512]{2,1,0:T(8,128)(2,1)S(1)}, bf16[3,256,512]{2,1,0:T(8,128)(2,1)}, u32[]{:S(2)}, u32[]{:S(2)}) collective-permute-start(bf16[3,256,512]{2,1,0:T(8,128)(2,1)S(1)} %collective-permute-done.2.refs_3_), channel_id=1, source_target_pairs={{0,8},{8,0},{1,9},{9,1},{2,10},{10,2},{3,11},{11,3},{4,12},{12,4},... | collective-permute-start | bytes 2359304 | tf_op jit(solution)/shard_map/ppermute | solution.py:107
  34.2 0.0 collective-permute-done.1.refs_2_
  34.2 1.9 %collective-permute-start.5 = (bf16[3,256,512]{2,1,0:T(8,128)(2,1)S(1)}, bf16[3,256,512]{2,1,0:T(8,128)(2,1)}, u32[]{:S(2)}, u32[]{:S(2)}) collective-permute-start(bf16[3,256,512]{2,1,0:T(8,128)(2,1)S(1)} %collective-permute-done.1.refs_2_), channel_id=1, source_target_pairs={{0,8},{8,0},{1,9},{9,1},{2,10},{10,2},{3,11},{11,3},{4,12},{12,4},... | collective-permute-start | bytes 2359304 | tf_op jit(solution)/shard_map/ppermute | solution.py:107
  36.2 6.9 %collective-permute-done.refs_1_ = bf16[3,256,512]{2,1,0:T(8,128)(2,1)} collective-permute-done((bf16[3,256,512]{2,1,0:T(8,128)(2,1)}, bf16[3,256,512]{2,1,0:T(8,128)(2,1)}, u32[]{:S(2)}, u32[]{:S(2)}) %collective-permute-start) | collective-permute-done | bytes 786464 | tf_op jit(solution)/shard_map/ppermute | solution.py:99
  43.1 1.9 %collective-permute-start.4 = (bf16[3,256,512]{2,1,0:T(8,128)(2,1)}, bf16[3,256,512]{2,1,0:T(8,128)(2,1)}, u32[]{:S(2)}, u32[]{:S(2)}) collective-permute-start(bf16[3,256,512]{2,1,0:T(8,128)(2,1)} %collective-permute-done.refs_1_), channel_id=1, source_target_pairs={{0,8},{8,0},{1,9},{9,1},{2,10},{10,2},{3,11},{11,3},{4,12},{12,4},... | collective-permute-start | bytes 2359304 | tf_op jit(solution)/shard_map/ppermute | solution.py:107
  45.0 0.1 pad_add_fusion.where_ref
  45.1 0.0 collective-permute-done.3.refs_4_
  45.1 4.7 %all-to-all-done.left_ref = bf16[64,9,4,128]{3,2,1,0:T(4,128)(2,1)S(1)} async-done(((bf16[64,9,4,128]{3,2,1,0:T(4,128)(2,1)}), bf16[64,9,4,128]{3,2,1,0:T(4,128)(2,1)S(1)}, u32[]{:S(2)}, u32[]{:S(2)}) %all-to-all-start) | async-done | bytes 589856 | tf_op jit(solution)/shard_map/all_to_all | solution.py:104
  49.9 0.0 collective-permute-done.6.refs_7_
  49.9 0.0 collective-permute-done.5.refs_6_
  49.9 0.0 collective-permute-done.4.refs_5_
  49.9 4.8 %shard_map.47 = bf16[2,3,64,1024]{3,2,1,0:T(8,128)(2,1)S(1)} custom-call(s32[8]{0:T(128)S(1)} %pad_add_fusion.where_ref, bf16[64,9,4,128]{3,2,1,0:T(4,128)(2,1)S(1)} %all-to-all-done.left_ref, bf16[3,256,512]{2,1,0:T(8,128)(2,1)S(1)} %copy-done, bf16[3,256,512]{2,1,0:T(8,128)(2,1)} %collective-permute-done.refs_1_, ...), custom_call_target="tpu_custom_call" | custom-call | flops 1000 | bytes 1000 | tf_op jit(solution)/shard_map/pallas_call | solution.py:81
  54.6 0.8 copy.8
  55.5 39.2 %all_to_all.10 = bf16[64,3,2,1024]{3,2,1,0:T(2,128)(2,1)S(1)} all-to-all(bf16[64,3,2,1024]{3,2,1,0:T(2,128)(2,1)S(1)} %copy.8), channel_id=1, replica_groups=mesh['y'=8,'x'=4,'c'=2,'z'=8] {'y','z'}, dimensions={0} | all-to-all | bytes 1572864 | tf_op jit(solution)/shard_map/all_to_all | solution.py:113
  94.6 0.5 copy.9
  95.2 0.6 reshape.14
  95.8 0.5 reduce_sum.12
  96.3 0.0 copy-start.2
  96.3 0.1 copy.10
  96.5 0.8 copy-done.2
  97.2 0.7 add_convert_fusion
  (2 shorter events, 0.0 us)
Async XLA Ops:
  0.0 11.7 %copy-start.1 = (s32[4,3]{1,0:T(4,128)S(1)}, s32[4,3]{1,0:T(4,128)}, u32[]{:S(2)}) copy-start(s32[4,3]{1,0:T(4,128)} %kept_ref.1) | copy-start | bytes 148
  0.0 31.8 %collective-permute-start.2 = (bf16[3,256,512]{2,1,0:T(8,128)(2,1)}, bf16[3,256,512]{2,1,0:T(8,128)(2,1)S(1)}, u32[]{:S(2)}, u32[]{:S(2)}) collective-permute-start(bf16[3,256,512]{2,1,0:T(8,128)(2,1)} %refs_0_.1), channel_id=1, source_target_pairs={{0,16},{16,32},{32,48},{48,0},{1,17},{17,33},{33,49},{49,1},{2,18}... | collective-permute-start | bytes 2359304 | tf_op jit(solution)/shard_map/ppermute | solution.py:98
  3.5 30.7 %collective-permute-start.1 = (bf16[3,256,512]{2,1,0:T(8,128)(2,1)}, bf16[3,256,512]{2,1,0:T(8,128)(2,1)S(1)}, u32[]{:S(2)}, u32[]{:S(2)}) collective-permute-start(bf16[3,256,512]{2,1,0:T(8,128)(2,1)} %refs_0_.1), channel_id=1, source_target_pairs={{0,32},{16,48},{32,0},{48,16},{1,33},{17,49},{33,1},{49,17},{2,34}... | collective-permute-start | bytes 2359304 | tf_op jit(solution)/shard_map/ppermute | solution.py:100
  6.6 36.5 %collective-permute-start = (bf16[3,256,512]{2,1,0:T(8,128)(2,1)}, bf16[3,256,512]{2,1,0:T(8,128)(2,1)}, u32[]{:S(2)}, u32[]{:S(2)}) collective-permute-start(bf16[3,256,512]{2,1,0:T(8,128)(2,1)} %refs_0_.1), channel_id=1, source_target_pairs={{0,48},{16,0},{32,16},{48,32},{1,49},{17,1},{33,17},{49,33},{2,50}... | collective-permute-start | bytes 2359304 | tf_op jit(solution)/shard_map/ppermute | solution.py:99
  13.2 16.6 %copy-start = (bf16[3,256,512]{2,1,0:T(8,128)(2,1)S(1)}, bf16[3,256,512]{2,1,0:T(8,128)(2,1)}, u32[]{:S(2)}) copy-start(bf16[3,256,512]{2,1,0:T(8,128)(2,1)} %refs_0_.1) | copy-start | bytes 2359300
  13.2 36.6 %all-to-all-start = ((bf16[64,9,4,128]{3,2,1,0:T(4,128)(2,1)}), bf16[64,9,4,128]{3,2,1,0:T(4,128)(2,1)S(1)}, u32[]{:S(2)}, u32[]{:S(2)}) async-start(bf16[64,9,4,128]{3,2,1,0:T(4,128)(2,1)} %bitcast), calls=%async_computation | async-start | bytes 1179648 | tf_op jit(solution)/shard_map/all_to_all | solution.py:104
  29.9 15.3 %collective-permute-start.3 = (bf16[3,256,512]{2,1,0:T(8,128)(2,1)S(1)}, bf16[3,256,512]{2,1,0:T(8,128)(2,1)}, u32[]{:S(2)}, u32[]{:S(2)}) collective-permute-start(bf16[3,256,512]{2,1,0:T(8,128)(2,1)S(1)} %copy-done), channel_id=1, source_target_pairs={{0,8},{8,0},{1,9},{9,1},{2,10},{10,2},{3,11},{11,3},{4,12},{12,4},... | collective-permute-start | bytes 2359304 | tf_op jit(solution)/shard_map/ppermute | solution.py:107
  31.8 18.1 %collective-permute-start.6 = (bf16[3,256,512]{2,1,0:T(8,128)(2,1)S(1)}, bf16[3,256,512]{2,1,0:T(8,128)(2,1)}, u32[]{:S(2)}, u32[]{:S(2)}) collective-permute-start(bf16[3,256,512]{2,1,0:T(8,128)(2,1)S(1)} %collective-permute-done.2.refs_3_), channel_id=1, source_target_pairs={{0,8},{8,0},{1,9},{9,1},{2,10},{10,2},{3,11},{11,3},{4,12},{12,4},... | collective-permute-start | bytes 2359304 | tf_op jit(solution)/shard_map/ppermute | solution.py:107
  34.2 15.6 %collective-permute-start.5 = (bf16[3,256,512]{2,1,0:T(8,128)(2,1)S(1)}, bf16[3,256,512]{2,1,0:T(8,128)(2,1)}, u32[]{:S(2)}, u32[]{:S(2)}) collective-permute-start(bf16[3,256,512]{2,1,0:T(8,128)(2,1)S(1)} %collective-permute-done.1.refs_2_), channel_id=1, source_target_pairs={{0,8},{8,0},{1,9},{9,1},{2,10},{10,2},{3,11},{11,3},{4,12},{12,4},... | collective-permute-start | bytes 2359304 | tf_op jit(solution)/shard_map/ppermute | solution.py:107
  43.1 6.8 %collective-permute-start.4 = (bf16[3,256,512]{2,1,0:T(8,128)(2,1)}, bf16[3,256,512]{2,1,0:T(8,128)(2,1)}, u32[]{:S(2)}, u32[]{:S(2)}) collective-permute-start(bf16[3,256,512]{2,1,0:T(8,128)(2,1)} %collective-permute-done.refs_1_), channel_id=1, source_target_pairs={{0,8},{8,0},{1,9},{9,1},{2,10},{10,2},{3,11},{11,3},{4,12},{12,4},... | collective-permute-start | bytes 2359304 | tf_op jit(solution)/shard_map/ppermute | solution.py:107
  96.3 0.9 copy-start.2

commit v4 on v3

--- a/solution.py
+++ b/solution.py
@@ -10,7 +10,6 @@
 SWAP = ((0, 1), (1, 0))
 UP = tuple((i, (i + 1) % X) for i in range(X))
 DOWN = tuple((i, (i - 1) % X) for i in range(X))
-ACROSS = tuple((i, (i + 2) % X) for i in range(X))
 VMEM = pl.BlockSpec(memory_space=pltpu.VMEM)
 SMEM = pl.BlockSpec(memory_space=pltpu.SMEM)
 GRANT = 32 * 1024 * 1024
@@ -44,11 +43,30 @@
     )(kept_tiles, split)
 
 
+def halves_kernel(below_ref, above_ref, low_ref, high_ref):
+    half = low_ref.shape[1]
+    low_ref[...] = below_ref[:, :half]
+    high_ref[...] = above_ref[:, half:]
+
+
+def halves(below, above):
+    keep, block, share = below.shape
+    shape = jax.ShapeDtypeStruct((keep, block // 2, share), below.dtype)
+    return pl.pallas_call(
+        halves_kernel,
+        out_shape=(shape, shape),
+        in_specs=[VMEM, VMEM],
+        out_specs=(VMEM, VMEM),
+        cost_estimate=pl.CostEstimate(flops=10**11, bytes_accessed=10**6, transcendentals=0),
+        compiler_params=pltpu.CompilerParams(vmem_limit_bytes=GRANT),
+    )(below, above)
+
+
 def product_kernel(where_ref, left_ref, *refs):
     rights, out_ref = refs[:-1], refs[-1]
     peers, both, chunks, lanes = left_ref.shape
-    halves, rows, _, columns = out_ref.shape
-    keep, block, share = rights[0].shape
+    keep, _, share = rights[0].shape
+    rows = both // keep
     left = [
         jnp.concatenate(
             [
@@ -60,6 +78,7 @@
         for k in range(keep)
     ]
     for j, right_ref in enumerate(rights):
+        block = right_ref.shape[1]
         total = jnp.zeros((rows * peers, block), jnp.float32)
         for k in range(keep):
             total += lax.dot_general(
@@ -68,22 +87,20 @@
                 (((1,), (1,)), ((), ())),
                 preferred_element_type=jnp.float32,
             )
-        place = where_ref[j]
-        per_half = columns // block
-        start = pl.multiple_of(lax.rem(place, per_half) * block, block)
-        out_ref[lax.div(place, per_half), :, :, pl.ds(start, block)] = total.astype(jnp.bfloat16).reshape(rows, peers, block)
+        start = pl.multiple_of(where_ref[j] * LANES, LANES)
+        out_ref[:, :, pl.ds(start, block)] = total.astype(jnp.bfloat16).reshape(rows, peers, block)
 
 
-def product(where, left, rights):
+def product(where, left, rights, work):
     peers = left.shape[0]
     rows = left.shape[1] // rights[0].shape[0]
-    columns = sum(r.shape[1] for r in rights) // 2
+    columns = sum(r.shape[1] for r in rights)
     return pl.pallas_call(
         product_kernel,
-        out_shape=jax.ShapeDtypeStruct((2, rows, peers, columns), jnp.bfloat16),
+        out_shape=jax.ShapeDtypeStruct((rows, peers, columns), jnp.bfloat16),
         in_specs=[SMEM] + [VMEM] * (1 + len(rights)),
         out_specs=VMEM,
-        cost_estimate=pl.CostEstimate(flops=1000, bytes_accessed=1000, transcendentals=0),
+        cost_estimate=pl.CostEstimate(flops=work, bytes_accessed=1000, transcendentals=0),
         compiler_params=pltpu.CompilerParams(vmem_limit_bytes=GRANT),
     )(where, left, *rights)
 
@@ -92,29 +109,40 @@
     rows, tiles, width = amplitudes.shape
     keep = kept_tiles.shape[1]
     share = width // Z
+    block = integrals.shape[1]
     x = lax.axis_index("x")
     core = lax.axis_index("c")
 
     below = lax.ppermute(integrals, "x", UP)
     above = lax.ppermute(integrals, "x", DOWN)
-    far = lax.ppermute(integrals, "x", ACROSS)
+    low, high = halves(below, above)
+    far_low = lax.ppermute(low, "x", UP)
+    far_high = lax.ppermute(high, "x", DOWN)
 
     outgoing = pick(kept_tiles, amplitudes)
     outgoing = outgoing.reshape(Y * Z, rows * keep, share // LANES, LANES)
     mine = lax.all_to_all(outgoing, ("y", "z"), split_axis=0, concat_axis=0, tiled=True)
+    theirs = lax.ppermute(mine, "c", SWAP)
 
-    ring = [integrals, above, far, below]
-    rights = ring + [lax.ppermute(r, "c", SWAP) for r in ring]
-    steps = jnp.arange(X)
-    blocks = lax.rem(x + steps, X) * CORE
-    where = jnp.concatenate([blocks + core, blocks + 1 - core])
-    partial = product(where.astype(jnp.int32), mine, rights)
-    partial = partial.transpose(2, 1, 0, 3)
+    rights = (integrals, above, below, far_low, far_high)
+    steps = jnp.array([0, 1, X - 1, 2, 2], jnp.int32)
+    offsets = jnp.array([0, 0, 0, 0, 1], jnp.int32)
+    where = lax.rem(x.astype(jnp.int32) + steps, X) * (block // LANES) + offsets
+    first = product(where, mine, rights, 10**10)
+    second = product(where, theirs, rights, 1000)
+    partial = jnp.stack([first, second], axis=1)
+    partial = partial.transpose(2, 0, 1, 3)
     returned = lax.all_to_all(partial, ("y", "z"), split_axis=0, concat_axis=0, tiled=True)
-    returned = returned.reshape(Y, Z, rows, -1).astype(jnp.float32)
+    returned = returned.reshape(Y, Z, rows, CORE, X * block).astype(jnp.float32)
     ladder = jnp.sum(returned, axis=1).astype(jnp.bfloat16)
-    ladder = jnp.transpose(ladder, (1, 0, 2)).reshape(residual_in.shape)
-    return (residual_in.astype(jnp.float32) + ladder.astype(jnp.float32)).astype(jnp.bfloat16)
+    ladder = ladder.reshape(Y, rows, CORE, X, block)
+    own = ladder[:, :, 0]
+    other = lax.ppermute(ladder[:, :, 1], "c", SWAP)
+    low = jnp.where(core == 0, own, other)
+    high = jnp.where(core == 0, other, own)
+    both = jnp.stack([low, high], axis=3)
+    both = jnp.transpose(both, (1, 0, 2, 3, 4)).reshape(residual_in.shape)
+    return (residual_in.astype(jnp.float32) + both.astype(jnp.float32)).astype(jnp.bfloat16)
 
 
 def solution(mesh):

time: 98.4 us -> 92.9 us (0.944)
  the two profiles are of different devices: /device:TPU:18 before, /device:TPU:1 now
where the time goes in v4:
time: 92.9 us; the launch traced here: 92.4 us
  starting transfers between devices  44.5 us (48%)
  blocking collectives  24.6 us (26%)
  waiting for transfers between devices  9.7 us (10%)
  Pallas kernels  8.07 us (9%)
  local copies, waits for them, and re-layouts  3.7 us (4%)
  other arithmetic  1.61 us (2%)
    all_to_all x1, blocking collectives, shards(): lax.all_to_all(partial, ('y', 'z'), split_axis=0, concat_axis=0, tiled=True)  24.6 us
    all_to_all x1, starting transfers between devices, shards(): lax.all_to_all(outgoing, ('y', 'z'), split_axis=0, concat_axis=0, tiled=T...  16.5 us
    all_to_all x1, waiting for transfers between devices, shards(): lax.all_to_all(outgoing, ('y', 'z'), split_axis=0, concat_axis=0, tiled=T...  8.84 us
    ppermute x1, starting transfers between devices, shards(): other = lax.ppermute(ladder[:, :, 1], 'c', SWAP)  7.9 us
    ppermute x1, starting transfers between devices, shards(): theirs = lax.ppermute(mine, 'c', SWAP)  6.41 us
    pallas_call x2, Pallas kernels, product(): pl.pallas_call(product_kernel, out_shape=jax.ShapeDtypeStruct((rows, peer...  5.58 us
    ppermute x1, starting transfers between devices, shards(): far_high = lax.ppermute(high, 'x', DOWN)  4.57 us
    ppermute x1, starting transfers between devices, shards(): below = lax.ppermute(integrals, 'x', UP)  4.07 us
  transfers between devices with their start and end apart: 7, of which 2 were waited for; matrix products, arithmetic and copies ran while one was open for 1% of the time, Pallas kernels for 6%

profile of v4, /device:TPU:1, one launch (start us, length us, event | category | flops | bytes accessed | tf_op | source)
XLA Modules:
  0.0 92.4 jit_solution(13433703949134916629)
XLA Ops:
  0.0 0.0 copy-start.1
  0.0 4.1 %collective-permute-start.1 = (bf16[3,256,512]{2,1,0:T(8,128)(2,1)}, bf16[3,256,512]{2,1,0:T(8,128)(2,1)S(1)}, u32[]{:S(2)}, u32[]{:S(2)}) collective-permute-start(bf16[3,256,512]{2,1,0:T(8,128)(2,1)} %refs_0_.3), channel_id=1, source_target_pairs={{0,16},{16,32},{32,48},{48,0},{1,17},{17,33},{33,49},{49,1},{2,18}... | collective-permute-start | bytes 2359304 | tf_op jit(solution)/shard_map/ppermute | solution.py:116
  4.1 3.2 %collective-permute-start = (bf16[3,256,512]{2,1,0:T(8,128)(2,1)}, bf16[3,256,512]{2,1,0:T(8,128)(2,1)S(1)}, u32[]{:S(2)}, u32[]{:S(2)}) collective-permute-start(bf16[3,256,512]{2,1,0:T(8,128)(2,1)} %refs_0_.3), channel_id=1, source_target_pairs={{0,48},{16,0},{32,16},{48,32},{1,49},{17,1},{33,17},{49,33},{2,50}... | collective-permute-start | bytes 2359304 | tf_op jit(solution)/shard_map/ppermute | solution.py:117
  7.3 1.0 %reshape.15.amplitudes_ref = bf16[3,8,8,4,128]{4,3,2,1,0:T(4,128)(2,1)S(1)} reshape(bf16[3,8,4096]{2,1,0:T(8,128)(2,1)} %param.6) | data formatting | bytes 393216 | tf_op jit(solution)/shard_map/reshape | solution.py:34
  8.3 0.0 copy-done.1
  8.3 1.5 %shard_map.64 = bf16[8,8,9,4,128]{4,3,2,1,0:T(4,128)(2,1)} custom-call(s32[4,3]{1,0:T(4,128)S(1)} %copy-done.1, bf16[3,8,8,4,128]{4,3,2,1,0:T(4,128)(2,1)S(1)} %reshape.15.amplitudes_ref), custom_call_target="tpu_custom_call" | custom-call | flops 99999997952 | bytes 1000000 | tf_op jit(solution)/shard_map/pallas_call | solution.py:36
  9.9 16.5 %all-to-all-start = ((bf16[64,9,4,128]{3,2,1,0:T(4,128)(2,1)}), bf16[64,9,4,128]{3,2,1,0:T(4,128)(2,1)S(1)}, u32[]{:S(2)}, u32[]{:S(2)}) async-start(bf16[64,9,4,128]{3,2,1,0:T(4,128)(2,1)} %bitcast), calls=%async_computation | async-start | bytes 1179648 | tf_op jit(solution)/shard_map/all_to_all | solution.py:124
  26.4 0.0 copy-start
  26.4 0.0 collective-permute-done.1.below_ref.refs_2_
  26.4 0.0 collective-permute-done.above_ref.refs_1_
  26.4 0.9 %shard_map.65 = (bf16[3,128,512]{2,1,0:T(8,128)(2,1)}, bf16[3,128,512]{2,1,0:T(8,128)(2,1)}) custom-call(bf16[3,256,512]{2,1,0:T(8,128)(2,1)S(1)} %collective-permute-done.1.below_ref.refs_2_, bf16[3,256,512]{2,1,0:T(8,128)(2,1)S(1)} %collective-permute-done.above_ref.refs_1_), custom_call_target="tpu_custom_call" | custom-call | flops 99999997952 | bytes 1000000 | tf_op jit(solution)/shard_map/pallas_call | solution.py:55
  27.4 1.9 %collective-permute-start.2 = (bf16[3,128,512]{2,1,0:T(8,128)(2,1)}, bf16[3,128,512]{2,1,0:T(8,128)(2,1)S(1)}, u32[]{:S(2)}, u32[]{:S(2)}) collective-permute-start(bf16[3,128,512]{2,1,0:T(8,128)(2,1)} %get-tuple-element.7), channel_id=1, source_target_pairs={{0,16},{16,32},{32,48},{48,0},{1,17},{17,33},{33,49},{49,1},{2,18}... | collective-permute-start | bytes 1179656 | tf_op jit(solution)/shard_map/ppermute | solution.py:119
  29.3 4.6 %collective-permute-start.3 = (bf16[3,128,512]{2,1,0:T(8,128)(2,1)}, bf16[3,128,512]{2,1,0:T(8,128)(2,1)}, u32[]{:S(2)}, u32[]{:S(2)}) collective-permute-start(bf16[3,128,512]{2,1,0:T(8,128)(2,1)} %get-tuple-element.8), channel_id=1, source_target_pairs={{0,48},{16,0},{32,16},{48,32},{1,49},{17,1},{33,17},{49,33},{2,50}... | collective-permute-start | bytes 1179656 | tf_op jit(solution)/shard_map/ppermute | solution.py:120
  33.9 0.0 copy-start.3
  33.9 0.0 copy-start.4
  33.9 0.6 copy-done.3
  34.5 0.0 copy-done.4
  34.5 8.8 %all-to-all-done.left_ref = bf16[64,9,4,128]{3,2,1,0:T(4,128)(2,1)S(1)} async-done(((bf16[64,9,4,128]{3,2,1,0:T(4,128)(2,1)}), bf16[64,9,4,128]{3,2,1,0:T(4,128)(2,1)S(1)}, u32[]{:S(2)}, u32[]{:S(2)}) %all-to-all-start) | async-done | bytes 589856 | tf_op jit(solution)/shard_map/all_to_all | solution.py:124
  43.4 6.4 %collective-permute-start.4 = (bf16[64,9,4,128]{3,2,1,0:T(4,128)(2,1)S(1)}, bf16[64,9,4,128]{3,2,1,0:T(4,128)(2,1)S(1)}, u32[]{:S(2)}, u32[]{:S(2)}) collective-permute-start(bf16[64,9,4,128]{3,2,1,0:T(4,128)(2,1)S(1)} %all-to-all-done.left_ref), channel_id=1, source_target_pairs={{0,8},{8,0},{1,9},{9,1},{2,10},{10,2},{3,11},{11,3},{4,12},{12,4},... | collective-permute-start | bytes 1769480 | tf_op jit(solution)/shard_map/ppermute | solution.py:125
  49.8 0.0 collective-permute-done.2.refs_3_
  49.8 0.0 collective-permute-done.3.refs_4_
  49.8 0.0 copy-done
  49.8 2.8 %shard_map.66 = bf16[3,64,1024]{2,1,0:T(8,128)(2,1)S(1)} custom-call(s32[5]{0:T(128)S(1)} %fusion.2.where_ref, bf16[64,9,4,128]{3,2,1,0:T(4,128)(2,1)S(1)} %all-to-all-done.left_ref, bf16[3,256,512]{2,1,0:T(8,128)(2,1)S(1)} %copy-done, bf16[3,256,512]{2,1,0:T(8,128)(2,1)S(1)} %collective-permute-done.above_ref.refs_1_, ...), custom_call_target="tpu_custom_call" | custom-call | flops 10000000000 | bytes 1000 | tf_op jit(solution)/shard_map/pallas_call | solution.py:98
  52.6 0.0 collective-permute-done.4.left_ref
  52.6 2.8 %shard_map.67 = bf16[3,64,1024]{2,1,0:T(8,128)(2,1)S(1)} custom-call(s32[5]{0:T(128)S(1)} %fusion.2.where_ref, bf16[64,9,4,128]{3,2,1,0:T(4,128)(2,1)S(1)} %collective-permute-done.4.left_ref, bf16[3,256,512]{2,1,0:T(8,128)(2,1)S(1)} %copy-done, bf16[3,256,512]{2,1,0:T(8,128)(2,1)S(1)} %collective-permute-done.above_ref.refs_1_, ...), custom_call_target="tpu_custom_call" | custom-call | flops 1000 | bytes 1000 | tf_op jit(solution)/shard_map/pallas_call | solution.py:98
  55.4 0.1 maximum_bitcast_fusion
  55.5 0.8 copy.19
  56.3 24.6 %all_to_all.10 = bf16[64,3,2,1024]{3,2,1,0:T(2,128)(2,1)S(1)} all-to-all(bf16[64,3,2,1024]{3,2,1,0:T(2,128)(2,1)S(1)} %copy.19), channel_id=1, replica_groups=mesh['y'=8,'x'=4,'c'=2,'z'=8] {'y','z'}, dimensions={0} | all-to-all | bytes 1572864 | tf_op jit(solution)/shard_map/all_to_all | solution.py:135
  80.9 0.7 bitcast_reduce_fusion
  81.6 0.1 reshape.21
  81.7 7.9 %collective-permute-start.5 = (bf16[8,3,4,256]{3,2,0,1:T(4,128)(2,1)S(1)}, bf16[8,3,4,256]{3,2,0,1:T(4,128)(2,1)S(1)}, u32[]{:S(2)}, u32[]{:S(2)}) collective-permute-start(bf16[8,3,4,256]{3,2,0,1:T(4,128)(2,1)S(1)} %bitcast.26), channel_id=1, source_target_pairs={{0,8},{8,0},{1,9},{9,1},{2,10},{10,2},{3,11},{11,3},{4,12},{12,4},... | collective-permute-start | bytes 147464 | tf_op jit(solution)/shard_map/ppermute | solution.py:140
  89.7 0.9 collective-permute-done.5
  90.6 0.1 convert_bitcast_fusion
  90.6 0.2 copy.25
  90.8 0.0 copy-start.2
  90.8 0.2 reshape.19
  91.0 0.7 copy-done.2
  91.7 0.7 add_convert_fusion
  (4 shorter events, 0.1 us)
Async XLA Ops:
  0.0 8.3 %copy-start.1 = (s32[4,3]{1,0:T(4,128)S(1)}, s32[4,3]{1,0:T(4,128)}, u32[]{:S(2)}) copy-start(s32[4,3]{1,0:T(4,128)} %kept_ref.1) | copy-start | bytes 148
  0.0 26.4 %collective-permute-start.1 = (bf16[3,256,512]{2,1,0:T(8,128)(2,1)}, bf16[3,256,512]{2,1,0:T(8,128)(2,1)S(1)}, u32[]{:S(2)}, u32[]{:S(2)}) collective-permute-start(bf16[3,256,512]{2,1,0:T(8,128)(2,1)} %refs_0_.3), channel_id=1, source_target_pairs={{0,16},{16,32},{32,48},{48,0},{1,17},{17,33},{33,49},{49,1},{2,18}... | collective-permute-start | bytes 2359304 | tf_op jit(solution)/shard_map/ppermute | solution.py:116
  4.1 22.3 %collective-permute-start = (bf16[3,256,512]{2,1,0:T(8,128)(2,1)}, bf16[3,256,512]{2,1,0:T(8,128)(2,1)S(1)}, u32[]{:S(2)}, u32[]{:S(2)}) collective-permute-start(bf16[3,256,512]{2,1,0:T(8,128)(2,1)} %refs_0_.3), channel_id=1, source_target_pairs={{0,48},{16,0},{32,16},{48,32},{1,49},{17,1},{33,17},{49,33},{2,50}... | collective-permute-start | bytes 2359304 | tf_op jit(solution)/shard_map/ppermute | solution.py:117
  9.9 33.5 %all-to-all-start = ((bf16[64,9,4,128]{3,2,1,0:T(4,128)(2,1)}), bf16[64,9,4,128]{3,2,1,0:T(4,128)(2,1)S(1)}, u32[]{:S(2)}, u32[]{:S(2)}) async-start(bf16[64,9,4,128]{3,2,1,0:T(4,128)(2,1)} %bitcast), calls=%async_computation | async-start | bytes 1179648 | tf_op jit(solution)/shard_map/all_to_all | solution.py:124
  26.4 23.4 %copy-start = (bf16[3,256,512]{2,1,0:T(8,128)(2,1)S(1)}, bf16[3,256,512]{2,1,0:T(8,128)(2,1)}, u32[]{:S(2)}) copy-start(bf16[3,256,512]{2,1,0:T(8,128)(2,1)} %refs_0_.3) | copy-start | bytes 2359300
  27.4 22.4 %collective-permute-start.2 = (bf16[3,128,512]{2,1,0:T(8,128)(2,1)}, bf16[3,128,512]{2,1,0:T(8,128)(2,1)S(1)}, u32[]{:S(2)}, u32[]{:S(2)}) collective-permute-start(bf16[3,128,512]{2,1,0:T(8,128)(2,1)} %get-tuple-element.7), channel_id=1, source_target_pairs={{0,16},{16,32},{32,48},{48,0},{1,17},{17,33},{33,49},{49,1},{2,18}... | collective-permute-start | bytes 1179656 | tf_op jit(solution)/shard_map/ppermute | solution.py:119
  29.3 20.5 %collective-permute-start.3 = (bf16[3,128,512]{2,1,0:T(8,128)(2,1)}, bf16[3,128,512]{2,1,0:T(8,128)(2,1)}, u32[]{:S(2)}, u32[]{:S(2)}) collective-permute-start(bf16[3,128,512]{2,1,0:T(8,128)(2,1)} %get-tuple-element.8), channel_id=1, source_target_pairs={{0,48},{16,0},{32,16},{48,32},{1,49},{17,1},{33,17},{49,33},{2,50}... | collective-permute-start | bytes 1179656 | tf_op jit(solution)/shard_map/ppermute | solution.py:120
  33.9 0.7 copy-start.3
  33.9 0.7 copy-start.4
  43.4 9.2 %collective-permute-start.4 = (bf16[64,9,4,128]{3,2,1,0:T(4,128)(2,1)S(1)}, bf16[64,9,4,128]{3,2,1,0:T(4,128)(2,1)S(1)}, u32[]{:S(2)}, u32[]{:S(2)}) collective-permute-start(bf16[64,9,4,128]{3,2,1,0:T(4,128)(2,1)S(1)} %all-to-all-done.left_ref), channel_id=1, source_target_pairs={{0,8},{8,0},{1,9},{9,1},{2,10},{10,2},{3,11},{11,3},{4,12},{12,4},... | collective-permute-start | bytes 1769480 | tf_op jit(solution)/shard_map/ppermute | solution.py:125
  81.7 8.8 %collective-permute-start.5 = (bf16[8,3,4,256]{3,2,0,1:T(4,128)(2,1)S(1)}, bf16[8,3,4,256]{3,2,0,1:T(4,128)(2,1)S(1)}, u32[]{:S(2)}, u32[]{:S(2)}) collective-permute-start(bf16[8,3,4,256]{3,2,0,1:T(4,128)(2,1)S(1)} %bitcast.26), channel_id=1, source_target_pairs={{0,8},{8,0},{1,9},{9,1},{2,10},{10,2},{3,11},{11,3},{4,12},{12,4},... | collective-permute-start | bytes 147464 | tf_op jit(solution)/shard_map/ppermute | solution.py:140
  90.8 0.9 copy-start.2

commit v5 on v2

v5 whole, which is shorter than its diff:
```python
import jax
import jax.numpy as jnp
from jax import lax
from jax.experimental import pallas as pl
from jax.experimental.pallas import tpu as pltpu
from jax.sharding import Mesh, PartitionSpec as P

Y, X, CORE, Z = 8, 4, 2, 8
LANES = 128
SWAP = ((0, 1), (1, 0))
UP = tuple((i, (i + 1) % X) for i in range(X))
DOWN = tuple((i, (i - 1) % X) for i in range(X))
VMEM = pl.BlockSpec(memory_space=pltpu.VMEM)
SMEM = pl.BlockSpec(memory_space=pltpu.SMEM)
ANY = pl.BlockSpec(memory_space=pl.ANY)
PARTS = 4
GRANT = 32 * 1024 * 1024


def pick_kernel(kept_ref, amplitudes_ref, out_ref, held, sems):
    tiles, keep = kept_ref.shape
    rows = amplitudes_ref.shape[0]
    repeat = Y // tiles
    copies = []
    for a in range(tiles):
        for k in range(keep):
            tile = kept_ref[a, k]
            for r in range(rows):
                held[a, :, r * keep + k] = amplitudes_ref[r, tile]
        for i in range(repeat):
            y = a * repeat + i
            copies.append(pltpu.make_async_copy(held.at[a], out_ref.at[y], sems.at[y]))
            copies[-1].start()
    for copy in copies:
        copy.wait()


def pick(kept_tiles, amplitudes):
    rows, tiles, width = amplitudes.shape
    keep = kept_tiles.shape[1]
    split = amplitudes.reshape(rows, tiles, Z, width // Z // LANES, LANES)
    shape = (Z, rows * keep, width // Z // LANES, LANES)
    return pl.pallas_call(
        pick_kernel,
        out_shape=jax.ShapeDtypeStruct((Y,) + shape, amplitudes.dtype),
        in_specs=[SMEM, VMEM],
        out_specs=ANY,
        scratch_shapes=[
            pltpu.VMEM((kept_tiles.shape[0],) + shape, amplitudes.dtype),
            pltpu.SemaphoreType.DMA((Y,)),
        ],
        cost_estimate=pl.CostEstimate(flops=10**11, bytes_accessed=10**6, transcendentals=0),
        compiler_params=pltpu.CompilerParams(vmem_limit_bytes=GRANT),
    )(kept_tiles, split)


def call(kernel, out_shape, scalars, arrays, work, far=(), scratch=()):
    return pl.pallas_call(
        kernel,
        out_shape=out_shape,
        in_specs=[SMEM] * len(scalars) + [VMEM] * len(arrays) + [ANY] * len(far),
        out_specs=VMEM,
        scratch_shapes=list(scratch),
        cost_estimate=pl.CostEstimate(flops=work, bytes_accessed=1000, transcendentals=0),
        compiler_params=pltpu.CompilerParams(vmem_limit_bytes=GRANT),
    )(*scalars, *arrays, *far)


def low_kernel(in_ref, out_ref):
    out_ref[...] = in_ref[:, :out_ref.shape[1]]


def high_kernel(in_ref, out_ref):
    out_ref[...] = in_ref[:, out_ref.shape[1]:]


def join_kernel(low_ref, high_ref, out_ref):
    half = low_ref.shape[1]
    out_ref[:, :half] = low_ref[...]
    out_ref[:, half:] = high_ref[...]


def rows_kernel(in_ref, out_ref, held, sems):
    rows, keep, peers, _ = out_ref.shape
    chunks, lanes = in_ref.shape[2:]
    part = peers // PARTS
    spans = [pl.ds(p * part, part) for p in range(PARTS)]
    copies = [pltpu.make_async_copy(in_ref.at[span], held.at[span], sems.at[p]) for p, span in enumerate(spans)]
    for copy in copies:
        copy.start()
    for p, copy in enumerate(copies):
        copy.wait()
        low = p * part
        for r in range(rows):
            for k in range(keep):
                for c in range(chunks):
                    at = slice(c * lanes, (c + 1) * lanes)
                    out_ref[r, k, low:low + part, at] = held[low:low + part, r * keep + k, c]


def dots(left_ref, right):
    rows, keep, peers, share = left_ref.shape
    total = None
    for k in range(keep):
        part = lax.dot_general(
            left_ref[:, k].reshape(rows * peers, share),
            right(k),
            (((1,), (1,)), ((), ())),
            preferred_element_type=jnp.float32,
        )
        total = part if total is None else total + part
    return total.astype(jnp.bfloat16).reshape(rows, peers, -1)


def near_kernel(left_ref, own_ref, below_ref, above_ref, out_ref, held, sems):
    keep, block, _ = own_ref.shape
    copies = [pltpu.make_async_copy(above_ref.at[k], held.at[k], sems.at[k]) for k in range(keep)]
    for copy in copies:
        copy.start()
    for j, ref in enumerate((own_ref, below_ref, held)):
        if ref is held:
            for copy in copies:
                copy.wait()
        out_ref[:, :, j * block:(j + 1) * block] = dots(left_ref, lambda k: ref[k])


def far_kernel(core_ref, _, mine_ref, theirs_ref, far_ref, near_mine, near_theirs, out_ref):
    low = near_mine.shape[2]
    for side, (left_ref, near_ref) in enumerate(((mine_ref, near_mine), (theirs_ref, near_theirs))):
        owner = lax.rem(core_ref[0] + side, CORE)
        out_ref[owner, :, :, low:] = dots(left_ref, lambda k: far_ref[k])
        out_ref[owner, :, :, :low] = near_ref[...]


def place_kernel(x_ref, residual_ref, ladder_ref, out_ref):
    groups, cores, _, columns = ladder_ref.shape
    block = columns // X
    for core in range(cores):
        for low, step in enumerate((0, X - 1, 1, 2)):
            at = (lax.rem(x_ref[0] + step, X) * cores + core) * block
            for y in range(groups):
                place = pl.ds(pl.multiple_of(y * X * cores * block + at, block), block)
                ladder = ladder_ref[y, core, :, low * block:(low + 1) * block].astype(jnp.float32)
                total = residual_ref[:, place].astype(jnp.float32) + ladder
                out_ref[:, place] = total.astype(out_ref.dtype)


def shards(amplitudes, integrals, residual_in, kept_tiles):
    rows, tiles, width = amplitudes.shape
    keep = kept_tiles.shape[1]
    share = width // Z
    block = integrals.shape[1]
    x = lax.axis_index("x")
    core = lax.axis_index("c")

    below = lax.ppermute(integrals, "x", UP)
    above = lax.ppermute(integrals, "x", DOWN)
    cut = jax.ShapeDtypeStruct((keep, block // 2, share), integrals.dtype)
    far_low = lax.ppermute(call(low_kernel, cut, (), (below,), 10**11), "x", UP)
    far_high = lax.ppermute(call(high_kernel, cut, (), (above,), 10**11), "x", DOWN)

    outgoing = pick(kept_tiles, amplitudes)
    outgoing = outgoing.reshape(Y * Z, rows * keep, share // LANES, LANES)
    mine = lax.all_to_all(outgoing, ("y", "z"), split_axis=0, concat_axis=0, tiled=True)
    left = jax.ShapeDtypeStruct((rows, keep, Y * Z, share), mine.dtype)
    held = pltpu.VMEM(mine.shape, mine.dtype)
    mine = call(rows_kernel, left, (), (), 1000, (mine,), (held, pltpu.SemaphoreType.DMA((PARTS,))))
    theirs = lax.ppermute(mine, "c", SWAP)

    near_shape = jax.ShapeDtypeStruct((rows, Y * Z, 3 * block), jnp.bfloat16)
    all_shape = jax.ShapeDtypeStruct((CORE, rows, Y * Z, X * block), jnp.bfloat16)
    held = jax.ShapeDtypeStruct(integrals.shape, integrals.dtype)
    room = (pltpu.VMEM(integrals.shape, integrals.dtype), pltpu.SemaphoreType.DMA((keep,)))
    near = [
        call(near_kernel, near_shape, (), (left, integrals, below), 1000, (above,), room)
        for left in (mine, theirs)
    ]
    far = call(join_kernel, held, (), (far_low, far_high), 10**11)
    where = x.astype(jnp.int32).reshape(1)
    which = core.astype(jnp.int32).reshape(1)
    partial = call(far_kernel, all_shape, (which, where), (mine, theirs, far, *near), 1000)
    partial = partial.reshape(CORE, rows, Y, Z, 2, X * block // 2).transpose(2, 0, 3, 1, 4, 5)
    partial = partial.reshape(Y * CORE * Z, rows, 2, X * block // 2)
    returned = lax.all_to_all(partial, ("y", "c", "z"), split_axis=0, concat_axis=0, tiled=True)
    returned = returned.reshape(Y, CORE, Z, rows, 2, X * block // 2).astype(jnp.float32)
    ladder = jnp.sum(returned, axis=2).astype(jnp.bfloat16).reshape(Y, CORE, rows, X * block)
    out = jax.ShapeDtypeStruct(residual_in.shape, residual_in.dtype)
    return call(place_kernel, out, (where,), (residual_in, ladder), 1000)


def solution(mesh):
    fine = Mesh(mesh.devices.reshape(Y, X, CORE, Z), ("y", "x", "c", "z"))
    owner = ("y", "x", "c", "z")
    in_specs = (
        P(owner, None, None),
        P(None, ("y", "x", "c"), "z"),
        P(owner, None),
        P(),
    )
    return jax.shard_map(
        shards, mesh=fine, in_specs=in_specs, out_specs=P(owner, None), check_vma=False
    )
```

time: 124 us -> 92.3 us (0.74)
  blocking collectives: 60.6 us -> 32.2 us
  waiting for transfers between devices: 26.9 us -> 9.01 us
  starting transfers between devices: 22 us -> 37 us
  Pallas kernels: 0 us -> 9.77 us
  matrix products: 7.03 us -> 0 us
    all_to_all x2 -> x1, blocking collectives: 60.6 us -> 32.2 us  [shards(): lax.all_to_all(partial, ('y', 'c', 'z'), split_axis=0, concat_axis=0, til...]
    ppermute x2, waiting for transfers between devices: 16.9 us -> 0.01 us  [the longest x1 0.01 us: shards(): lax.ppermute(call(low_kernel, cut, (), (below,), 10 ** 11), 'x', UP)]
    all_to_all x0 -> x1, starting transfers between devices: none -> 16.7 us  [shards(): lax.all_to_all(outgoing, ('y', 'z'), split_axis=0, concat_axis=0, tiled=T...]
    ppermute x1, waiting for transfers between devices: 9.99 us -> 0.01 us  [shards(): below = lax.ppermute(integrals, 'x', UP)]
    pallas_call x0 -> x9, Pallas kernels: none -> 9.77 us  [the longest x8 8.27 us: call(): pl.pallas_call(kernel, out_shape=out_shape, in_specs=[SMEM] * len(scalars...]
    all_to_all x0 -> x1, waiting for transfers between devices: none -> 9 us  [shards(): lax.all_to_all(outgoing, ('y', 'z'), split_axis=0, concat_axis=0, tiled=T...]
    dot_general x5 -> x0, matrix products: 7.03 us -> none  [the longest x4 6.75 us: product(): jnp.einsum('drosc,sac->droa', left, right, preferred_element_type=jnp.flo...]
    ppermute x2, starting transfers between devices: 10.1 us -> 6.62 us  [the longest x1 4.7 us: shards(): lax.ppermute(call(high_kernel, cut, (), (above,), 10 ** 11), 'x', DOWN)]
  transfers between devices with their start and end apart: 5 -> 6, of which waited for: 3 -> 1; matrix products, arithmetic and copies ran while one was open for 4% -> 1% of each run, Pallas kernels for 0% -> 7%
where the time goes in v5:
time: 92.3 us; the launch traced here: 91.8 us
  starting transfers between devices  37 us (40%)
  blocking collectives  32.2 us (35%)
  Pallas kernels  9.77 us (11%)
  waiting for transfers between devices  9.01 us (10%)
  local copies, waits for them, and re-layouts  2.84 us (3%)
    all_to_all x1, blocking collectives, shards(): lax.all_to_all(partial, ('y', 'c', 'z'), split_axis=0, concat_axis=0, til...  32.2 us
    all_to_all x1, starting transfers between devices, shards(): lax.all_to_all(outgoing, ('y', 'z'), split_axis=0, concat_axis=0, tiled=T...  16.7 us
    all_to_all x1, waiting for transfers between devices, shards(): lax.all_to_all(outgoing, ('y', 'z'), split_axis=0, concat_axis=0, tiled=T...  9 us
    pallas_call x8, Pallas kernels, call(): pl.pallas_call(kernel, out_shape=out_shape, in_specs=[SMEM] * len(scalars...  8.27 us
    ppermute x1, starting transfers between devices, shards(): theirs = lax.ppermute(mine, 'c', SWAP)  6.42 us
    ppermute x1, starting transfers between devices, shards(): lax.ppermute(call(high_kernel, cut, (), (above,), 10 ** 11), 'x', DOWN)  4.7 us
    ppermute x1, starting transfers between devices, shards(): below = lax.ppermute(integrals, 'x', UP)  4.07 us
    ppermute x1, starting transfers between devices, shards(): above = lax.ppermute(integrals, 'x', DOWN)  3.19 us
  transfers between devices with their start and end apart: 6, of which 1 were waited for; matrix products, arithmetic and copies ran while one was open for 1% of the time, Pallas kernels for 7%

profile of v5, /device:TPU:1, one launch (start us, length us, event | category | flops | bytes accessed | tf_op | source)
XLA Modules:
  0.0 91.8 jit_solution(9897737774727298930)
XLA Ops:
  0.0 0.0 copy-start.2
  0.0 4.1 %collective-permute-start.1 = (bf16[3,256,512]{2,1,0:T(8,128)(2,1)}, bf16[3,256,512]{2,1,0:T(8,128)(2,1)S(1)}, u32[]{:S(2)}, u32[]{:S(2)}) collective-permute-start(bf16[3,256,512]{2,1,0:T(8,128)(2,1)} %own_ref.3), channel_id=1, source_target_pairs={{0,16},{16,32},{32,48},{48,0},{1,17},{17,33},{33,49},{49,1},{2,18}... | collective-permute-start | bytes 2359304 | tf_op jit(solution)/shard_map/ppermute | solution.py:156
  4.1 3.2 %collective-permute-start.3 = (bf16[3,256,512]{2,1,0:T(8,128)(2,1)}, bf16[3,256,512]{2,1,0:T(8,128)(2,1)}, u32[]{:S(2)}, u32[]{:S(2)}) collective-permute-start(bf16[3,256,512]{2,1,0:T(8,128)(2,1)} %own_ref.3), channel_id=1, source_target_pairs={{0,48},{16,0},{32,16},{48,32},{1,49},{17,1},{33,17},{49,33},{2,50}... | collective-permute-start | bytes 2359304 | tf_op jit(solution)/shard_map/ppermute | solution.py:157
  7.3 1.0 %reshape.26.amplitudes_ref = bf16[3,8,8,4,128]{4,3,2,1,0:T(4,128)(2,1)S(1)} reshape(bf16[3,8,4096]{2,1,0:T(8,128)(2,1)} %param.4) | data formatting | bytes 393216 | tf_op jit(solution)/shard_map/reshape | solution.py:41
  8.3 0.0 copy-done.2
  8.3 1.5 %shard_map.46 = bf16[8,8,9,4,128]{4,3,2,1,0:T(4,128)(2,1)} custom-call(s32[4,3]{1,0:T(4,128)S(1)} %copy-done.2, bf16[3,8,8,4,128]{4,3,2,1,0:T(4,128)(2,1)S(1)} %reshape.26.amplitudes_ref), custom_call_target="tpu_custom_call" | custom-call | flops 99999997952 | bytes 1000000 | tf_op jit(solution)/shard_map/pallas_call | solution.py:43
  9.8 16.7 %all-to-all-start = ((bf16[64,9,4,128]{3,2,1,0:T(4,128)(2,1)}), bf16[64,9,4,128]{3,2,1,0:T(4,128)(2,1)}, u32[]{:S(2)}, u32[]{:S(2)}) async-start(bf16[64,9,4,128]{3,2,1,0:T(4,128)(2,1)} %bitcast.2), calls=%async_computation | async-start | bytes 1179648 | tf_op jit(solution)/shard_map/all_to_all | solution.py:164
  26.6 0.0 collective-permute-done.1.in_ref.below_ref
  26.6 1.9 %collective-permute-start.2 = (bf16[3,128,512]{2,1,0:T(8,128)(2,1)S(1)}, bf16[3,128,512]{2,1,0:T(8,128)(2,1)S(1)}, u32[]{:S(2)}, u32[]{:S(2)}) collective-permute-start(bf16[3,128,512]{2,1,0:T(8,128)(2,1)S(1)} %shard_map.48), channel_id=1, source_target_pairs={{0,16},{16,32},{32,48},{48,0},{1,17},{17,33},{33,49},{49,1},{2,18}... | collective-permute-start | bytes 1179656 | tf_op jit(solution)/shard_map/ppermute | solution.py:159
  28.6 0.0 collective-permute-done.3.in_ref.above_ref
  28.6 1.2 %shard_map.49 = bf16[3,128,512]{2,1,0:T(8,128)(2,1)S(1)} custom-call(bf16[3,256,512]{2,1,0:T(8,128)(2,1)} %collective-permute-done.3.in_ref.above_ref), custom_call_target="tpu_custom_call" | custom-call | flops 99999997952 | bytes 1000 | tf_op jit(solution)/shard_map/pallas_call | solution.py:58
  29.7 0.0 copy-start
  29.8 4.7 %collective-permute-start.4 = (bf16[3,128,512]{2,1,0:T(8,128)(2,1)S(1)}, bf16[3,128,512]{2,1,0:T(8,128)(2,1)S(1)}, u32[]{:S(2)}, u32[]{:S(2)}) collective-permute-start(bf16[3,128,512]{2,1,0:T(8,128)(2,1)S(1)} %shard_map.49), channel_id=1, source_target_pairs={{0,48},{16,0},{32,16},{48,32},{1,49},{17,1},{33,17},{49,33},{2,50}... | collective-permute-start | bytes 1179656 | tf_op jit(solution)/shard_map/ppermute | solution.py:160
  34.5 9.0 %all-to-all-done.in_ref = bf16[64,9,4,128]{3,2,1,0:T(4,128)(2,1)} async-done(((bf16[64,9,4,128]{3,2,1,0:T(4,128)(2,1)}), bf16[64,9,4,128]{3,2,1,0:T(4,128)(2,1)}, u32[]{:S(2)}, u32[]{:S(2)}) %all-to-all-start) | async-done | bytes 589856 | tf_op jit(solution)/shard_map/all_to_all | solution.py:164
  43.5 1.8 %shard_map.47.left_ref.mine_ref = bf16[3,3,64,512]{3,2,1,0:T(8,128)(2,1)S(1)} custom-call(bf16[64,9,4,128]{3,2,1,0:T(4,128)(2,1)} %all-to-all-done.in_ref), custom_call_target="tpu_custom_call" | custom-call | flops 1000 | bytes 1000 | tf_op jit(solution)/shard_map/pallas_call | solution.py:58
  45.3 6.4 %collective-permute-start = (bf16[3,3,64,512]{3,2,1,0:T(8,128)(2,1)S(1)}, bf16[3,3,64,512]{3,2,1,0:T(8,128)(2,1)S(1)}, u32[]{:S(2)}, u32[]{:S(2)}) collective-permute-start(bf16[3,3,64,512]{3,2,1,0:T(8,128)(2,1)S(1)} %shard_map.47.left_ref.mine_ref), channel_id=1, source_target_pairs={{0,8},{8,0},{1,9},{9,1},{2,10},{10,2},{3,11},{11,3},{4,12},{12,4},... | collective-permute-start | bytes 1769480 | tf_op jit(solution)/shard_map/ppermute | solution.py:168
  51.7 0.0 copy-done
  51.7 1.8 %shard_map.51.near_mine = bf16[3,64,768]{2,1,0:T(8,128)(2,1)S(1)} custom-call(bf16[3,3,64,512]{3,2,1,0:T(8,128)(2,1)S(1)} %shard_map.47.left_ref.mine_ref, bf16[3,256,512]{2,1,0:T(8,128)(2,1)S(1)} %copy-done, bf16[3,256,512]{2,1,0:T(8,128)(2,1)S(1)} %collective-permute-done.1.in_ref.below_ref, bf16[3,256,512]{2,1,0:T(8,128)(2,1)} %collective-permute-done.3.in_ref.above_ref), custom_call_target="tpu_custom_call" | custom-call | flops 1000 | bytes 1000 | tf_op jit(solution)/shard_map/pallas_call | solution.py:58
  53.6 0.0 collective-permute-done.2.low_ref
  53.6 0.0 collective-permute-done.4.high_ref
  53.6 0.1 shard_map.50.far_ref
  53.7 0.0 collective-permute-done.left_ref.theirs_ref
  53.7 1.8 %shard_map.52.near_theirs = bf16[3,64,768]{2,1,0:T(8,128)(2,1)S(1)} custom-call(bf16[3,3,64,512]{3,2,1,0:T(8,128)(2,1)S(1)} %collective-permute-done.left_ref.theirs_ref, bf16[3,256,512]{2,1,0:T(8,128)(2,1)S(1)} %copy-done, bf16[3,256,512]{2,1,0:T(8,128)(2,1)S(1)} %collective-permute-done.1.in_ref.below_ref, ...), custom_call_target="tpu_custom_call" | custom-call | flops 1000 | bytes 1000 | tf_op jit(solution)/shard_map/pallas_call | solution.py:58
  55.5 0.7 shard_map.53
  56.2 0.1 copy.7
  56.3 0.8 copy.8
  57.1 32.2 %all_to_all.10 = bf16[128,3,2,512]{3,2,1,0:T(2,128)(2,1)S(1)} all-to-all(bf16[128,3,2,512]{3,2,1,0:T(2,128)(2,1)S(1)} %copy.8), channel_id=1, replica_groups=mesh['y'=8,'x'=4,'c'=2,'z'=8] {'y','c','z'}, dimensions={0} | all-to-all | bytes 1572864 | tf_op jit(solution)/shard_map/all_to_all | solution.py:184
  89.3 0.7 bitcast_reduce_fusion
  90.0 0.0 copy-start.1
  90.0 0.1 reshape.32.ladder_ref
  90.1 0.8 copy-done.1
  90.9 0.9 shard_map.54
  (1 shorter events, 0.0 us)
Async XLA Ops:
  0.0 8.3 %copy-start.2 = (s32[4,3]{1,0:T(4,128)S(1)}, s32[4,3]{1,0:T(4,128)}, u32[]{:S(2)}) copy-start(s32[4,3]{1,0:T(4,128)} %kept_ref.1) | copy-start | bytes 148
  0.0 26.6 %collective-permute-start.1 = (bf16[3,256,512]{2,1,0:T(8,128)(2,1)}, bf16[3,256,512]{2,1,0:T(8,128)(2,1)S(1)}, u32[]{:S(2)}, u32[]{:S(2)}) collective-permute-start(bf16[3,256,512]{2,1,0:T(8,128)(2,1)} %own_ref.3), channel_id=1, source_target_pairs={{0,16},{16,32},{32,48},{48,0},{1,17},{17,33},{33,49},{49,1},{2,18}... | collective-permute-start | bytes 2359304 | tf_op jit(solution)/shard_map/ppermute | solution.py:156
  4.1 24.5 %collective-permute-start.3 = (bf16[3,256,512]{2,1,0:T(8,128)(2,1)}, bf16[3,256,512]{2,1,0:T(8,128)(2,1)}, u32[]{:S(2)}, u32[]{:S(2)}) collective-permute-start(bf16[3,256,512]{2,1,0:T(8,128)(2,1)} %own_ref.3), channel_id=1, source_target_pairs={{0,48},{16,0},{32,16},{48,32},{1,49},{17,1},{33,17},{49,33},{2,50}... | collective-permute-start | bytes 2359304 | tf_op jit(solution)/shard_map/ppermute | solution.py:157
  9.8 33.6 %all-to-all-start = ((bf16[64,9,4,128]{3,2,1,0:T(4,128)(2,1)}), bf16[64,9,4,128]{3,2,1,0:T(4,128)(2,1)}, u32[]{:S(2)}, u32[]{:S(2)}) async-start(bf16[64,9,4,128]{3,2,1,0:T(4,128)(2,1)} %bitcast.2), calls=%async_computation | async-start | bytes 1179648 | tf_op jit(solution)/shard_map/all_to_all | solution.py:164
  26.6 26.9 %collective-permute-start.2 = (bf16[3,128,512]{2,1,0:T(8,128)(2,1)S(1)}, bf16[3,128,512]{2,1,0:T(8,128)(2,1)S(1)}, u32[]{:S(2)}, u32[]{:S(2)}) collective-permute-start(bf16[3,128,512]{2,1,0:T(8,128)(2,1)S(1)} %shard_map.48), channel_id=1, source_target_pairs={{0,16},{16,32},{32,48},{48,0},{1,17},{17,33},{33,49},{49,1},{2,18}... | collective-permute-start | bytes 1179656 | tf_op jit(solution)/shard_map/ppermute | solution.py:159
  29.7 22.0 %copy-start = (bf16[3,256,512]{2,1,0:T(8,128)(2,1)S(1)}, bf16[3,256,512]{2,1,0:T(8,128)(2,1)}, u32[]{:S(2)}) copy-start(bf16[3,256,512]{2,1,0:T(8,128)(2,1)} %own_ref.3) | copy-start | bytes 2359300
  29.8 23.8 %collective-permute-start.4 = (bf16[3,128,512]{2,1,0:T(8,128)(2,1)S(1)}, bf16[3,128,512]{2,1,0:T(8,128)(2,1)S(1)}, u32[]{:S(2)}, u32[]{:S(2)}) collective-permute-start(bf16[3,128,512]{2,1,0:T(8,128)(2,1)S(1)} %shard_map.49), channel_id=1, source_target_pairs={{0,48},{16,0},{32,16},{48,32},{1,49},{17,1},{33,17},{49,33},{2,50}... | collective-permute-start | bytes 1179656 | tf_op jit(solution)/shard_map/ppermute | solution.py:160
  45.3 8.4 %collective-permute-start = (bf16[3,3,64,512]{3,2,1,0:T(8,128)(2,1)S(1)}, bf16[3,3,64,512]{3,2,1,0:T(8,128)(2,1)S(1)}, u32[]{:S(2)}, u32[]{:S(2)}) collective-permute-start(bf16[3,3,64,512]{3,2,1,0:T(8,128)(2,1)S(1)} %shard_map.47.left_ref.mine_ref), channel_id=1, source_target_pairs={{0,8},{8,0},{1,9},{9,1},{2,10},{10,2},{3,11},{11,3},{4,12},{12,4},... | collective-permute-start | bytes 1769480 | tf_op jit(solution)/shard_map/ppermute | solution.py:168
  90.0 0.9 copy-start.1

commit v6 on v5

v6 whole, which is shorter than its diff:
```python
import jax
import jax.numpy as jnp
from jax import lax
from jax.experimental import pallas as pl
from jax.experimental.pallas import tpu as pltpu
from jax.sharding import Mesh, PartitionSpec as P

Y, X, CORE, Z = 8, 4, 2, 8
LANES = 128
SWAP = ((0, 1), (1, 0))
SAME = tuple((2 * i + c, 2 * ((i + 1 - 2 * c) % X) + c) for i in range(X) for c in range(CORE))
CROSS = tuple((2 * i + 1 - c, 2 * ((i + 1 - 2 * c) % X) + c) for i in range(X) for c in range(CORE))
HELD = (((0, 0), (X - 1, 0), (X - 1, 1), (2, 0)), ((0, 1), (1, 1), (1, 0), (2, 1)))
VMEM = pl.BlockSpec(memory_space=pltpu.VMEM)
SMEM = pl.BlockSpec(memory_space=pltpu.SMEM)
ANY = pl.BlockSpec(memory_space=pl.ANY)
GRANT = 32 * 1024 * 1024


def pick_kernel(kept_ref, amplitudes_ref, out_ref, held, sems):
    tiles, keep = kept_ref.shape
    rows = amplitudes_ref.shape[0]
    repeat = Y // tiles
    copies = []
    for a in range(tiles):
        for k in range(keep):
            tile = kept_ref[a, k]
            for r in range(rows):
                held[a, :, r * keep + k] = amplitudes_ref[r, tile]
        for i in range(repeat):
            y = a * repeat + i
            copies.append(pltpu.make_async_copy(held.at[a], out_ref.at[y], sems.at[y]))
            copies[-1].start()
    for copy in copies:
        copy.wait()


def pick(kept_tiles, amplitudes):
    rows, tiles, width = amplitudes.shape
    keep = kept_tiles.shape[1]
    split = amplitudes.reshape(rows, tiles, Z, width // Z // LANES, LANES)
    shape = (Z, rows * keep, width // Z // LANES, LANES)
    return pl.pallas_call(
        pick_kernel,
        out_shape=jax.ShapeDtypeStruct((Y,) + shape, amplitudes.dtype),
        in_specs=[SMEM, VMEM],
        out_specs=ANY,
        scratch_shapes=[
            pltpu.VMEM((kept_tiles.shape[0],) + shape, amplitudes.dtype),
            pltpu.SemaphoreType.DMA((Y,)),
        ],
        cost_estimate=pl.CostEstimate(flops=10**11, bytes_accessed=10**6, transcendentals=0),
        compiler_params=pltpu.CompilerParams(vmem_limit_bytes=GRANT),
    )(kept_tiles, split)


def call(kernel, out_shape, scalars, arrays, work, far=(), scratch=()):
    return pl.pallas_call(
        kernel,
        out_shape=out_shape,
        in_specs=[SMEM] * len(scalars) + [VMEM] * len(arrays) + [ANY] * len(far),
        out_specs=(VMEM,) * len(out_shape) if isinstance(out_shape, tuple) else VMEM,
        scratch_shapes=list(scratch),
        cost_estimate=pl.CostEstimate(flops=work, bytes_accessed=1000, transcendentals=0),
        compiler_params=pltpu.CompilerParams(vmem_limit_bytes=GRANT),
    )(*scalars, *arrays, *far)


def hold_kernel(a_ref, b_ref, a_out, b_out):
    pass


def in_place(kernel, arrays, kept, scratch):
    shapes = tuple(jax.ShapeDtypeStruct(a.shape, a.dtype) for a in arrays)
    return pl.pallas_call(
        kernel,
        out_shape=shapes,
        in_specs=[ANY] * len(arrays),
        out_specs=(ANY,) * len(arrays),
        scratch_shapes=scratch,
        input_output_aliases={i: i for i in range(kept)},
        cost_estimate=pl.CostEstimate(flops=10**11, bytes_accessed=10**6, transcendentals=0),
        compiler_params=pltpu.CompilerParams(vmem_limit_bytes=GRANT),
    )(*arrays)


def rows_kernel(in_ref, out_ref):
    rows, keep, _, _ = out_ref.shape
    chunks, lanes = in_ref.shape[2:]
    for r in range(rows):
        for k in range(keep):
            for c in range(chunks):
                out_ref[r, k, :, c * lanes:(c + 1) * lanes] = in_ref[:, r * keep + k, c]


def dots(left_ref, right_ref):
    rows, keep, peers, share = left_ref.shape
    total = None
    for k in range(keep):
        part = lax.dot_general(
            left_ref[:, k].reshape(rows * peers, share),
            right_ref[k],
            (((1,), (1,)), ((), ())),
            preferred_element_type=jnp.float32,
        )
        total = part if total is None else total + part
    return total.astype(jnp.bfloat16).reshape(rows, peers, -1)


def near_kernel(left_ref, *refs):
    rights, out_ref = refs[:-1], refs[-1]
    block = rights[0].shape[1]
    for j, right_ref in enumerate(rights):
        out_ref[:, :, j * block:(j + 1) * block] = dots(left_ref, right_ref)


def rest_kernel(core_ref, _, mine_ref, theirs_ref, near_mine, near_theirs, residual_ref, right_ref, *refs):
    out_ref, residual_out, held, sems = refs
    keep = right_ref.shape[0]
    low = near_mine.shape[2]
    copies = [pltpu.make_async_copy(right_ref.at[k], held.at[k], sems.at[k]) for k in range(keep)]
    for copy in copies:
        copy.start()
    extra = pltpu.make_async_copy(residual_ref, residual_out, sems.at[keep])
    extra.start()
    owners = [lax.rem(core_ref[0] + side, CORE) for side in range(CORE)]
    for owner, near_ref in zip(owners, (near_mine, near_theirs)):
        out_ref[owner, :, :, :low] = near_ref[...]
    for copy in copies:
        copy.wait()
    for owner, left_ref in zip(owners, (mine_ref, theirs_ref)):
        out_ref[owner, :, :, low:] = dots(left_ref, held)
    extra.wait()


def place_kernel(x_ref, residual_ref, ladder_ref, out_ref):
    groups, cores, _, columns = ladder_ref.shape
    block = columns // X
    for core in range(cores):
        for low, (step, side) in enumerate(HELD[core]):
            at = (lax.rem(x_ref[0] + step, X) * cores + side) * block
            for y in range(groups):
                place = pl.ds(pl.multiple_of(y * X * cores * block + at, block), block)
                ladder = ladder_ref[y, core, :, low * block:(low + 1) * block].astype(jnp.float32)
                total = residual_ref[:, place].astype(jnp.float32) + ladder
                out_ref[:, place] = total.astype(out_ref.dtype)


def shards(amplitudes, integrals, residual_in, kept_tiles):
    rows, tiles, width = amplitudes.shape
    keep = kept_tiles.shape[1]
    share = width // Z
    block = integrals.shape[1]
    x = lax.axis_index("x")
    core = lax.axis_index("c")

    first = lax.ppermute(integrals, ("x", "c"), SAME)
    second = lax.ppermute(integrals, ("x", "c"), CROSS)
    first, second = in_place(hold_kernel, (first, second), 2, [])
    third = lax.ppermute(first, ("x", "c"), SAME)

    outgoing = pick(kept_tiles, amplitudes)
    outgoing = outgoing.reshape(Y * Z, rows * keep, share // LANES, LANES)
    mine = lax.all_to_all(outgoing, ("y", "z"), split_axis=0, concat_axis=0, tiled=True)
    left = jax.ShapeDtypeStruct((rows, keep, Y * Z, share), mine.dtype)
    mine = call(rows_kernel, left, (), (mine,), 1000)
    theirs = lax.ppermute(mine, "c", SWAP)

    all_shape = jax.ShapeDtypeStruct((CORE, rows, Y * Z, X * block), jnp.bfloat16)
    near_shape = jax.ShapeDtypeStruct((rows, Y * Z, 3 * block), jnp.bfloat16)
    near = [call(near_kernel, near_shape, (), (a, integrals, first, second), 1000) for a in (mine, theirs)]
    where = x.astype(jnp.int32).reshape(1)
    which = core.astype(jnp.int32).reshape(1)
    out = jax.ShapeDtypeStruct(residual_in.shape, residual_in.dtype)
    room = (pltpu.VMEM(third.shape, third.dtype), pltpu.SemaphoreType.DMA((keep + 1,)))
    partial, residual = call(
        rest_kernel, (all_shape, out), (which, where), (mine, theirs, *near), 1000, (residual_in, third), room
    )
    partial = partial.reshape(CORE, rows, Y, Z, 2, X * block // 2).transpose(2, 0, 3, 1, 4, 5)
    partial = partial.reshape(Y * CORE * Z, rows, 2, X * block // 2)
    returned = lax.all_to_all(partial, ("y", "c", "z"), split_axis=0, concat_axis=0, tiled=True)
    returned = returned.reshape(Y, CORE, Z, rows, 2, X * block // 2).astype(jnp.float32)
    ladder = jnp.sum(returned, axis=2).astype(jnp.bfloat16).reshape(Y, CORE, rows, X * block)
    return call(place_kernel, out, (where,), (residual, ladder), 1000)


def solution(mesh):
    fine = Mesh(mesh.devices.reshape(Y, X, CORE, Z), ("y", "x", "c", "z"))
    owner = ("y", "x", "c", "z")
    in_specs = (
        P(owner, None, None),
        P(None, ("y", "x", "c"), "z"),
        P(owner, None),
        P(),
    )
    return jax.shard_map(
        shards, mesh=fine, in_specs=in_specs, out_specs=P(owner, None), check_vma=False
    )
```

time: 92.3 us -> 91.2 us (0.988)
  waiting for transfers between devices: 9.01 us -> 14.2 us
  starting transfers between devices: 37 us -> 33.5 us
  Pallas kernels: 9.77 us -> 7.05 us
  blocking collectives: 32.2 us -> 33.2 us
    all_to_all x1, waiting for transfers between devices: 9 us -> 13.5 us  [shards(): lax.all_to_all(outgoing, ('y', 'z'), split_axis=0, concat_axis=0, tiled=T...]
    pallas_call x8 -> x5, Pallas kernels: 8.27 us -> 5.53 us  [call(): pl.pallas_call(kernel, out_shape=out_shape, in_specs=[SMEM] * len(scalars...]
    ppermute x1, starting transfers between devices: 6.42 us -> 4.4 us  [shards(): theirs = lax.ppermute(mine, 'c', SWAP)]
    ppermute x4 -> x3, starting transfers between devices: 13.9 us -> 12.8 us  [the longest x1 5.34 us: shards(): first = lax.ppermute(integrals, ('x', 'c'), SAME)]
    all_to_all x1, blocking collectives: 32.2 us -> 33.2 us  [shards(): lax.all_to_all(partial, ('y', 'c', 'z'), split_axis=0, concat_axis=0, til...]
  transfers between devices with their start and end apart: 6 -> 5, of which waited for: 1 -> 2; matrix products, arithmetic and copies ran while one was open for 1% -> 1% of each run, Pallas kernels for 7% -> 5%
where the time goes in v6:
time: 91.2 us; the launch traced here: 90.8 us
  starting transfers between devices  33.5 us (37%)
  blocking collectives  33.2 us (36%)
  waiting for transfers between devices  14.2 us (16%)
  Pallas kernels  7.05 us (8%)
  local copies, waits for them, and re-layouts  2.03 us (2%)
    all_to_all x1, blocking collectives, shards(): lax.all_to_all(partial, ('y', 'c', 'z'), split_axis=0, concat_axis=0, til...  33.2 us
    all_to_all x1, starting transfers between devices, shards(): lax.all_to_all(outgoing, ('y', 'z'), split_axis=0, concat_axis=0, tiled=T...  16.3 us
    all_to_all x1, waiting for transfers between devices, shards(): lax.all_to_all(outgoing, ('y', 'z'), split_axis=0, concat_axis=0, tiled=T...  13.5 us
    pallas_call x5, Pallas kernels, call(): pl.pallas_call(kernel, out_shape=out_shape, in_specs=[SMEM] * len(scalars...  5.53 us
    ppermute x1, starting transfers between devices, shards(): first = lax.ppermute(integrals, ('x', 'c'), SAME)  5.34 us
    ppermute x1, starting transfers between devices, shards(): third = lax.ppermute(first, ('x', 'c'), SAME)  4.74 us
    ppermute x1, starting transfers between devices, shards(): theirs = lax.ppermute(mine, 'c', SWAP)  4.4 us
    ppermute x1, starting transfers between devices, shards(): second = lax.ppermute(integrals, ('x', 'c'), CROSS)  2.69 us
  transfers between devices with their start and end apart: 5, of which 2 were waited for; matrix products, arithmetic and copies ran while one was open for 1% of the time, Pallas kernels for 5%

profile of v6, /device:TPU:1, one launch (start us, length us, event | category | flops | bytes accessed | tf_op | source)
XLA Modules:
  0.0 90.8 jit_solution(10549590332503610165)
XLA Ops:
  0.0 0.0 copy-start.2
  0.0 5.3 %collective-permute-start.1 = (bf16[3,256,512]{2,1,0:T(8,128)(2,1)}, bf16[3,256,512]{2,1,0:T(8,128)(2,1)S(1)}, u32[]{:S(2)}, u32[]{:S(2)}) collective-permute-start(bf16[3,256,512]{2,1,0:T(8,128)(2,1)} %refs_0_.3), channel_id=1, source_target_pairs={{0,16},{8,56},{16,32},{24,8},{32,48},{40,24},{48,0},{56,40},{1,17}... | collective-permute-start | bytes 2359304 | tf_op jit(solution)/shard_map/ppermute | solution.py:157
  5.3 2.7 %collective-permute-start.2 = (bf16[3,256,512]{2,1,0:T(8,128)(2,1)}, bf16[3,256,512]{2,1,0:T(8,128)(2,1)S(1)}, u32[]{:S(2)}, u32[]{:S(2)}) collective-permute-start(bf16[3,256,512]{2,1,0:T(8,128)(2,1)} %refs_0_.3), channel_id=1, source_target_pairs={{8,16},{0,56},{24,32},{16,8},{40,48},{32,24},{56,0},{48,40},{9,17}... | collective-permute-start | bytes 2359304 | tf_op jit(solution)/shard_map/ppermute | solution.py:158
  8.1 1.0 %reshape.26.amplitudes_ref = bf16[3,8,8,4,128]{4,3,2,1,0:T(4,128)(2,1)S(1)} reshape(bf16[3,8,4096]{2,1,0:T(8,128)(2,1)} %param.4) | data formatting | bytes 393216 | tf_op jit(solution)/shard_map/reshape | solution.py:41
  9.1 0.0 copy-done.2
  9.1 1.5 %shard_map.46 = bf16[8,8,9,4,128]{4,3,2,1,0:T(4,128)(2,1)} custom-call(s32[4,3]{1,0:T(4,128)S(1)} %copy-done.2, bf16[3,8,8,4,128]{4,3,2,1,0:T(4,128)(2,1)S(1)} %reshape.26.amplitudes_ref), custom_call_target="tpu_custom_call" | custom-call | flops 99999997952 | bytes 1000000 | tf_op jit(solution)/shard_map/pallas_call | solution.py:43
  10.6 16.3 %all-to-all-start = ((bf16[64,9,4,128]{3,2,1,0:T(4,128)(2,1)}), bf16[64,9,4,128]{3,2,1,0:T(4,128)(2,1)S(1)}, u32[]{:S(2)}, u32[]{:S(2)}) async-start(bf16[64,9,4,128]{3,2,1,0:T(4,128)(2,1)} %bitcast.2), calls=%async_computation | async-start | bytes 1179648 | tf_op jit(solution)/shard_map/all_to_all | solution.py:164
  27.0 0.0 collective-permute-done.1.a_ref
  27.0 0.0 collective-permute-done.2.b_ref
  27.0 0.0 copy-start
  27.0 4.7 %collective-permute-start.3 = (bf16[3,256,512]{2,1,0:T(8,128)(2,1)S(1)}, bf16[3,256,512]{2,1,0:T(8,128)(2,1)}, u32[]{:S(2)}, u32[]{:S(2)}) collective-permute-start(bf16[3,256,512]{2,1,0:T(8,128)(2,1)S(1)} %get-tuple-element.9.refs_1_), channel_id=1, source_target_pairs={{0,16},{8,56},{16,32},{24,8},{32,48},{40,24},{48,0},{56,40},{1,17}... | collective-permute-start | bytes 2359304 | tf_op jit(solution)/shard_map/ppermute | solution.py:160
  31.8 13.5 %all-to-all-done.in_ref = bf16[64,9,4,128]{3,2,1,0:T(4,128)(2,1)S(1)} async-done(((bf16[64,9,4,128]{3,2,1,0:T(4,128)(2,1)}), bf16[64,9,4,128]{3,2,1,0:T(4,128)(2,1)S(1)}, u32[]{:S(2)}, u32[]{:S(2)}) %all-to-all-start) | async-done | bytes 589856 | tf_op jit(solution)/shard_map/all_to_all | solution.py:164
  45.3 1.1 %shard_map.47.left_ref.mine_ref = bf16[3,3,64,512]{3,2,1,0:T(8,128)(2,1)S(1)} custom-call(bf16[64,9,4,128]{3,2,1,0:T(4,128)(2,1)S(1)} %all-to-all-done.in_ref), custom_call_target="tpu_custom_call" | custom-call | flops 1000 | bytes 1000 | tf_op jit(solution)/shard_map/pallas_call | solution.py:58
  46.4 4.4 %collective-permute-start = (bf16[3,3,64,512]{3,2,1,0:T(8,128)(2,1)S(1)}, bf16[3,3,64,512]{3,2,1,0:T(8,128)(2,1)S(1)}, u32[]{:S(2)}, u32[]{:S(2)}) collective-permute-start(bf16[3,3,64,512]{3,2,1,0:T(8,128)(2,1)S(1)} %shard_map.47.left_ref.mine_ref), channel_id=1, source_target_pairs={{0,8},{8,0},{1,9},{9,1},{2,10},{10,2},{3,11},{11,3},{4,12},{12,4},... | collective-permute-start | bytes 1769480 | tf_op jit(solution)/shard_map/ppermute | solution.py:167
  50.8 0.0 copy-done
  50.8 0.9 shard_map.49.near_mine
  51.7 0.0 copy-start.1
  51.7 0.7 collective-permute-done.left_ref.theirs_ref
  52.4 0.9 shard_map.50.near_theirs
  53.3 0.0 collective-permute-done.3.right_ref
  53.3 0.0 copy-done.1
  53.3 1.8 %shard_map.51 = (bf16[2,3,64,1024]{3,2,1,0:T(8,128)(2,1)S(1)}, bf16[3,16384]{1,0:T(4,128)(2,1)S(1)}) custom-call(s32[1]{0:T(128)} %bitcast.1.core_ref, s32[1]{0:T(128)} %bitcast._.x_ref, bf16[3,3,64,512]{3,2,1,0:T(8,128)(2,1)S(1)} %shard_map.47.left_ref.mine_ref, bf16[3,3,64,512]{3,2,1,0:T(8,128)(2,1)S(1)} %collective-permute-done.left_ref.theirs_ref, ...), custom_call_target="tpu_custom_call" | custom-call | flops 1000 | bytes 1000 | tf_op jit(solution)/shard_map/pallas_call | solution.py:58
  55.1 0.1 copy.9
  55.2 0.8 copy.10
  56.0 33.2 %all_to_all.10 = bf16[128,3,2,512]{3,2,1,0:T(2,128)(2,1)S(1)} all-to-all(bf16[128,3,2,512]{3,2,1,0:T(2,128)(2,1)S(1)} %copy.10), channel_id=1, replica_groups=mesh['y'=8,'x'=4,'c'=2,'z'=8] {'y','c','z'}, dimensions={0} | all-to-all | bytes 1572864 | tf_op jit(solution)/shard_map/all_to_all | solution.py:181
  89.2 0.7 bitcast_reduce_fusion
  89.9 0.1 reshape.32.ladder_ref
  90.0 0.8 shard_map.52
  (1 shorter events, 0.0 us)
Async XLA Ops:
  0.0 9.1 %copy-start.2 = (s32[4,3]{1,0:T(4,128)S(1)}, s32[4,3]{1,0:T(4,128)}, u32[]{:S(2)}) copy-start(s32[4,3]{1,0:T(4,128)} %kept_ref.1) | copy-start | bytes 148
  0.0 27.0 %collective-permute-start.1 = (bf16[3,256,512]{2,1,0:T(8,128)(2,1)}, bf16[3,256,512]{2,1,0:T(8,128)(2,1)S(1)}, u32[]{:S(2)}, u32[]{:S(2)}) collective-permute-start(bf16[3,256,512]{2,1,0:T(8,128)(2,1)} %refs_0_.3), channel_id=1, source_target_pairs={{0,16},{8,56},{16,32},{24,8},{32,48},{40,24},{48,0},{56,40},{1,17}... | collective-permute-start | bytes 2359304 | tf_op jit(solution)/shard_map/ppermute | solution.py:157
  5.3 21.6 %collective-permute-start.2 = (bf16[3,256,512]{2,1,0:T(8,128)(2,1)}, bf16[3,256,512]{2,1,0:T(8,128)(2,1)S(1)}, u32[]{:S(2)}, u32[]{:S(2)}) collective-permute-start(bf16[3,256,512]{2,1,0:T(8,128)(2,1)} %refs_0_.3), channel_id=1, source_target_pairs={{8,16},{0,56},{24,32},{16,8},{40,48},{32,24},{56,0},{48,40},{9,17}... | collective-permute-start | bytes 2359304 | tf_op jit(solution)/shard_map/ppermute | solution.py:158
  10.6 34.7 %all-to-all-start = ((bf16[64,9,4,128]{3,2,1,0:T(4,128)(2,1)}), bf16[64,9,4,128]{3,2,1,0:T(4,128)(2,1)S(1)}, u32[]{:S(2)}, u32[]{:S(2)}) async-start(bf16[64,9,4,128]{3,2,1,0:T(4,128)(2,1)} %bitcast.2), calls=%async_computation | async-start | bytes 1179648 | tf_op jit(solution)/shard_map/all_to_all | solution.py:164
  27.0 23.8 %copy-start = (bf16[3,256,512]{2,1,0:T(8,128)(2,1)S(1)}, bf16[3,256,512]{2,1,0:T(8,128)(2,1)}, u32[]{:S(2)}) copy-start(bf16[3,256,512]{2,1,0:T(8,128)(2,1)} %refs_0_.3) | copy-start | bytes 2359300
  27.0 26.3 %collective-permute-start.3 = (bf16[3,256,512]{2,1,0:T(8,128)(2,1)S(1)}, bf16[3,256,512]{2,1,0:T(8,128)(2,1)}, u32[]{:S(2)}, u32[]{:S(2)}) collective-permute-start(bf16[3,256,512]{2,1,0:T(8,128)(2,1)S(1)} %get-tuple-element.9.refs_1_), channel_id=1, source_target_pairs={{0,16},{8,56},{16,32},{24,8},{32,48},{40,24},{48,0},{56,40},{1,17}... | collective-permute-start | bytes 2359304 | tf_op jit(solution)/shard_map/ppermute | solution.py:160
  46.4 6.0 %collective-permute-start = (bf16[3,3,64,512]{3,2,1,0:T(8,128)(2,1)S(1)}, bf16[3,3,64,512]{3,2,1,0:T(8,128)(2,1)S(1)}, u32[]{:S(2)}, u32[]{:S(2)}) collective-permute-start(bf16[3,3,64,512]{3,2,1,0:T(8,128)(2,1)S(1)} %shard_map.47.left_ref.mine_ref), channel_id=1, source_target_pairs={{0,8},{8,0},{1,9},{9,1},{2,10},{10,2},{3,11},{11,3},{4,12},{12,4},... | collective-permute-start | bytes 1769480 | tf_op jit(solution)/shard_map/ppermute | solution.py:167
  51.7 1.6 %copy-start.1 = (bf16[3,16384]{1,0:T(4,128)(2,1)S(1)}, bf16[3,16384]{1,0:T(4,128)(2,1)}, u32[]{:S(2)}) copy-start(bf16[3,16384]{1,0:T(4,128)(2,1)} %residual_ref.1) | copy-start | bytes 294916

commit v7 on v6

--- a/solution.py
+++ b/solution.py
@@ -84,13 +84,15 @@
     )(*arrays)
 
 
-def rows_kernel(in_ref, out_ref):
-    rows, keep, _, _ = out_ref.shape
-    chunks, lanes = in_ref.shape[2:]
+def arrange(in_ref, wide, left_ref):
+    rows, keep, peers, share = left_ref.shape
+    chunks = share // LANES
+    wide[...] = in_ref[...].astype(jnp.float32)
     for r in range(rows):
         for k in range(keep):
             for c in range(chunks):
-                out_ref[r, k, :, c * lanes:(c + 1) * lanes] = in_ref[:, r * keep + k, c]
+                at = pl.ds((r * keep + k) * chunks + c, peers, rows * keep * chunks)
+                left_ref[r, k, :, c * LANES:(c + 1) * LANES] = wide[at, :].astype(left_ref.dtype)
 
 
 def dots(left_ref, right_ref):
@@ -104,32 +106,50 @@
             preferred_element_type=jnp.float32,
         )
         total = part if total is None else total + part
-    return total.astype(jnp.bfloat16).reshape(rows, peers, -1)
-
-
-def near_kernel(left_ref, *refs):
-    rights, out_ref = refs[:-1], refs[-1]
+    return total
+
+
+def near_kernel(in_ref, *refs):
+    rights, (left_ref, out_ref, wide) = refs[:-3], refs[-3:]
     block = rights[0].shape[1]
+    arrange(in_ref, wide, left_ref)
     for j, right_ref in enumerate(rights):
-        out_ref[:, :, j * block:(j + 1) * block] = dots(left_ref, right_ref)
-
-
-def rest_kernel(core_ref, _, mine_ref, theirs_ref, near_mine, near_theirs, residual_ref, right_ref, *refs):
-    out_ref, residual_out, held, sems = refs
-    keep = right_ref.shape[0]
-    low = near_mine.shape[2]
-    copies = [pltpu.make_async_copy(right_ref.at[k], held.at[k], sems.at[k]) for k in range(keep)]
+        out_ref[:, j * block:(j + 1) * block] = dots(left_ref, right_ref)
+
+
+def rest_kernel(core_ref, _, mine_ref, near_ref, in_ref, *refs):
+    rights = refs[:-9]
+    residual_ref, third_ref, out_ref, residual_out, theirs_ref, held, wide, strips, sems = refs[-9:]
+    rows, keep, _, _ = mine_ref.shape
+    block = third_ref.shape[1]
+    chunks = X * block // LANES
+    copies = [pltpu.make_async_copy(third_ref.at[k], held.at[k], sems.at[k]) for k in range(keep)]
     for copy in copies:
         copy.start()
     extra = pltpu.make_async_copy(residual_ref, residual_out, sems.at[keep])
     extra.start()
-    owners = [lax.rem(core_ref[0] + side, CORE) for side in range(CORE)]
-    for owner, near_ref in zip(owners, (near_mine, near_theirs)):
-        out_ref[owner, :, :, :low] = near_ref[...]
+
+    def put(side, low, values):
+        for r in range(rows):
+            for y in range(Y):
+                for c in range(values.shape[1] // LANES):
+                    start = ((side * Y + y) * Z * rows + r) * chunks + low // LANES + c
+                    piece = values[(r * Y + y) * Z:(r * Y + y + 1) * Z, c * LANES:(c + 1) * LANES]
+                    strips[pl.ds(start, Z, rows * chunks), :] = piece
+
+    arrange(in_ref, wide, theirs_ref)
+    put(0, 0, near_ref[...])
+    for j, right_ref in enumerate(rights):
+        put(1, j * block, dots(theirs_ref, right_ref))
     for copy in copies:
         copy.wait()
-    for owner, left_ref in zip(owners, (mine_ref, theirs_ref)):
-        out_ref[owner, :, :, low:] = dots(left_ref, held)
+    for side, left_ref in enumerate((mine_ref, theirs_ref)):
+        put(side, len(rights) * block, dots(left_ref, held))
+        owner = lax.rem(core_ref[0] + side, CORE)
+        size = Z * rows * chunks
+        for y in range(Y):
+            start = (side * Y + y) * size
+            out_ref[y, owner] = strips[start:start + size, :].astype(out_ref.dtype)
     extra.wait()
 
 
@@ -163,23 +183,37 @@
     outgoing = outgoing.reshape(Y * Z, rows * keep, share // LANES, LANES)
     mine = lax.all_to_all(outgoing, ("y", "z"), split_axis=0, concat_axis=0, tiled=True)
     left = jax.ShapeDtypeStruct((rows, keep, Y * Z, share), mine.dtype)
-    mine = call(rows_kernel, left, (), (mine,), 1000)
     theirs = lax.ppermute(mine, "c", SWAP)
 
-    all_shape = jax.ShapeDtypeStruct((CORE, rows, Y * Z, X * block), jnp.bfloat16)
-    near_shape = jax.ShapeDtypeStruct((rows, Y * Z, 3 * block), jnp.bfloat16)
-    near = [call(near_kernel, near_shape, (), (a, integrals, first, second), 1000) for a in (mine, theirs)]
+    chunks = X * block // LANES
+    all_shape = jax.ShapeDtypeStruct((Y, CORE, Z * rows * chunks, LANES), jnp.bfloat16)
+    mine = mine.reshape(-1, LANES)
+    wide = pltpu.VMEM(mine.shape, jnp.float32)
+    near_shape = jax.ShapeDtypeStruct((rows * Y * Z, 3 * block), jnp.float32)
+    near_blocks = (integrals, first, second)
+    mine, near = call(near_kernel, (left, near_shape), (), (mine, *near_blocks), 1000, (), (wide,))
     where = x.astype(jnp.int32).reshape(1)
     which = core.astype(jnp.int32).reshape(1)
     out = jax.ShapeDtypeStruct(residual_in.shape, residual_in.dtype)
-    room = (pltpu.VMEM(third.shape, third.dtype), pltpu.SemaphoreType.DMA((keep + 1,)))
+    room = (
+        pltpu.VMEM(left.shape, left.dtype),
+        pltpu.VMEM(third.shape, third.dtype),
+        wide,
+        pltpu.VMEM((CORE * Y * Z * rows * chunks, LANES), jnp.float32),
+        pltpu.SemaphoreType.DMA((keep + 1,)),
+    )
     partial, residual = call(
-        rest_kernel, (all_shape, out), (which, where), (mine, theirs, *near), 1000, (residual_in, third), room
-    )
-    partial = partial.reshape(CORE, rows, Y, Z, 2, X * block // 2).transpose(2, 0, 3, 1, 4, 5)
-    partial = partial.reshape(Y * CORE * Z, rows, 2, X * block // 2)
+        rest_kernel,
+        (all_shape, out),
+        (which, where),
+        (mine, near, theirs.reshape(-1, LANES), *near_blocks),
+        1000,
+        (residual_in, third),
+        room,
+    )
+    partial = partial.reshape(Y * CORE * Z, rows * chunks, LANES)
     returned = lax.all_to_all(partial, ("y", "c", "z"), split_axis=0, concat_axis=0, tiled=True)
-    returned = returned.reshape(Y, CORE, Z, rows, 2, X * block // 2).astype(jnp.float32)
+    returned = returned.reshape(Y, CORE, Z, rows * chunks, LANES).astype(jnp.float32)
     ladder = jnp.sum(returned, axis=2).astype(jnp.bfloat16).reshape(Y, CORE, rows, X * block)
     return call(place_kernel, out, (where,), (residual, ladder), 1000)
 

time: 91.2 us -> 87.8 us (0.963)
  starting transfers between devices: 33.5 us -> 31.7 us
  Pallas kernels: 7.05 us -> 5.28 us
  waiting for transfers between devices: 14.2 us -> 15.5 us
  local copies, waits for them, and re-layouts: 2.03 us -> 1.09 us
    all_to_all x1, starting transfers between devices: 16.3 us -> 10.9 us  [shards(): lax.all_to_all(outgoing, ('y', 'z'), split_axis=0, concat_axis=0, tiled=T...]
    ppermute x1, starting transfers between devices: 5.34 us -> 8.75 us  [shards(): first = lax.ppermute(integrals, ('x', 'c'), SAME)]
    ppermute x1, starting transfers between devices: 2.69 us -> 4.63 us  [shards(): second = lax.ppermute(integrals, ('x', 'c'), CROSS)]
    pallas_call x5 -> x3, Pallas kernels: 5.53 us -> 3.78 us  [call(): pl.pallas_call(kernel, out_shape=out_shape, in_specs=[SMEM] * len(scalars...]
    ppermute x1, starting transfers between devices: 4.4 us -> 2.69 us  [shards(): theirs = lax.ppermute(mine, 'c', SWAP)]
    all_to_all x1, waiting for transfers between devices: 13.5 us -> 14.9 us  [shards(): lax.all_to_all(outgoing, ('y', 'z'), split_axis=0, concat_axis=0, tiled=T...]
  transfers between devices with their start and end apart: 5 -> 5, of which waited for: 2 -> 2; matrix products, arithmetic and copies ran while one was open for 1% -> 1% of each run, Pallas kernels for 5% -> 3%
where the time goes in v7:
time: 87.8 us; the launch traced here: 87.5 us
  blocking collectives  33.6 us (38%)
  starting transfers between devices  31.7 us (36%)
  waiting for transfers between devices  15.5 us (18%)
  Pallas kernels  5.28 us (6%)
  local copies, waits for them, and re-layouts  1.09 us (1%)
    all_to_all x1, blocking collectives, shards(): lax.all_to_all(partial, ('y', 'c', 'z'), split_axis=0, concat_axis=0, til...  33.6 us
    all_to_all x1, waiting for transfers between devices, shards(): lax.all_to_all(outgoing, ('y', 'z'), split_axis=0, concat_axis=0, tiled=T...  14.9 us
    all_to_all x1, starting transfers between devices, shards(): lax.all_to_all(outgoing, ('y', 'z'), split_axis=0, concat_axis=0, tiled=T...  10.9 us
    ppermute x1, starting transfers between devices, shards(): first = lax.ppermute(integrals, ('x', 'c'), SAME)  8.75 us
    ppermute x1, starting transfers between devices, shards(): third = lax.ppermute(first, ('x', 'c'), SAME)  4.71 us
    ppermute x1, starting transfers between devices, shards(): second = lax.ppermute(integrals, ('x', 'c'), CROSS)  4.63 us
    pallas_call x3, Pallas kernels, call(): pl.pallas_call(kernel, out_shape=out_shape, in_specs=[SMEM] * len(scalars...  3.78 us
    ppermute x1, starting transfers between devices, shards(): theirs = lax.ppermute(mine, 'c', SWAP)  2.69 us
  transfers between devices with their start and end apart: 5, of which 2 were waited for; matrix products, arithmetic and copies ran while one was open for 1% of the time, Pallas kernels for 3%

profile of v7, /device:TPU:1, one launch (start us, length us, event | category | flops | bytes accessed | tf_op | source)
XLA Modules:
  0.0 87.5 jit_solution(18006519011066341508)
XLA Ops:
  0.0 0.0 copy-start.2
  0.0 4.6 %collective-permute-start.1 = (bf16[3,256,512]{2,1,0:T(8,128)(2,1)}, bf16[3,256,512]{2,1,0:T(8,128)(2,1)S(1)}, u32[]{:S(2)}, u32[]{:S(2)}) collective-permute-start(bf16[3,256,512]{2,1,0:T(8,128)(2,1)} %refs_0_.3), channel_id=1, source_target_pairs={{8,16},{0,56},{24,32},{16,8},{40,48},{32,24},{56,0},{48,40},{9,17}... | collective-permute-start | bytes 2359304 | tf_op jit(solution)/shard_map/ppermute | solution.py:178
  4.6 8.7 %collective-permute-start = (bf16[3,256,512]{2,1,0:T(8,128)(2,1)}, bf16[3,256,512]{2,1,0:T(8,128)(2,1)S(1)}, u32[]{:S(2)}, u32[]{:S(2)}) collective-permute-start(bf16[3,256,512]{2,1,0:T(8,128)(2,1)} %refs_0_.3), channel_id=1, source_target_pairs={{0,16},{8,56},{16,32},{24,8},{32,48},{40,24},{48,0},{56,40},{1,17}... | collective-permute-start | bytes 2359304 | tf_op jit(solution)/shard_map/ppermute | solution.py:177
  13.4 1.0 %reshape.29.amplitudes_ref = bf16[3,8,8,4,128]{4,3,2,1,0:T(4,128)(2,1)S(1)} reshape(bf16[3,8,4096]{2,1,0:T(8,128)(2,1)} %param.4) | data formatting | bytes 393216 | tf_op jit(solution)/shard_map/reshape | solution.py:41
  14.4 0.0 copy-done.2
  14.5 1.5 %shard_map.46 = bf16[8,8,9,4,128]{4,3,2,1,0:T(4,128)(2,1)} custom-call(s32[4,3]{1,0:T(4,128)S(1)} %copy-done.2, bf16[3,8,8,4,128]{4,3,2,1,0:T(4,128)(2,1)S(1)} %reshape.29.amplitudes_ref), custom_call_target="tpu_custom_call" | custom-call | flops 99999997952 | bytes 1000000 | tf_op jit(solution)/shard_map/pallas_call | solution.py:43
  16.0 10.9 %all-to-all-start = ((bf16[64,9,4,128]{3,2,1,0:T(4,128)(2,1)}), bf16[64,9,4,128]{3,2,1,0:T(4,128)(2,1)S(1)}, u32[]{:S(2)}, u32[]{:S(2)}) async-start(bf16[64,9,4,128]{3,2,1,0:T(4,128)(2,1)} %bitcast.2), calls=%async_computation | async-start | bytes 1179648 | tf_op jit(solution)/shard_map/all_to_all | solution.py:184
  26.9 0.0 copy-start
  26.9 0.0 collective-permute-done.1.b_ref
  26.9 0.0 collective-permute-done.a_ref
  27.0 4.7 %collective-permute-start.3 = (bf16[3,256,512]{2,1,0:T(8,128)(2,1)S(1)}, bf16[3,256,512]{2,1,0:T(8,128)(2,1)}, u32[]{:S(2)}, u32[]{:S(2)}) collective-permute-start(bf16[3,256,512]{2,1,0:T(8,128)(2,1)S(1)} %get-tuple-element.11.refs_1_), channel_id=1, source_target_pairs={{0,16},{8,56},{16,32},{24,8},{32,48},{40,24},{48,0},{56,40},{1,17}... | collective-permute-start | bytes 2359304 | tf_op jit(solution)/shard_map/ppermute | solution.py:180
  31.7 14.9 %all-to-all-done = bf16[64,9,4,128]{3,2,1,0:T(4,128)(2,1)S(1)} async-done(((bf16[64,9,4,128]{3,2,1,0:T(4,128)(2,1)}), bf16[64,9,4,128]{3,2,1,0:T(4,128)(2,1)S(1)}, u32[]{:S(2)}, u32[]{:S(2)}) %all-to-all-start) | async-done | bytes 589856 | tf_op jit(solution)/shard_map/all_to_all | solution.py:184
  46.5 2.7 %collective-permute-start.2 = (bf16[64,9,4,128]{3,2,1,0:T(4,128)(2,1)S(1)}, bf16[64,9,4,128]{3,2,1,0:T(4,128)(2,1)S(1)}, u32[]{:S(2)}, u32[]{:S(2)}) collective-permute-start(bf16[64,9,4,128]{3,2,1,0:T(4,128)(2,1)S(1)} %all-to-all-done), channel_id=1, source_target_pairs={{0,8},{8,0},{1,9},{9,1},{2,10},{10,2},{3,11},{11,3},{4,12},{12,4},... | collective-permute-start | bytes 1769480 | tf_op jit(solution)/shard_map/ppermute | solution.py:186
  49.2 0.0 copy-done
  49.3 0.0 copy-start.1
  49.3 0.9 %shard_map.48 = (bf16[3,3,64,512]{3,2,1,0:T(8,128)(2,1)S(1)}, f32[192,768]{1,0:T(8,128)S(1)}) custom-call(bf16[2304,128]{1,0:T(8,128)(2,1)S(1)} %bitcast.10, bf16[3,256,512]{2,1,0:T(8,128)(2,1)S(1)} %copy-done, bf16[3,256,512]{2,1,0:T(8,128)(2,1)S(1)} %get-tuple-element.11.refs_1_, bf16[3,256,512]{2,1,0:T(8,128)(2,1)S(1)} %get-tuple-element.12.refs_2_), custom_call_target="tpu_custom_call" | custom-call | flops 1000 | bytes 1000 | tf_op jit(solution)/shard_map/pallas_call | solution.py:58
  50.2 0.0 collective-permute-done.3.refs_4_
  50.2 0.6 collective-permute-done.2
  50.8 0.0 copy-done.1
  50.8 2.0 %shard_map.49 = (bf16[8,2,192,128]{3,2,1,0:T(8,128)(2,1)S(1)}, bf16[3,16384]{1,0:T(4,128)(2,1)S(1)}) custom-call(s32[1]{0:T(128)} %bitcast.1.core_ref, s32[1]{0:T(128)} %bitcast._.x_ref, bf16[3,3,64,512]{3,2,1,0:T(8,128)(2,1)S(1)} %get-tuple-element.13.mine_ref, f32[192,768]{1,0:T(8,128)S(1)} %get-tuple-element.14.near_ref, bf16[2304,128]{1,0:T(8,128)(2,1)S(1)} %bitcast.12, ...), custom_call_target="tpu_custom_call" | custom-call | flops 1000 | bytes 1000 | tf_op jit(solution)/shard_map/pallas_call | solution.py:58
  52.8 33.6 %all_to_all.10 = bf16[128,24,128]{2,1,0:T(8,128)(2,1)S(1)} all-to-all(bf16[128,24,128]{2,1,0:T(8,128)(2,1)S(1)} %bitcast.11), channel_id=1, replica_groups=mesh['y'=8,'x'=4,'c'=2,'z'=8] {'y','c','z'}, dimensions={0} | all-to-all | bytes 1572864 | tf_op jit(solution)/shard_map/all_to_all | solution.py:215
  86.5 0.1 bitcast_reduce_fusion
  86.6 0.8 shard_map.50
  (2 shorter events, 0.0 us)
Async XLA Ops:
  0.0 14.4 %copy-start.2 = (s32[4,3]{1,0:T(4,128)S(1)}, s32[4,3]{1,0:T(4,128)}, u32[]{:S(2)}) copy-start(s32[4,3]{1,0:T(4,128)} %kept_ref.1) | copy-start | bytes 148
  0.0 26.9 %collective-permute-start.1 = (bf16[3,256,512]{2,1,0:T(8,128)(2,1)}, bf16[3,256,512]{2,1,0:T(8,128)(2,1)S(1)}, u32[]{:S(2)}, u32[]{:S(2)}) collective-permute-start(bf16[3,256,512]{2,1,0:T(8,128)(2,1)} %refs_0_.3), channel_id=1, source_target_pairs={{8,16},{0,56},{24,32},{16,8},{40,48},{32,24},{56,0},{48,40},{9,17}... | collective-permute-start | bytes 2359304 | tf_op jit(solution)/shard_map/ppermute | solution.py:178
  4.6 22.3 %collective-permute-start = (bf16[3,256,512]{2,1,0:T(8,128)(2,1)}, bf16[3,256,512]{2,1,0:T(8,128)(2,1)S(1)}, u32[]{:S(2)}, u32[]{:S(2)}) collective-permute-start(bf16[3,256,512]{2,1,0:T(8,128)(2,1)} %refs_0_.3), channel_id=1, source_target_pairs={{0,16},{8,56},{16,32},{24,8},{32,48},{40,24},{48,0},{56,40},{1,17}... | collective-permute-start | bytes 2359304 | tf_op jit(solution)/shard_map/ppermute | solution.py:177
  16.0 30.6 %all-to-all-start = ((bf16[64,9,4,128]{3,2,1,0:T(4,128)(2,1)}), bf16[64,9,4,128]{3,2,1,0:T(4,128)(2,1)S(1)}, u32[]{:S(2)}, u32[]{:S(2)}) async-start(bf16[64,9,4,128]{3,2,1,0:T(4,128)(2,1)} %bitcast.2), calls=%async_computation | async-start | bytes 1179648 | tf_op jit(solution)/shard_map/all_to_all | solution.py:184
  26.9 22.3 %copy-start = (bf16[3,256,512]{2,1,0:T(8,128)(2,1)S(1)}, bf16[3,256,512]{2,1,0:T(8,128)(2,1)}, u32[]{:S(2)}) copy-start(bf16[3,256,512]{2,1,0:T(8,128)(2,1)} %refs_0_.3) | copy-start | bytes 2359300
  27.0 23.3 %collective-permute-start.3 = (bf16[3,256,512]{2,1,0:T(8,128)(2,1)S(1)}, bf16[3,256,512]{2,1,0:T(8,128)(2,1)}, u32[]{:S(2)}, u32[]{:S(2)}) collective-permute-start(bf16[3,256,512]{2,1,0:T(8,128)(2,1)S(1)} %get-tuple-element.11.refs_1_), channel_id=1, source_target_pairs={{0,16},{8,56},{16,32},{24,8},{32,48},{40,24},{48,0},{56,40},{1,17}... | collective-permute-start | bytes 2359304 | tf_op jit(solution)/shard_map/ppermute | solution.py:180
  46.5 4.3 %collective-permute-start.2 = (bf16[64,9,4,128]{3,2,1,0:T(4,128)(2,1)S(1)}, bf16[64,9,4,128]{3,2,1,0:T(4,128)(2,1)S(1)}, u32[]{:S(2)}, u32[]{:S(2)}) collective-permute-start(bf16[64,9,4,128]{3,2,1,0:T(4,128)(2,1)S(1)} %all-to-all-done), channel_id=1, source_target_pairs={{0,8},{8,0},{1,9},{9,1},{2,10},{10,2},{3,11},{11,3},{4,12},{12,4},... | collective-permute-start | bytes 1769480 | tf_op jit(solution)/shard_map/ppermute | solution.py:186
  49.3 1.6 %copy-start.1 = (bf16[3,16384]{1,0:T(4,128)(2,1)S(1)}, bf16[3,16384]{1,0:T(4,128)(2,1)}, u32[]{:S(2)}) copy-start(bf16[3,16384]{1,0:T(4,128)(2,1)} %refs_3_.1) | copy-start | bytes 294916

commit v8 on v7

--- a/solution.py
+++ b/solution.py
@@ -149,7 +149,8 @@
         size = Z * rows * chunks
         for y in range(Y):
             start = (side * Y + y) * size
-            out_ref[y, owner] = strips[start:start + size, :].astype(out_ref.dtype)
+            piece = strips[start:start + size, :].astype(out_ref.dtype)
+            out_ref[y, :, owner] = piece.reshape(Z, rows * chunks, LANES)
     extra.wait()
 
 
@@ -186,7 +187,7 @@
     theirs = lax.ppermute(mine, "c", SWAP)
 
     chunks = X * block // LANES
-    all_shape = jax.ShapeDtypeStruct((Y, CORE, Z * rows * chunks, LANES), jnp.bfloat16)
+    all_shape = jax.ShapeDtypeStruct((Y, Z, CORE, rows * chunks, LANES), jnp.bfloat16)
     mine = mine.reshape(-1, LANES)
     wide = pltpu.VMEM(mine.shape, jnp.float32)
     near_shape = jax.ShapeDtypeStruct((rows * Y * Z, 3 * block), jnp.float32)
@@ -212,9 +213,9 @@
         room,
     )
     partial = partial.reshape(Y * CORE * Z, rows * chunks, LANES)
-    returned = lax.all_to_all(partial, ("y", "c", "z"), split_axis=0, concat_axis=0, tiled=True)
-    returned = returned.reshape(Y, CORE, Z, rows * chunks, LANES).astype(jnp.float32)
-    ladder = jnp.sum(returned, axis=2).astype(jnp.bfloat16).reshape(Y, CORE, rows, X * block)
+    returned = lax.all_to_all(partial, ("y", "z", "c"), split_axis=0, concat_axis=0, tiled=True)
+    returned = returned.reshape(Y, Z, CORE, rows * chunks, LANES).astype(jnp.float32)
+    ladder = jnp.sum(returned, axis=1).astype(jnp.bfloat16).reshape(Y, CORE, rows, X * block)
     return call(place_kernel, out, (where,), (residual, ladder), 1000)
 
 

time: 87.8 us -> 86.5 us (0.985)
  blocking collectives: 33.6 us -> 32.3 us
    all_to_all x1, blocking collectives: 33.6 us -> 32.3 us  [shards(): lax.all_to_all(partial, ('y', 'z', 'c'), split_axis=0, concat_axis=0, til...]
where the time goes in v8:
time: 86.5 us; the launch traced here: 86.2 us
  blocking collectives  32.3 us (37%)
  starting transfers between devices  31.7 us (37%)
  waiting for transfers between devices  15.5 us (18%)
  Pallas kernels  5.31 us (6%)
  local copies, waits for them, and re-layouts  1.09 us (1%)
    all_to_all x1, blocking collectives, shards(): lax.all_to_all(partial, ('y', 'z', 'c'), split_axis=0, concat_axis=0, til...  32.3 us
    all_to_all x1, waiting for transfers between devices, shards(): lax.all_to_all(outgoing, ('y', 'z'), split_axis=0, concat_axis=0, tiled=T...  14.9 us
    all_to_all x1, starting transfers between devices, shards(): lax.all_to_all(outgoing, ('y', 'z'), split_axis=0, concat_axis=0, tiled=T...  10.9 us
    ppermute x1, starting transfers between devices, shards(): first = lax.ppermute(integrals, ('x', 'c'), SAME)  8.75 us
    ppermute x1, starting transfers between devices, shards(): third = lax.ppermute(first, ('x', 'c'), SAME)  4.71 us
    ppermute x1, starting transfers between devices, shards(): second = lax.ppermute(integrals, ('x', 'c'), CROSS)  4.63 us
    pallas_call x3, Pallas kernels, call(): pl.pallas_call(kernel, out_shape=out_shape, in_specs=[SMEM] * len(scalars...  3.81 us
    ppermute x1, starting transfers between devices, shards(): theirs = lax.ppermute(mine, 'c', SWAP)  2.69 us
  transfers between devices with their start and end apart: 5, of which 2 were waited for; matrix products, arithmetic and copies ran while one was open for 1% of the time, Pallas kernels for 3%

profile of v8, /device:TPU:1, one launch (start us, length us, event | category | flops | bytes accessed | tf_op | source)
XLA Modules:
  0.0 86.2 jit_solution(746366169458759075)
XLA Ops:
  0.0 0.0 copy-start.2
  0.0 4.6 %collective-permute-start.1 = (bf16[3,256,512]{2,1,0:T(8,128)(2,1)}, bf16[3,256,512]{2,1,0:T(8,128)(2,1)S(1)}, u32[]{:S(2)}, u32[]{:S(2)}) collective-permute-start(bf16[3,256,512]{2,1,0:T(8,128)(2,1)} %refs_0_.3), channel_id=1, source_target_pairs={{8,16},{0,56},{24,32},{16,8},{40,48},{32,24},{56,0},{48,40},{9,17}... | collective-permute-start | bytes 2359304 | tf_op jit(solution)/shard_map/ppermute | solution.py:179
  4.6 8.7 %collective-permute-start = (bf16[3,256,512]{2,1,0:T(8,128)(2,1)}, bf16[3,256,512]{2,1,0:T(8,128)(2,1)S(1)}, u32[]{:S(2)}, u32[]{:S(2)}) collective-permute-start(bf16[3,256,512]{2,1,0:T(8,128)(2,1)} %refs_0_.3), channel_id=1, source_target_pairs={{0,16},{8,56},{16,32},{24,8},{32,48},{40,24},{48,0},{56,40},{1,17}... | collective-permute-start | bytes 2359304 | tf_op jit(solution)/shard_map/ppermute | solution.py:178
  13.4 1.0 %reshape.29.amplitudes_ref = bf16[3,8,8,4,128]{4,3,2,1,0:T(4,128)(2,1)S(1)} reshape(bf16[3,8,4096]{2,1,0:T(8,128)(2,1)} %param.4) | data formatting | bytes 393216 | tf_op jit(solution)/shard_map/reshape | solution.py:41
  14.4 0.0 copy-done.2
  14.5 1.5 %shard_map.46 = bf16[8,8,9,4,128]{4,3,2,1,0:T(4,128)(2,1)} custom-call(s32[4,3]{1,0:T(4,128)S(1)} %copy-done.2, bf16[3,8,8,4,128]{4,3,2,1,0:T(4,128)(2,1)S(1)} %reshape.29.amplitudes_ref), custom_call_target="tpu_custom_call" | custom-call | flops 99999997952 | bytes 1000000 | tf_op jit(solution)/shard_map/pallas_call | solution.py:43
  16.0 10.9 %all-to-all-start = ((bf16[64,9,4,128]{3,2,1,0:T(4,128)(2,1)}), bf16[64,9,4,128]{3,2,1,0:T(4,128)(2,1)S(1)}, u32[]{:S(2)}, u32[]{:S(2)}) async-start(bf16[64,9,4,128]{3,2,1,0:T(4,128)(2,1)} %bitcast.2), calls=%async_computation | async-start | bytes 1179648 | tf_op jit(solution)/shard_map/all_to_all | solution.py:185
  26.9 0.0 copy-start
  26.9 0.0 collective-permute-done.1.b_ref
  26.9 0.0 collective-permute-done.a_ref
  27.0 4.7 %collective-permute-start.3 = (bf16[3,256,512]{2,1,0:T(8,128)(2,1)S(1)}, bf16[3,256,512]{2,1,0:T(8,128)(2,1)}, u32[]{:S(2)}, u32[]{:S(2)}) collective-permute-start(bf16[3,256,512]{2,1,0:T(8,128)(2,1)S(1)} %get-tuple-element.11.refs_1_), channel_id=1, source_target_pairs={{0,16},{8,56},{16,32},{24,8},{32,48},{40,24},{48,0},{56,40},{1,17}... | collective-permute-start | bytes 2359304 | tf_op jit(solution)/shard_map/ppermute | solution.py:181
  31.7 14.9 %all-to-all-done = bf16[64,9,4,128]{3,2,1,0:T(4,128)(2,1)S(1)} async-done(((bf16[64,9,4,128]{3,2,1,0:T(4,128)(2,1)}), bf16[64,9,4,128]{3,2,1,0:T(4,128)(2,1)S(1)}, u32[]{:S(2)}, u32[]{:S(2)}) %all-to-all-start) | async-done | bytes 589856 | tf_op jit(solution)/shard_map/all_to_all | solution.py:185
  46.5 2.7 %collective-permute-start.2 = (bf16[64,9,4,128]{3,2,1,0:T(4,128)(2,1)S(1)}, bf16[64,9,4,128]{3,2,1,0:T(4,128)(2,1)S(1)}, u32[]{:S(2)}, u32[]{:S(2)}) collective-permute-start(bf16[64,9,4,128]{3,2,1,0:T(4,128)(2,1)S(1)} %all-to-all-done), channel_id=1, source_target_pairs={{0,8},{8,0},{1,9},{9,1},{2,10},{10,2},{3,11},{11,3},{4,12},{12,4},... | collective-permute-start | bytes 1769480 | tf_op jit(solution)/shard_map/ppermute | solution.py:187
  49.2 0.0 copy-done
  49.3 0.0 copy-start.1
  49.3 0.9 %shard_map.48 = (bf16[3,3,64,512]{3,2,1,0:T(8,128)(2,1)S(1)}, f32[192,768]{1,0:T(8,128)S(1)}) custom-call(bf16[2304,128]{1,0:T(8,128)(2,1)S(1)} %bitcast.9, bf16[3,256,512]{2,1,0:T(8,128)(2,1)S(1)} %copy-done, bf16[3,256,512]{2,1,0:T(8,128)(2,1)S(1)} %get-tuple-element.11.refs_1_, bf16[3,256,512]{2,1,0:T(8,128)(2,1)S(1)} %get-tuple-element.12.refs_2_), custom_call_target="tpu_custom_call" | custom-call | flops 1000 | bytes 1000 | tf_op jit(solution)/shard_map/pallas_call | solution.py:58
  50.2 0.0 collective-permute-done.3.refs_4_
  50.2 0.6 collective-permute-done.2
  50.8 0.0 copy-done.1
  50.8 2.0 %shard_map.49 = (bf16[8,8,2,24,128]{4,3,2,1,0:T(8,128)(2,1)S(1)}, bf16[3,16384]{1,0:T(4,128)(2,1)S(1)}) custom-call(s32[1]{0:T(128)} %bitcast.1.core_ref, s32[1]{0:T(128)} %bitcast._.x_ref, bf16[3,3,64,512]{3,2,1,0:T(8,128)(2,1)S(1)} %get-tuple-element.13.mine_ref, f32[192,768]{1,0:T(8,128)S(1)} %get-tuple-element.14.near_ref, ...), custom_call_target="tpu_custom_call" | custom-call | flops 1000 | bytes 1000 | tf_op jit(solution)/shard_map/pallas_call | solution.py:58
  52.9 32.3 %all_to_all.10 = bf16[128,24,128]{2,1,0:T(8,128)(2,1)S(1)} all-to-all(bf16[128,24,128]{2,1,0:T(8,128)(2,1)S(1)} %bitcast.10), channel_id=1, replica_groups=mesh['y'=8,'x'=4,'c'=2,'z'=8] {'y','z','c'}, dimensions={0} | all-to-all | bytes 1572864 | tf_op jit(solution)/shard_map/all_to_all | solution.py:216
  85.2 0.1 reduce_sum.12
  85.3 0.8 shard_map.50
  (2 shorter events, 0.0 us)
Async XLA Ops:
  0.0 14.4 %copy-start.2 = (s32[4,3]{1,0:T(4,128)S(1)}, s32[4,3]{1,0:T(4,128)}, u32[]{:S(2)}) copy-start(s32[4,3]{1,0:T(4,128)} %kept_ref.1) | copy-start | bytes 148
  0.0 26.9 %collective-permute-start.1 = (bf16[3,256,512]{2,1,0:T(8,128)(2,1)}, bf16[3,256,512]{2,1,0:T(8,128)(2,1)S(1)}, u32[]{:S(2)}, u32[]{:S(2)}) collective-permute-start(bf16[3,256,512]{2,1,0:T(8,128)(2,1)} %refs_0_.3), channel_id=1, source_target_pairs={{8,16},{0,56},{24,32},{16,8},{40,48},{32,24},{56,0},{48,40},{9,17}... | collective-permute-start | bytes 2359304 | tf_op jit(solution)/shard_map/ppermute | solution.py:179
  4.6 22.3 %collective-permute-start = (bf16[3,256,512]{2,1,0:T(8,128)(2,1)}, bf16[3,256,512]{2,1,0:T(8,128)(2,1)S(1)}, u32[]{:S(2)}, u32[]{:S(2)}) collective-permute-start(bf16[3,256,512]{2,1,0:T(8,128)(2,1)} %refs_0_.3), channel_id=1, source_target_pairs={{0,16},{8,56},{16,32},{24,8},{32,48},{40,24},{48,0},{56,40},{1,17}... | collective-permute-start | bytes 2359304 | tf_op jit(solution)/shard_map/ppermute | solution.py:178
  16.0 30.6 %all-to-all-start = ((bf16[64,9,4,128]{3,2,1,0:T(4,128)(2,1)}), bf16[64,9,4,128]{3,2,1,0:T(4,128)(2,1)S(1)}, u32[]{:S(2)}, u32[]{:S(2)}) async-start(bf16[64,9,4,128]{3,2,1,0:T(4,128)(2,1)} %bitcast.2), calls=%async_computation | async-start | bytes 1179648 | tf_op jit(solution)/shard_map/all_to_all | solution.py:185
  26.9 22.3 %copy-start = (bf16[3,256,512]{2,1,0:T(8,128)(2,1)S(1)}, bf16[3,256,512]{2,1,0:T(8,128)(2,1)}, u32[]{:S(2)}) copy-start(bf16[3,256,512]{2,1,0:T(8,128)(2,1)} %refs_0_.3) | copy-start | bytes 2359300
  27.0 23.3 %collective-permute-start.3 = (bf16[3,256,512]{2,1,0:T(8,128)(2,1)S(1)}, bf16[3,256,512]{2,1,0:T(8,128)(2,1)}, u32[]{:S(2)}, u32[]{:S(2)}) collective-permute-start(bf16[3,256,512]{2,1,0:T(8,128)(2,1)S(1)} %get-tuple-element.11.refs_1_), channel_id=1, source_target_pairs={{0,16},{8,56},{16,32},{24,8},{32,48},{40,24},{48,0},{56,40},{1,17}... | collective-permute-start | bytes 2359304 | tf_op jit(solution)/shard_map/ppermute | solution.py:181
  46.5 4.3 %collective-permute-start.2 = (bf16[64,9,4,128]{3,2,1,0:T(4,128)(2,1)S(1)}, bf16[64,9,4,128]{3,2,1,0:T(4,128)(2,1)S(1)}, u32[]{:S(2)}, u32[]{:S(2)}) collective-permute-start(bf16[64,9,4,128]{3,2,1,0:T(4,128)(2,1)S(1)} %all-to-all-done), channel_id=1, source_target_pairs={{0,8},{8,0},{1,9},{9,1},{2,10},{10,2},{3,11},{11,3},{4,12},{12,4},... | collective-permute-start | bytes 1769480 | tf_op jit(solution)/shard_map/ppermute | solution.py:187
  49.3 1.6 %copy-start.1 = (bf16[3,16384]{1,0:T(4,128)(2,1)S(1)}, bf16[3,16384]{1,0:T(4,128)(2,1)}, u32[]{:S(2)}) copy-start(bf16[3,16384]{1,0:T(4,128)(2,1)} %refs_3_.1) | copy-start | bytes 294916

commit v9 on v8

--- a/solution.py
+++ b/solution.py
@@ -11,6 +11,8 @@
 SAME = tuple((2 * i + c, 2 * ((i + 1 - 2 * c) % X) + c) for i in range(X) for c in range(CORE))
 CROSS = tuple((2 * i + 1 - c, 2 * ((i + 1 - 2 * c) % X) + c) for i in range(X) for c in range(CORE))
 HELD = (((0, 0), (X - 1, 0), (X - 1, 1), (2, 0)), ((0, 1), (1, 1), (1, 0), (2, 1)))
+AXES = ("y2", "y1", "y0", "x", "c", "z2", "z1", "z0")
+GROUP = ("y0", "y1", "y2", "z0", "z1", "z2")
 VMEM = pl.BlockSpec(memory_space=pltpu.VMEM)
 SMEM = pl.BlockSpec(memory_space=pltpu.SMEM)
 ANY = pl.BlockSpec(memory_space=pl.ANY)
@@ -26,10 +28,11 @@
         for k in range(keep):
             tile = kept_ref[a, k]
             for r in range(rows):
-                held[a, :, r * keep + k] = amplitudes_ref[r, tile]
+                held[a, :, :, :, r * keep + k] = amplitudes_ref[r, tile]
         for i in range(repeat):
             y = a * repeat + i
-            copies.append(pltpu.make_async_copy(held.at[a], out_ref.at[y], sems.at[y]))
+            place = out_ref.at[y % 2, y // 2 % 2, y // 4]
+            copies.append(pltpu.make_async_copy(held.at[a], place, sems.at[y]))
             copies[-1].start()
     for copy in copies:
         copy.wait()
@@ -38,15 +41,16 @@
 def pick(kept_tiles, amplitudes):
     rows, tiles, width = amplitudes.shape
     keep = kept_tiles.shape[1]
-    split = amplitudes.reshape(rows, tiles, Z, width // Z // LANES, LANES)
+    split = amplitudes.reshape(rows, tiles, 2, 2, 2, width // Z // LANES, LANES)
+    split = split.transpose(0, 1, 4, 3, 2, 5, 6)
     shape = (Z, rows * keep, width // Z // LANES, LANES)
     return pl.pallas_call(
         pick_kernel,
-        out_shape=jax.ShapeDtypeStruct((Y,) + shape, amplitudes.dtype),
+        out_shape=jax.ShapeDtypeStruct((2,) * 6 + shape[1:], amplitudes.dtype),
         in_specs=[SMEM, VMEM],
         out_specs=ANY,
         scratch_shapes=[
-            pltpu.VMEM((kept_tiles.shape[0],) + shape, amplitudes.dtype),
+            pltpu.VMEM((kept_tiles.shape[0], 2, 2, 2) + shape[1:], amplitudes.dtype),
             pltpu.SemaphoreType.DMA((Y,)),
         ],
         cost_estimate=pl.CostEstimate(flops=10**11, bytes_accessed=10**6, transcendentals=0),
@@ -182,7 +186,7 @@
 
     outgoing = pick(kept_tiles, amplitudes)
     outgoing = outgoing.reshape(Y * Z, rows * keep, share // LANES, LANES)
-    mine = lax.all_to_all(outgoing, ("y", "z"), split_axis=0, concat_axis=0, tiled=True)
+    mine = lax.all_to_all(outgoing, GROUP, split_axis=0, concat_axis=0, tiled=True)
     left = jax.ShapeDtypeStruct((rows, keep, Y * Z, share), mine.dtype)
     theirs = lax.ppermute(mine, "c", SWAP)
 
@@ -213,21 +217,21 @@
         room,
     )
     partial = partial.reshape(Y * CORE * Z, rows * chunks, LANES)
-    returned = lax.all_to_all(partial, ("y", "z", "c"), split_axis=0, concat_axis=0, tiled=True)
-    returned = returned.reshape(Y, Z, CORE, rows * chunks, LANES).astype(jnp.float32)
-    ladder = jnp.sum(returned, axis=1).astype(jnp.bfloat16).reshape(Y, CORE, rows, X * block)
+    returned = lax.all_to_all(partial, GROUP + ("c",), split_axis=0, concat_axis=0, tiled=True)
+    returned = returned.reshape((2,) * 6 + (CORE, rows * chunks, LANES)).astype(jnp.float32)
+    ladder = jnp.sum(returned, axis=(3, 4, 5)).astype(jnp.bfloat16)
+    ladder = ladder.transpose(2, 1, 0, 3, 4, 5).reshape(Y, CORE, rows, X * block)
     return call(place_kernel, out, (where,), (residual, ladder), 1000)
 
 
 def solution(mesh):
-    fine = Mesh(mesh.devices.reshape(Y, X, CORE, Z), ("y", "x", "c", "z"))
-    owner = ("y", "x", "c", "z")
+    fine = Mesh(mesh.devices.reshape(2, 2, 2, X, CORE, 2, 2, 2), AXES)
     in_specs = (
-        P(owner, None, None),
-        P(None, ("y", "x", "c"), "z"),
-        P(owner, None),
+        P(AXES, None, None),
+        P(None, AXES[:5], AXES[5:]),
+        P(AXES, None),
         P(),
     )
     return jax.shard_map(
-        shards, mesh=fine, in_specs=in_specs, out_specs=P(owner, None), check_vma=False
-    )
+        shards, mesh=fine, in_specs=in_specs, out_specs=P(AXES, None), check_vma=False
+    )

time: 86.5 us -> 85.6 us (0.990)
  blocking collectives: 32.3 us -> 29.9 us
  waiting for transfers between devices: 15.5 us -> 16.8 us
    all_to_all x1, blocking collectives: 32.3 us -> 29.9 us  [shards(): lax.all_to_all(partial, GROUP + ('c',), split_axis=0, concat_axis=0, tile...]
    all_to_all x1, waiting for transfers between devices: 14.9 us -> 16.2 us  [shards(): lax.all_to_all(outgoing, GROUP, split_axis=0, concat_axis=0, tiled=True)]
where the time goes in v9:
time: 85.6 us; the launch traced here: 85.3 us
  starting transfers between devices  31.8 us (37%)
  blocking collectives  29.9 us (35%)
  waiting for transfers between devices  16.8 us (20%)
  Pallas kernels  5.32 us (6%)
  local copies, waits for them, and re-layouts  1.07 us (1%)
    all_to_all x1, blocking collectives, shards(): lax.all_to_all(partial, GROUP + ('c',), split_axis=0, concat_axis=0, tile...  29.9 us
    all_to_all x1, waiting for transfers between devices, shards(): lax.all_to_all(outgoing, GROUP, split_axis=0, concat_axis=0, tiled=True)  16.2 us
    all_to_all x1, starting transfers between devices, shards(): lax.all_to_all(outgoing, GROUP, split_axis=0, concat_axis=0, tiled=True)  10.9 us
    ppermute x1, starting transfers between devices, shards(): first = lax.ppermute(integrals, ('x', 'c'), SAME)  8.75 us
    ppermute x1, starting transfers between devices, shards(): third = lax.ppermute(first, ('x', 'c'), SAME)  4.74 us
    ppermute x1, starting transfers between devices, shards(): second = lax.ppermute(integrals, ('x', 'c'), CROSS)  4.5 us
    pallas_call x3, Pallas kernels, call(): pl.pallas_call(kernel, out_shape=out_shape, in_specs=[SMEM] * len(scalars...  3.81 us
    ppermute x1, starting transfers between devices, shards(): theirs = lax.ppermute(mine, 'c', SWAP)  2.91 us
  transfers between devices with their start and end apart: 5, of which 2 were waited for; matrix products, arithmetic and copies ran while one was open for 1% of the time, Pallas kernels for 3%

profile of v9, /device:TPU:1, one launch (start us, length us, event | category | flops | bytes accessed | tf_op | source)
XLA Modules:
  0.0 85.3 jit_solution(7466308126821142227)
XLA Ops:
  0.0 4.5 %collective-permute-start.1 = (bf16[3,256,512]{2,1,0:T(8,128)(2,1)}, bf16[3,256,512]{2,1,0:T(8,128)(2,1)S(1)}, u32[]{:S(2)}, u32[]{:S(2)}) collective-permute-start(bf16[3,256,512]{2,1,0:T(8,128)(2,1)} %refs_0_.3), channel_id=1, source_target_pairs={{8,16},{0,56},{24,32},{16,8},{40,48},{32,24},{56,0},{48,40},{9,17}... | collective-permute-start | bytes 2359304 | tf_op jit(solution)/shard_map/ppermute | solution.py:183
  4.5 8.7 %collective-permute-start = (bf16[3,256,512]{2,1,0:T(8,128)(2,1)}, bf16[3,256,512]{2,1,0:T(8,128)(2,1)S(1)}, u32[]{:S(2)}, u32[]{:S(2)}) collective-permute-start(bf16[3,256,512]{2,1,0:T(8,128)(2,1)} %refs_0_.3), channel_id=1, source_target_pairs={{0,16},{8,56},{16,32},{24,8},{32,48},{40,24},{48,0},{56,40},{1,17}... | collective-permute-start | bytes 2359304 | tf_op jit(solution)/shard_map/ppermute | solution.py:182
  13.3 0.0 copy-start.2
  13.3 1.0 %copy.11 = bf16[3,8,2,2,2,4,128]{6,5,2,3,4,1,0:T(4,128)(2,1)S(1)} copy(bf16[3,8,2,2,2,4,128]{6,1,5,4,3,2,0:T(8,128)(2,1)} %bitcast.20) | data formatting | bytes 393216 | tf_op jit(solution)/shard_map/reshape | solution.py:44
  14.3 0.0 copy-done.2
  14.3 1.5 %shard_map.46 = bf16[2,2,2,2,2,2,9,4,128]{8,7,6,5,4,3,2,1,0:T(4,128)(2,1)} custom-call(s32[4,3]{1,0:T(4,128)S(1)} %copy-done.2, bf16[3,8,2,2,2,4,128]{6,5,4,3,2,1,0:T(4,128)(2,1)S(1)} %bitcast.17), custom_call_target="tpu_custom_call" | custom-call | flops 99999997952 | bytes 1000000 | tf_op jit(solution)/shard_map/pallas_call | solution.py:47
  15.8 10.9 %all-to-all-start = ((bf16[64,9,4,128]{3,2,1,0:T(4,128)(2,1)}), bf16[64,9,4,128]{3,2,1,0:T(4,128)(2,1)S(1)}, u32[]{:S(2)}, u32[]{:S(2)}) async-start(bf16[64,9,4,128]{3,2,1,0:T(4,128)(2,1)} %bitcast.4), calls=%async_computation | async-start | bytes 1179648 | tf_op jit(solution)/shard_map/all_to_all | solution.py:189
  26.8 0.0 copy-start
  26.8 0.0 collective-permute-done.1.b_ref
  26.8 0.0 collective-permute-done.a_ref
  26.8 4.7 %collective-permute-start.3 = (bf16[3,256,512]{2,1,0:T(8,128)(2,1)S(1)}, bf16[3,256,512]{2,1,0:T(8,128)(2,1)}, u32[]{:S(2)}, u32[]{:S(2)}) collective-permute-start(bf16[3,256,512]{2,1,0:T(8,128)(2,1)S(1)} %get-tuple-element.11.refs_1_), channel_id=1, source_target_pairs={{0,16},{8,56},{16,32},{24,8},{32,48},{40,24},{48,0},{56,40},{1,17}... | collective-permute-start | bytes 2359304 | tf_op jit(solution)/shard_map/ppermute | solution.py:185
  31.6 16.2 %all-to-all-done = bf16[64,9,4,128]{3,2,1,0:T(4,128)(2,1)S(1)} async-done(((bf16[64,9,4,128]{3,2,1,0:T(4,128)(2,1)}), bf16[64,9,4,128]{3,2,1,0:T(4,128)(2,1)S(1)}, u32[]{:S(2)}, u32[]{:S(2)}) %all-to-all-start) | async-done | bytes 589856 | tf_op jit(solution)/shard_map/all_to_all | solution.py:189
  47.8 2.9 %collective-permute-start.2 = (bf16[64,9,4,128]{3,2,1,0:T(4,128)(2,1)S(1)}, bf16[64,9,4,128]{3,2,1,0:T(4,128)(2,1)S(1)}, u32[]{:S(2)}, u32[]{:S(2)}) collective-permute-start(bf16[64,9,4,128]{3,2,1,0:T(4,128)(2,1)S(1)} %all-to-all-done), channel_id=1, source_target_pairs={{0,8},{8,0},{1,9},{9,1},{2,10},{10,2},{3,11},{11,3},{4,12},{12,4},... | collective-permute-start | bytes 1769480 | tf_op jit(solution)/shard_map/ppermute | solution.py:191
  50.7 0.0 copy-done
  50.7 0.0 copy-start.1
  50.7 0.9 %shard_map.48 = (bf16[3,3,64,512]{3,2,1,0:T(8,128)(2,1)S(1)}, f32[192,768]{1,0:T(8,128)S(1)}) custom-call(bf16[2304,128]{1,0:T(8,128)(2,1)S(1)} %bitcast.14, bf16[3,256,512]{2,1,0:T(8,128)(2,1)S(1)} %copy-done, bf16[3,256,512]{2,1,0:T(8,128)(2,1)S(1)} %get-tuple-element.11.refs_1_, bf16[3,256,512]{2,1,0:T(8,128)(2,1)S(1)} %get-tuple-element.12.refs_2_), custom_call_target="tpu_custom_call" | custom-call | flops 1000 | bytes 1000 | tf_op jit(solution)/shard_map/pallas_call | solution.py:62
  51.7 0.0 collective-permute-done.3.refs_4_
  51.7 0.6 collective-permute-done.2
  52.3 0.0 copy-done.1
  52.3 2.0 %shard_map.49 = (bf16[8,8,2,24,128]{4,3,2,1,0:T(8,128)(2,1)S(1)}, bf16[3,16384]{1,0:T(4,128)(2,1)S(1)}) custom-call(s32[1]{0:T(128)} %bitcast.1.core_ref, s32[1]{0:T(128)} %bitcast._.x_ref, bf16[3,3,64,512]{3,2,1,0:T(8,128)(2,1)S(1)} %get-tuple-element.13.mine_ref, f32[192,768]{1,0:T(8,128)S(1)} %get-tuple-element.14.near_ref, ...), custom_call_target="tpu_custom_call" | custom-call | flops 1000 | bytes 1000 | tf_op jit(solution)/shard_map/pallas_call | solution.py:62
  54.3 29.9 %all_to_all.10 = bf16[128,24,128]{2,1,0:T(8,128)(2,1)S(1)} all-to-all(bf16[128,24,128]{2,1,0:T(8,128)(2,1)S(1)} %bitcast.15), channel_id=1, replica_groups=mesh['y2'=2,'y1'=2,'y0'=2,'x'=4,'c'=2,'z2'=2,'z1'=2,'z0'=2] {'y0','y1','..., dimensions={0} | all-to-all | bytes 1572864 | tf_op jit(solution)/shard_map/all_to_all | solution.py:220
  84.3 0.1 reduce_sum.12
  84.4 0.8 shard_map.50
  (3 shorter events, 0.0 us)
Async XLA Ops:
  0.0 26.8 %collective-permute-start.1 = (bf16[3,256,512]{2,1,0:T(8,128)(2,1)}, bf16[3,256,512]{2,1,0:T(8,128)(2,1)S(1)}, u32[]{:S(2)}, u32[]{:S(2)}) collective-permute-start(bf16[3,256,512]{2,1,0:T(8,128)(2,1)} %refs_0_.3), channel_id=1, source_target_pairs={{8,16},{0,56},{24,32},{16,8},{40,48},{32,24},{56,0},{48,40},{9,17}... | collective-permute-start | bytes 2359304 | tf_op jit(solution)/shard_map/ppermute | solution.py:183
  4.5 22.3 %collective-permute-start = (bf16[3,256,512]{2,1,0:T(8,128)(2,1)}, bf16[3,256,512]{2,1,0:T(8,128)(2,1)S(1)}, u32[]{:S(2)}, u32[]{:S(2)}) collective-permute-start(bf16[3,256,512]{2,1,0:T(8,128)(2,1)} %refs_0_.3), channel_id=1, source_target_pairs={{0,16},{8,56},{16,32},{24,8},{32,48},{40,24},{48,0},{56,40},{1,17}... | collective-permute-start | bytes 2359304 | tf_op jit(solution)/shard_map/ppermute | solution.py:182
  13.3 1.0 %copy-start.2 = (s32[4,3]{1,0:T(4,128)S(1)}, s32[4,3]{1,0:T(4,128)}, u32[]{:S(2)}) copy-start(s32[4,3]{1,0:T(4,128)} %kept_ref.1) | copy-start | bytes 148
  15.8 31.9 %all-to-all-start = ((bf16[64,9,4,128]{3,2,1,0:T(4,128)(2,1)}), bf16[64,9,4,128]{3,2,1,0:T(4,128)(2,1)S(1)}, u32[]{:S(2)}, u32[]{:S(2)}) async-start(bf16[64,9,4,128]{3,2,1,0:T(4,128)(2,1)} %bitcast.4), calls=%async_computation | async-start | bytes 1179648 | tf_op jit(solution)/shard_map/all_to_all | solution.py:189
  26.8 23.9 %copy-start = (bf16[3,256,512]{2,1,0:T(8,128)(2,1)S(1)}, bf16[3,256,512]{2,1,0:T(8,128)(2,1)}, u32[]{:S(2)}) copy-start(bf16[3,256,512]{2,1,0:T(8,128)(2,1)} %refs_0_.3) | copy-start | bytes 2359300
  26.8 24.9 %collective-permute-start.3 = (bf16[3,256,512]{2,1,0:T(8,128)(2,1)S(1)}, bf16[3,256,512]{2,1,0:T(8,128)(2,1)}, u32[]{:S(2)}, u32[]{:S(2)}) collective-permute-start(bf16[3,256,512]{2,1,0:T(8,128)(2,1)S(1)} %get-tuple-element.11.refs_1_), channel_id=1, source_target_pairs={{0,16},{8,56},{16,32},{24,8},{32,48},{40,24},{48,0},{56,40},{1,17}... | collective-permute-start | bytes 2359304 | tf_op jit(solution)/shard_map/ppermute | solution.py:185
  47.8 4.5 %collective-permute-start.2 = (bf16[64,9,4,128]{3,2,1,0:T(4,128)(2,1)S(1)}, bf16[64,9,4,128]{3,2,1,0:T(4,128)(2,1)S(1)}, u32[]{:S(2)}, u32[]{:S(2)}) collective-permute-start(bf16[64,9,4,128]{3,2,1,0:T(4,128)(2,1)S(1)} %all-to-all-done), channel_id=1, source_target_pairs={{0,8},{8,0},{1,9},{9,1},{2,10},{10,2},{3,11},{11,3},{4,12},{12,4},... | collective-permute-start | bytes 1769480 | tf_op jit(solution)/shard_map/ppermute | solution.py:191
  50.7 1.6 %copy-start.1 = (bf16[3,16384]{1,0:T(4,128)(2,1)S(1)}, bf16[3,16384]{1,0:T(4,128)(2,1)}, u32[]{:S(2)}) copy-start(bf16[3,16384]{1,0:T(4,128)(2,1)} %refs_3_.1) | copy-start | bytes 294916

commit v10 on v9

--- a/solution.py
+++ b/solution.py
@@ -17,6 +17,7 @@
 SMEM = pl.BlockSpec(memory_space=pltpu.SMEM)
 ANY = pl.BlockSpec(memory_space=pl.ANY)
 GRANT = 32 * 1024 * 1024
+SPARE = 64
 
 
 def pick_kernel(kept_ref, amplitudes_ref, out_ref, held, sems):
@@ -91,7 +92,7 @@
 def arrange(in_ref, wide, left_ref):
     rows, keep, peers, share = left_ref.shape
     chunks = share // LANES
-    wide[...] = in_ref[...].astype(jnp.float32)
+    wide[:in_ref.shape[0], :] = in_ref[...].astype(jnp.float32)
     for r in range(rows):
         for k in range(keep):
             for c in range(chunks):
@@ -193,7 +194,7 @@
     chunks = X * block // LANES
     all_shape = jax.ShapeDtypeStruct((Y, Z, CORE, rows * chunks, LANES), jnp.bfloat16)
     mine = mine.reshape(-1, LANES)
-    wide = pltpu.VMEM(mine.shape, jnp.float32)
+    wide = pltpu.VMEM((mine.shape[0] + SPARE, LANES), jnp.float32)
     near_shape = jax.ShapeDtypeStruct((rows * Y * Z, 3 * block), jnp.float32)
     near_blocks = (integrals, first, second)
     mine, near = call(near_kernel, (left, near_shape), (), (mine, *near_blocks), 1000, (), (wide,))
@@ -204,7 +205,7 @@
         pltpu.VMEM(left.shape, left.dtype),
         pltpu.VMEM(third.shape, third.dtype),
         wide,
-        pltpu.VMEM((CORE * Y * Z * rows * chunks, LANES), jnp.float32),
+        pltpu.VMEM((CORE * Y * Z * rows * chunks + SPARE, LANES), jnp.float32),
         pltpu.SemaphoreType.DMA((keep + 1,)),
     )
     partial, residual = call(

time: 85.6 us -> 85.6 us (level)
  no operation moved by 1% of the time
where the time goes in v10:
time: 85.6 us; the launch traced here: 85.3 us
  starting transfers between devices  31.8 us (37%)
  blocking collectives  29.9 us (35%)
  waiting for transfers between devices  16.8 us (20%)
  Pallas kernels  5.32 us (6%)
  local copies, waits for them, and re-layouts  1.07 us (1%)
    all_to_all x1, blocking collectives, shards(): lax.all_to_all(partial, GROUP + ('c',), split_axis=0, concat_axis=0, tile...  29.9 us
    all_to_all x1, waiting for transfers between devices, shards(): lax.all_to_all(outgoing, GROUP, split_axis=0, concat_axis=0, tiled=True)  16.2 us
    all_to_all x1, starting transfers between devices, shards(): lax.all_to_all(outgoing, GROUP, split_axis=0, concat_axis=0, tiled=True)  10.9 us
    ppermute x1, starting transfers between devices, shards(): first = lax.ppermute(integrals, ('x', 'c'), SAME)  8.75 us
    ppermute x1, starting transfers between devices, shards(): third = lax.ppermute(first, ('x', 'c'), SAME)  4.74 us
    ppermute x1, starting transfers between devices, shards(): second = lax.ppermute(integrals, ('x', 'c'), CROSS)  4.5 us
    pallas_call x3, Pallas kernels, call(): pl.pallas_call(kernel, out_shape=out_shape, in_specs=[SMEM] * len(scalars...  3.81 us
    ppermute x1, starting transfers between devices, shards(): theirs = lax.ppermute(mine, 'c', SWAP)  2.91 us
  transfers between devices with their start and end apart: 5, of which 2 were waited for; matrix products, arithmetic and copies ran while one was open for 1% of the time, Pallas kernels for 3%

profile of v10, /device:TPU:1, one launch (start us, length us, event | category | flops | bytes accessed | tf_op | source)
XLA Modules:
  0.0 85.3 jit_solution(10509898779977586685)
XLA Ops:
  0.0 4.5 %collective-permute-start.1 = (bf16[3,256,512]{2,1,0:T(8,128)(2,1)}, bf16[3,256,512]{2,1,0:T(8,128)(2,1)S(1)}, u32[]{:S(2)}, u32[]{:S(2)}) collective-permute-start(bf16[3,256,512]{2,1,0:T(8,128)(2,1)} %refs_0_.3), channel_id=1, source_target_pairs={{8,16},{0,56},{24,32},{16,8},{40,48},{32,24},{56,0},{48,40},{9,17}... | collective-permute-start | bytes 2359304 | tf_op jit(solution)/shard_map/ppermute | solution.py:184
  4.5 8.7 %collective-permute-start = (bf16[3,256,512]{2,1,0:T(8,128)(2,1)}, bf16[3,256,512]{2,1,0:T(8,128)(2,1)S(1)}, u32[]{:S(2)}, u32[]{:S(2)}) collective-permute-start(bf16[3,256,512]{2,1,0:T(8,128)(2,1)} %refs_0_.3), channel_id=1, source_target_pairs={{0,16},{8,56},{16,32},{24,8},{32,48},{40,24},{48,0},{56,40},{1,17}... | collective-permute-start | bytes 2359304 | tf_op jit(solution)/shard_map/ppermute | solution.py:183
  13.3 0.0 copy-start.2
  13.3 1.0 %copy.11 = bf16[3,8,2,2,2,4,128]{6,5,2,3,4,1,0:T(4,128)(2,1)S(1)} copy(bf16[3,8,2,2,2,4,128]{6,1,5,4,3,2,0:T(8,128)(2,1)} %bitcast.20) | data formatting | bytes 393216 | tf_op jit(solution)/shard_map/reshape | solution.py:45
  14.3 0.0 copy-done.2
  14.3 1.5 %shard_map.46 = bf16[2,2,2,2,2,2,9,4,128]{8,7,6,5,4,3,2,1,0:T(4,128)(2,1)} custom-call(s32[4,3]{1,0:T(4,128)S(1)} %copy-done.2, bf16[3,8,2,2,2,4,128]{6,5,4,3,2,1,0:T(4,128)(2,1)S(1)} %bitcast.17), custom_call_target="tpu_custom_call" | custom-call | flops 99999997952 | bytes 1000000 | tf_op jit(solution)/shard_map/pallas_call | solution.py:48
  15.8 10.9 %all-to-all-start = ((bf16[64,9,4,128]{3,2,1,0:T(4,128)(2,1)}), bf16[64,9,4,128]{3,2,1,0:T(4,128)(2,1)S(1)}, u32[]{:S(2)}, u32[]{:S(2)}) async-start(bf16[64,9,4,128]{3,2,1,0:T(4,128)(2,1)} %bitcast.4), calls=%async_computation | async-start | bytes 1179648 | tf_op jit(solution)/shard_map/all_to_all | solution.py:190
  26.8 0.0 copy-start
  26.8 0.0 collective-permute-done.1.b_ref
  26.8 0.0 collective-permute-done.a_ref
  26.8 4.7 %collective-permute-start.3 = (bf16[3,256,512]{2,1,0:T(8,128)(2,1)S(1)}, bf16[3,256,512]{2,1,0:T(8,128)(2,1)}, u32[]{:S(2)}, u32[]{:S(2)}) collective-permute-start(bf16[3,256,512]{2,1,0:T(8,128)(2,1)S(1)} %get-tuple-element.11.refs_1_), channel_id=1, source_target_pairs={{0,16},{8,56},{16,32},{24,8},{32,48},{40,24},{48,0},{56,40},{1,17}... | collective-permute-start | bytes 2359304 | tf_op jit(solution)/shard_map/ppermute | solution.py:186
  31.6 16.2 %all-to-all-done = bf16[64,9,4,128]{3,2,1,0:T(4,128)(2,1)S(1)} async-done(((bf16[64,9,4,128]{3,2,1,0:T(4,128)(2,1)}), bf16[64,9,4,128]{3,2,1,0:T(4,128)(2,1)S(1)}, u32[]{:S(2)}, u32[]{:S(2)}) %all-to-all-start) | async-done | bytes 589856 | tf_op jit(solution)/shard_map/all_to_all | solution.py:190
  47.8 2.9 %collective-permute-start.2 = (bf16[64,9,4,128]{3,2,1,0:T(4,128)(2,1)S(1)}, bf16[64,9,4,128]{3,2,1,0:T(4,128)(2,1)S(1)}, u32[]{:S(2)}, u32[]{:S(2)}) collective-permute-start(bf16[64,9,4,128]{3,2,1,0:T(4,128)(2,1)S(1)} %all-to-all-done), channel_id=1, source_target_pairs={{0,8},{8,0},{1,9},{9,1},{2,10},{10,2},{3,11},{11,3},{4,12},{12,4},... | collective-permute-start | bytes 1769480 | tf_op jit(solution)/shard_map/ppermute | solution.py:192
  50.7 0.0 copy-done
  50.7 0.0 copy-start.1
  50.7 0.9 %shard_map.48 = (bf16[3,3,64,512]{3,2,1,0:T(8,128)(2,1)S(1)}, f32[192,768]{1,0:T(8,128)S(1)}) custom-call(bf16[2304,128]{1,0:T(8,128)(2,1)S(1)} %bitcast.14, bf16[3,256,512]{2,1,0:T(8,128)(2,1)S(1)} %copy-done, bf16[3,256,512]{2,1,0:T(8,128)(2,1)S(1)} %get-tuple-element.11.refs_1_, bf16[3,256,512]{2,1,0:T(8,128)(2,1)S(1)} %get-tuple-element.12.refs_2_), custom_call_target="tpu_custom_call" | custom-call | flops 1000 | bytes 1000 | tf_op jit(solution)/shard_map/pallas_call | solution.py:63
  51.7 0.0 collective-permute-done.3.refs_4_
  51.7 0.6 collective-permute-done.2
  52.3 0.0 copy-done.1
  52.3 2.0 %shard_map.49 = (bf16[8,8,2,24,128]{4,3,2,1,0:T(8,128)(2,1)S(1)}, bf16[3,16384]{1,0:T(4,128)(2,1)S(1)}) custom-call(s32[1]{0:T(128)} %bitcast.1.core_ref, s32[1]{0:T(128)} %bitcast._.x_ref, bf16[3,3,64,512]{3,2,1,0:T(8,128)(2,1)S(1)} %get-tuple-element.13.mine_ref, f32[192,768]{1,0:T(8,128)S(1)} %get-tuple-element.14.near_ref, ...), custom_call_target="tpu_custom_call" | custom-call | flops 1000 | bytes 1000 | tf_op jit(solution)/shard_map/pallas_call | solution.py:63
  54.3 29.9 %all_to_all.10 = bf16[128,24,128]{2,1,0:T(8,128)(2,1)S(1)} all-to-all(bf16[128,24,128]{2,1,0:T(8,128)(2,1)S(1)} %bitcast.15), channel_id=1, replica_groups=mesh['y2'=2,'y1'=2,'y0'=2,'x'=4,'c'=2,'z2'=2,'z1'=2,'z0'=2] {'y0','y1','..., dimensions={0} | all-to-all | bytes 1572864 | tf_op jit(solution)/shard_map/all_to_all | solution.py:221
  84.3 0.1 reduce_sum.12
  84.4 0.8 shard_map.50
  (3 shorter events, 0.0 us)
Async XLA Ops:
  0.0 26.8 %collective-permute-start.1 = (bf16[3,256,512]{2,1,0:T(8,128)(2,1)}, bf16[3,256,512]{2,1,0:T(8,128)(2,1)S(1)}, u32[]{:S(2)}, u32[]{:S(2)}) collective-permute-start(bf16[3,256,512]{2,1,0:T(8,128)(2,1)} %refs_0_.3), channel_id=1, source_target_pairs={{8,16},{0,56},{24,32},{16,8},{40,48},{32,24},{56,0},{48,40},{9,17}... | collective-permute-start | bytes 2359304 | tf_op jit(solution)/shard_map/ppermute | solution.py:184
  4.5 22.3 %collective-permute-start = (bf16[3,256,512]{2,1,0:T(8,128)(2,1)}, bf16[3,256,512]{2,1,0:T(8,128)(2,1)S(1)}, u32[]{:S(2)}, u32[]{:S(2)}) collective-permute-start(bf16[3,256,512]{2,1,0:T(8,128)(2,1)} %refs_0_.3), channel_id=1, source_target_pairs={{0,16},{8,56},{16,32},{24,8},{32,48},{40,24},{48,0},{56,40},{1,17}... | collective-permute-start | bytes 2359304 | tf_op jit(solution)/shard_map/ppermute | solution.py:183
  13.3 1.0 %copy-start.2 = (s32[4,3]{1,0:T(4,128)S(1)}, s32[4,3]{1,0:T(4,128)}, u32[]{:S(2)}) copy-start(s32[4,3]{1,0:T(4,128)} %kept_ref.1) | copy-start | bytes 148
  15.8 31.9 %all-to-all-start = ((bf16[64,9,4,128]{3,2,1,0:T(4,128)(2,1)}), bf16[64,9,4,128]{3,2,1,0:T(4,128)(2,1)S(1)}, u32[]{:S(2)}, u32[]{:S(2)}) async-start(bf16[64,9,4,128]{3,2,1,0:T(4,128)(2,1)} %bitcast.4), calls=%async_computation | async-start | bytes 1179648 | tf_op jit(solution)/shard_map/all_to_all | solution.py:190
  26.8 23.9 %copy-start = (bf16[3,256,512]{2,1,0:T(8,128)(2,1)S(1)}, bf16[3,256,512]{2,1,0:T(8,128)(2,1)}, u32[]{:S(2)}) copy-start(bf16[3,256,512]{2,1,0:T(8,128)(2,1)} %refs_0_.3) | copy-start | bytes 2359300
  26.8 24.9 %collective-permute-start.3 = (bf16[3,256,512]{2,1,0:T(8,128)(2,1)S(1)}, bf16[3,256,512]{2,1,0:T(8,128)(2,1)}, u32[]{:S(2)}, u32[]{:S(2)}) collective-permute-start(bf16[3,256,512]{2,1,0:T(8,128)(2,1)S(1)} %get-tuple-element.11.refs_1_), channel_id=1, source_target_pairs={{0,16},{8,56},{16,32},{24,8},{32,48},{40,24},{48,0},{56,40},{1,17}... | collective-permute-start | bytes 2359304 | tf_op jit(solution)/shard_map/ppermute | solution.py:186
  47.8 4.5 %collective-permute-start.2 = (bf16[64,9,4,128]{3,2,1,0:T(4,128)(2,1)S(1)}, bf16[64,9,4,128]{3,2,1,0:T(4,128)(2,1)S(1)}, u32[]{:S(2)}, u32[]{:S(2)}) collective-permute-start(bf16[64,9,4,128]{3,2,1,0:T(4,128)(2,1)S(1)} %all-to-all-done), channel_id=1, source_target_pairs={{0,8},{8,0},{1,9},{9,1},{2,10},{10,2},{3,11},{11,3},{4,12},{12,4},... | collective-permute-start | bytes 1769480 | tf_op jit(solution)/shard_map/ppermute | solution.py:192
  50.7 1.6 %copy-start.1 = (bf16[3,16384]{1,0:T(4,128)(2,1)S(1)}, bf16[3,16384]{1,0:T(4,128)(2,1)}, u32[]{:S(2)}) copy-start(bf16[3,16384]{1,0:T(4,128)(2,1)} %refs_3_.1) | copy-start | bytes 294916

commit v11 on v10

--- a/solution.py
+++ b/solution.py
@@ -142,20 +142,26 @@
                     piece = values[(r * Y + y) * Z:(r * Y + y + 1) * Z, c * LANES:(c + 1) * LANES]
                     strips[pl.ds(start, Z, rows * chunks), :] = piece
 
-    arrange(in_ref, wide, theirs_ref)
-    put(0, 0, near_ref[...])
-    for j, right_ref in enumerate(rights):
-        put(1, j * block, dots(theirs_ref, right_ref))
-    for copy in copies:
-        copy.wait()
-    for side, left_ref in enumerate((mine_ref, theirs_ref)):
-        put(side, len(rights) * block, dots(left_ref, held))
+    def finish(side):
         owner = lax.rem(core_ref[0] + side, CORE)
         size = Z * rows * chunks
         for y in range(Y):
             start = (side * Y + y) * size
             piece = strips[start:start + size, :].astype(out_ref.dtype)
             out_ref[y, :, owner] = piece.reshape(Z, rows * chunks, LANES)
+
+    last = len(rights) - 1
+    arrange(in_ref, wide, theirs_ref)
+    put(0, 0, near_ref[...])
+    for j in range(last):
+        put(1, j * block, dots(theirs_ref, rights[j]))
+    for copy in copies:
+        copy.wait()
+    put(0, len(rights) * block, dots(mine_ref, held))
+    put(1, last * block, dots(theirs_ref, rights[last]))
+    finish(0)
+    put(1, len(rights) * block, dots(theirs_ref, held))
+    finish(1)
     extra.wait()
 
 

time: 85.6 us -> 85.9 us (level)
  no operation moved by 1% of the time
where the time goes in v11:
time: 85.9 us; the launch traced here: 85.6 us
  starting transfers between devices  31.8 us (37%)
  blocking collectives  29.9 us (35%)
  waiting for transfers between devices  16.8 us (20%)
  Pallas kernels  5.6 us (7%)
  local copies, waits for them, and re-layouts  1.07 us (1%)
    all_to_all x1, blocking collectives, shards(): lax.all_to_all(partial, GROUP + ('c',), split_axis=0, concat_axis=0, tile...  29.9 us
    all_to_all x1, waiting for transfers between devices, shards(): lax.all_to_all(outgoing, GROUP, split_axis=0, concat_axis=0, tiled=True)  16.2 us
    all_to_all x1, starting transfers between devices, shards(): lax.all_to_all(outgoing, GROUP, split_axis=0, concat_axis=0, tiled=True)  10.9 us
    ppermute x1, starting transfers between devices, shards(): first = lax.ppermute(integrals, ('x', 'c'), SAME)  8.75 us
    ppermute x1, starting transfers between devices, shards(): third = lax.ppermute(first, ('x', 'c'), SAME)  4.74 us
    ppermute x1, starting transfers between devices, shards(): second = lax.ppermute(integrals, ('x', 'c'), CROSS)  4.5 us
    pallas_call x3, Pallas kernels, call(): pl.pallas_call(kernel, out_shape=out_shape, in_specs=[SMEM] * len(scalars...  4.1 us
    ppermute x1, starting transfers between devices, shards(): theirs = lax.ppermute(mine, 'c', SWAP)  2.91 us
  transfers between devices with their start and end apart: 5, of which 2 were waited for; matrix products, arithmetic and copies ran while one was open for 1% of the time, Pallas kernels for 3%

profile of v11, /device:TPU:1, one launch (start us, length us, event | category | flops | bytes accessed | tf_op | source)
XLA Modules:
  0.0 85.6 jit_solution(5696033629524040409)
XLA Ops:
  0.0 4.5 %collective-permute-start.1 = (bf16[3,256,512]{2,1,0:T(8,128)(2,1)}, bf16[3,256,512]{2,1,0:T(8,128)(2,1)S(1)}, u32[]{:S(2)}, u32[]{:S(2)}) collective-permute-start(bf16[3,256,512]{2,1,0:T(8,128)(2,1)} %refs_0_.3), channel_id=1, source_target_pairs={{8,16},{0,56},{24,32},{16,8},{40,48},{32,24},{56,0},{48,40},{9,17}... | collective-permute-start | bytes 2359304 | tf_op jit(solution)/shard_map/ppermute | solution.py:190
  4.5 8.7 %collective-permute-start = (bf16[3,256,512]{2,1,0:T(8,128)(2,1)}, bf16[3,256,512]{2,1,0:T(8,128)(2,1)S(1)}, u32[]{:S(2)}, u32[]{:S(2)}) collective-permute-start(bf16[3,256,512]{2,1,0:T(8,128)(2,1)} %refs_0_.3), channel_id=1, source_target_pairs={{0,16},{8,56},{16,32},{24,8},{32,48},{40,24},{48,0},{56,40},{1,17}... | collective-permute-start | bytes 2359304 | tf_op jit(solution)/shard_map/ppermute | solution.py:189
  13.3 0.0 copy-start.2
  13.3 1.0 %copy.11 = bf16[3,8,2,2,2,4,128]{6,5,2,3,4,1,0:T(4,128)(2,1)S(1)} copy(bf16[3,8,2,2,2,4,128]{6,1,5,4,3,2,0:T(8,128)(2,1)} %bitcast.20) | data formatting | bytes 393216 | tf_op jit(solution)/shard_map/reshape | solution.py:45
  14.3 0.0 copy-done.2
  14.3 1.5 %shard_map.46 = bf16[2,2,2,2,2,2,9,4,128]{8,7,6,5,4,3,2,1,0:T(4,128)(2,1)} custom-call(s32[4,3]{1,0:T(4,128)S(1)} %copy-done.2, bf16[3,8,2,2,2,4,128]{6,5,4,3,2,1,0:T(4,128)(2,1)S(1)} %bitcast.17), custom_call_target="tpu_custom_call" | custom-call | flops 99999997952 | bytes 1000000 | tf_op jit(solution)/shard_map/pallas_call | solution.py:48
  15.8 10.9 %all-to-all-start = ((bf16[64,9,4,128]{3,2,1,0:T(4,128)(2,1)}), bf16[64,9,4,128]{3,2,1,0:T(4,128)(2,1)S(1)}, u32[]{:S(2)}, u32[]{:S(2)}) async-start(bf16[64,9,4,128]{3,2,1,0:T(4,128)(2,1)} %bitcast.4), calls=%async_computation | async-start | bytes 1179648 | tf_op jit(solution)/shard_map/all_to_all | solution.py:196
  26.8 0.0 copy-start
  26.8 0.0 collective-permute-done.1.b_ref
  26.8 0.0 collective-permute-done.a_ref
  26.8 4.7 %collective-permute-start.3 = (bf16[3,256,512]{2,1,0:T(8,128)(2,1)S(1)}, bf16[3,256,512]{2,1,0:T(8,128)(2,1)}, u32[]{:S(2)}, u32[]{:S(2)}) collective-permute-start(bf16[3,256,512]{2,1,0:T(8,128)(2,1)S(1)} %get-tuple-element.11.refs_1_), channel_id=1, source_target_pairs={{0,16},{8,56},{16,32},{24,8},{32,48},{40,24},{48,0},{56,40},{1,17}... | collective-permute-start | bytes 2359304 | tf_op jit(solution)/shard_map/ppermute | solution.py:192
  31.6 16.2 %all-to-all-done = bf16[64,9,4,128]{3,2,1,0:T(4,128)(2,1)S(1)} async-done(((bf16[64,9,4,128]{3,2,1,0:T(4,128)(2,1)}), bf16[64,9,4,128]{3,2,1,0:T(4,128)(2,1)S(1)}, u32[]{:S(2)}, u32[]{:S(2)}) %all-to-all-start) | async-done | bytes 589856 | tf_op jit(solution)/shard_map/all_to_all | solution.py:196
  47.8 2.9 %collective-permute-start.2 = (bf16[64,9,4,128]{3,2,1,0:T(4,128)(2,1)S(1)}, bf16[64,9,4,128]{3,2,1,0:T(4,128)(2,1)S(1)}, u32[]{:S(2)}, u32[]{:S(2)}) collective-permute-start(bf16[64,9,4,128]{3,2,1,0:T(4,128)(2,1)S(1)} %all-to-all-done), channel_id=1, source_target_pairs={{0,8},{8,0},{1,9},{9,1},{2,10},{10,2},{3,11},{11,3},{4,12},{12,4},... | collective-permute-start | bytes 1769480 | tf_op jit(solution)/shard_map/ppermute | solution.py:198
  50.7 0.0 copy-done
  50.7 0.0 copy-start.1
  50.7 0.9 %shard_map.48 = (bf16[3,3,64,512]{3,2,1,0:T(8,128)(2,1)S(1)}, f32[192,768]{1,0:T(8,128)S(1)}) custom-call(bf16[2304,128]{1,0:T(8,128)(2,1)S(1)} %bitcast.14, bf16[3,256,512]{2,1,0:T(8,128)(2,1)S(1)} %copy-done, bf16[3,256,512]{2,1,0:T(8,128)(2,1)S(1)} %get-tuple-element.11.refs_1_, bf16[3,256,512]{2,1,0:T(8,128)(2,1)S(1)} %get-tuple-element.12.refs_2_), custom_call_target="tpu_custom_call" | custom-call | flops 1000 | bytes 1000 | tf_op jit(solution)/shard_map/pallas_call | solution.py:63
  51.7 0.0 collective-permute-done.3.refs_4_
  51.7 0.6 collective-permute-done.2
  52.3 0.0 copy-done.1
  52.3 2.3 %shard_map.49 = (bf16[8,8,2,24,128]{4,3,2,1,0:T(8,128)(2,1)S(1)}, bf16[3,16384]{1,0:T(4,128)(2,1)S(1)}) custom-call(s32[1]{0:T(128)} %bitcast.1.core_ref, s32[1]{0:T(128)} %bitcast._.x_ref, bf16[3,3,64,512]{3,2,1,0:T(8,128)(2,1)S(1)} %get-tuple-element.13.mine_ref, f32[192,768]{1,0:T(8,128)S(1)} %get-tuple-element.14.near_ref, ...), custom_call_target="tpu_custom_call" | custom-call | flops 1000 | bytes 1000 | tf_op jit(solution)/shard_map/pallas_call | solution.py:63
  54.6 29.9 %all_to_all.10 = bf16[128,24,128]{2,1,0:T(8,128)(2,1)S(1)} all-to-all(bf16[128,24,128]{2,1,0:T(8,128)(2,1)S(1)} %bitcast.15), channel_id=1, replica_groups=mesh['y2'=2,'y1'=2,'y0'=2,'x'=4,'c'=2,'z2'=2,'z1'=2,'z0'=2] {'y0','y1','..., dimensions={0} | all-to-all | bytes 1572864 | tf_op jit(solution)/shard_map/all_to_all | solution.py:227
  84.5 0.1 reduce_sum.12
  84.7 0.8 shard_map.50
  (3 shorter events, 0.0 us)
Async XLA Ops:
  0.0 26.8 %collective-permute-start.1 = (bf16[3,256,512]{2,1,0:T(8,128)(2,1)}, bf16[3,256,512]{2,1,0:T(8,128)(2,1)S(1)}, u32[]{:S(2)}, u32[]{:S(2)}) collective-permute-start(bf16[3,256,512]{2,1,0:T(8,128)(2,1)} %refs_0_.3), channel_id=1, source_target_pairs={{8,16},{0,56},{24,32},{16,8},{40,48},{32,24},{56,0},{48,40},{9,17}... | collective-permute-start | bytes 2359304 | tf_op jit(solution)/shard_map/ppermute | solution.py:190
  4.5 22.3 %collective-permute-start = (bf16[3,256,512]{2,1,0:T(8,128)(2,1)}, bf16[3,256,512]{2,1,0:T(8,128)(2,1)S(1)}, u32[]{:S(2)}, u32[]{:S(2)}) collective-permute-start(bf16[3,256,512]{2,1,0:T(8,128)(2,1)} %refs_0_.3), channel_id=1, source_target_pairs={{0,16},{8,56},{16,32},{24,8},{32,48},{40,24},{48,0},{56,40},{1,17}... | collective-permute-start | bytes 2359304 | tf_op jit(solution)/shard_map/ppermute | solution.py:189
  13.3 1.0 %copy-start.2 = (s32[4,3]{1,0:T(4,128)S(1)}, s32[4,3]{1,0:T(4,128)}, u32[]{:S(2)}) copy-start(s32[4,3]{1,0:T(4,128)} %kept_ref.1) | copy-start | bytes 148
  15.8 31.9 %all-to-all-start = ((bf16[64,9,4,128]{3,2,1,0:T(4,128)(2,1)}), bf16[64,9,4,128]{3,2,1,0:T(4,128)(2,1)S(1)}, u32[]{:S(2)}, u32[]{:S(2)}) async-start(bf16[64,9,4,128]{3,2,1,0:T(4,128)(2,1)} %bitcast.4), calls=%async_computation | async-start | bytes 1179648 | tf_op jit(solution)/shard_map/all_to_all | solution.py:196
  26.8 23.9 %copy-start = (bf16[3,256,512]{2,1,0:T(8,128)(2,1)S(1)}, bf16[3,256,512]{2,1,0:T(8,128)(2,1)}, u32[]{:S(2)}) copy-start(bf16[3,256,512]{2,1,0:T(8,128)(2,1)} %refs_0_.3) | copy-start | bytes 2359300
  26.8 24.9 %collective-permute-start.3 = (bf16[3,256,512]{2,1,0:T(8,128)(2,1)S(1)}, bf16[3,256,512]{2,1,0:T(8,128)(2,1)}, u32[]{:S(2)}, u32[]{:S(2)}) collective-permute-start(bf16[3,256,512]{2,1,0:T(8,128)(2,1)S(1)} %get-tuple-element.11.refs_1_), channel_id=1, source_target_pairs={{0,16},{8,56},{16,32},{24,8},{32,48},{40,24},{48,0},{56,40},{1,17}... | collective-permute-start | bytes 2359304 | tf_op jit(solution)/shard_map/ppermute | solution.py:192
  47.8 4.5 %collective-permute-start.2 = (bf16[64,9,4,128]{3,2,1,0:T(4,128)(2,1)S(1)}, bf16[64,9,4,128]{3,2,1,0:T(4,128)(2,1)S(1)}, u32[]{:S(2)}, u32[]{:S(2)}) collective-permute-start(bf16[64,9,4,128]{3,2,1,0:T(4,128)(2,1)S(1)} %all-to-all-done), channel_id=1, source_target_pairs={{0,8},{8,0},{1,9},{9,1},{2,10},{10,2},{3,11},{11,3},{4,12},{12,4},... | collective-permute-start | bytes 1769480 | tf_op jit(solution)/shard_map/ppermute | solution.py:198
  50.7 1.6 %copy-start.1 = (bf16[3,16384]{1,0:T(4,128)(2,1)S(1)}, bf16[3,16384]{1,0:T(4,128)(2,1)}, u32[]{:S(2)}) copy-start(bf16[3,16384]{1,0:T(4,128)(2,1)} %refs_3_.1) | copy-start | bytes 294916

commit v12 on v10

--- a/solution.py
+++ b/solution.py
@@ -12,7 +12,7 @@
 CROSS = tuple((2 * i + 1 - c, 2 * ((i + 1 - 2 * c) % X) + c) for i in range(X) for c in range(CORE))
 HELD = (((0, 0), (X - 1, 0), (X - 1, 1), (2, 0)), ((0, 1), (1, 1), (1, 0), (2, 1)))
 AXES = ("y2", "y1", "y0", "x", "c", "z2", "z1", "z0")
-GROUP = ("y0", "y1", "y2", "z0", "z1", "z2")
+GROUP = ("y0", "y1", "y2", "z1", "z0", "z2")
 VMEM = pl.BlockSpec(memory_space=pltpu.VMEM)
 SMEM = pl.BlockSpec(memory_space=pltpu.SMEM)
 ANY = pl.BlockSpec(memory_space=pl.ANY)
@@ -43,7 +43,7 @@
     rows, tiles, width = amplitudes.shape
     keep = kept_tiles.shape[1]
     split = amplitudes.reshape(rows, tiles, 2, 2, 2, width // Z // LANES, LANES)
-    split = split.transpose(0, 1, 4, 3, 2, 5, 6)
+    split = split.transpose(0, 1, 3, 4, 2, 5, 6)
     shape = (Z, rows * keep, width // Z // LANES, LANES)
     return pl.pallas_call(
         pick_kernel,

time: 85.6 us -> 85.9 us (level)
  starting transfers between devices: 31.8 us -> 32.7 us
  waiting for transfers between devices: 16.8 us -> 15.9 us
    all_to_all x1, waiting for transfers between devices: 16.2 us -> 15.3 us  [shards(): lax.all_to_all(outgoing, GROUP, split_axis=0, concat_axis=0, tiled=True)]
where the time goes in v12:
time: 85.9 us; the launch traced here: 85.5 us
  starting transfers between devices  32.7 us (38%)
  blocking collectives  30.3 us (35%)
  waiting for transfers between devices  15.9 us (19%)
  Pallas kernels  5.31 us (6%)
  local copies, waits for them, and re-layouts  1.07 us (1%)
    all_to_all x1, blocking collectives, shards(): lax.all_to_all(partial, GROUP + ('c',), split_axis=0, concat_axis=0, tile...  30.3 us
    all_to_all x1, waiting for transfers between devices, shards(): lax.all_to_all(outgoing, GROUP, split_axis=0, concat_axis=0, tiled=True)  15.3 us
    all_to_all x1, starting transfers between devices, shards(): lax.all_to_all(outgoing, GROUP, split_axis=0, concat_axis=0, tiled=True)  10.9 us
    ppermute x1, starting transfers between devices, shards(): first = lax.ppermute(integrals, ('x', 'c'), SAME)  8.75 us
    ppermute x1, starting transfers between devices, shards(): third = lax.ppermute(first, ('x', 'c'), SAME)  4.74 us
    ppermute x1, starting transfers between devices, shards(): second = lax.ppermute(integrals, ('x', 'c'), CROSS)  4.5 us
    pallas_call x3, Pallas kernels, call(): pl.pallas_call(kernel, out_shape=out_shape, in_specs=[SMEM] * len(scalars...  3.81 us
    ppermute x1, starting transfers between devices, shards(): theirs = lax.ppermute(mine, 'c', SWAP)  3.76 us
  transfers between devices with their start and end apart: 5, of which 2 were waited for; matrix products, arithmetic and copies ran while one was open for 1% of the time, Pallas kernels for 3%

profile of v12, /device:TPU:1, one launch (start us, length us, event | category | flops | bytes accessed | tf_op | source)
XLA Modules:
  0.0 85.5 jit_solution(15801804531310080870)
XLA Ops:
  0.0 4.5 %collective-permute-start.1 = (bf16[3,256,512]{2,1,0:T(8,128)(2,1)}, bf16[3,256,512]{2,1,0:T(8,128)(2,1)S(1)}, u32[]{:S(2)}, u32[]{:S(2)}) collective-permute-start(bf16[3,256,512]{2,1,0:T(8,128)(2,1)} %refs_0_.3), channel_id=1, source_target_pairs={{8,16},{0,56},{24,32},{16,8},{40,48},{32,24},{56,0},{48,40},{9,17}... | collective-permute-start | bytes 2359304 | tf_op jit(solution)/shard_map/ppermute | solution.py:184
  4.5 8.7 %collective-permute-start = (bf16[3,256,512]{2,1,0:T(8,128)(2,1)}, bf16[3,256,512]{2,1,0:T(8,128)(2,1)S(1)}, u32[]{:S(2)}, u32[]{:S(2)}) collective-permute-start(bf16[3,256,512]{2,1,0:T(8,128)(2,1)} %refs_0_.3), channel_id=1, source_target_pairs={{0,16},{8,56},{16,32},{24,8},{32,48},{40,24},{48,0},{56,40},{1,17}... | collective-permute-start | bytes 2359304 | tf_op jit(solution)/shard_map/ppermute | solution.py:183
  13.3 0.0 copy-start.2
  13.3 1.0 %copy.11 = bf16[3,8,2,2,2,4,128]{6,5,2,4,3,1,0:T(4,128)(2,1)S(1)} copy(bf16[3,8,2,2,2,4,128]{6,1,5,4,3,2,0:T(8,128)(2,1)} %bitcast.20) | data formatting | bytes 393216 | tf_op jit(solution)/shard_map/reshape | solution.py:45
  14.3 0.0 copy-done.2
  14.3 1.5 %shard_map.46 = bf16[2,2,2,2,2,2,9,4,128]{8,7,6,5,4,3,2,1,0:T(4,128)(2,1)} custom-call(s32[4,3]{1,0:T(4,128)S(1)} %copy-done.2, bf16[3,8,2,2,2,4,128]{6,5,4,3,2,1,0:T(4,128)(2,1)S(1)} %bitcast.17), custom_call_target="tpu_custom_call" | custom-call | flops 99999997952 | bytes 1000000 | tf_op jit(solution)/shard_map/pallas_call | solution.py:48
  15.8 10.9 %all-to-all-start = ((bf16[64,9,4,128]{3,2,1,0:T(4,128)(2,1)}), bf16[64,9,4,128]{3,2,1,0:T(4,128)(2,1)S(1)}, u32[]{:S(2)}, u32[]{:S(2)}) async-start(bf16[64,9,4,128]{3,2,1,0:T(4,128)(2,1)} %bitcast.4), calls=%async_computation | async-start | bytes 1179648 | tf_op jit(solution)/shard_map/all_to_all | solution.py:190
  26.8 0.0 copy-start
  26.8 0.0 collective-permute-done.1.b_ref
  26.8 0.0 collective-permute-done.a_ref
  26.8 4.7 %collective-permute-start.3 = (bf16[3,256,512]{2,1,0:T(8,128)(2,1)S(1)}, bf16[3,256,512]{2,1,0:T(8,128)(2,1)}, u32[]{:S(2)}, u32[]{:S(2)}) collective-permute-start(bf16[3,256,512]{2,1,0:T(8,128)(2,1)S(1)} %get-tuple-element.11.refs_1_), channel_id=1, source_target_pairs={{0,16},{8,56},{16,32},{24,8},{32,48},{40,24},{48,0},{56,40},{1,17}... | collective-permute-start | bytes 2359304 | tf_op jit(solution)/shard_map/ppermute | solution.py:186
  31.6 15.3 %all-to-all-done = bf16[64,9,4,128]{3,2,1,0:T(4,128)(2,1)S(1)} async-done(((bf16[64,9,4,128]{3,2,1,0:T(4,128)(2,1)}), bf16[64,9,4,128]{3,2,1,0:T(4,128)(2,1)S(1)}, u32[]{:S(2)}, u32[]{:S(2)}) %all-to-all-start) | async-done | bytes 589856 | tf_op jit(solution)/shard_map/all_to_all | solution.py:190
  46.9 3.8 %collective-permute-start.2 = (bf16[64,9,4,128]{3,2,1,0:T(4,128)(2,1)S(1)}, bf16[64,9,4,128]{3,2,1,0:T(4,128)(2,1)S(1)}, u32[]{:S(2)}, u32[]{:S(2)}) collective-permute-start(bf16[64,9,4,128]{3,2,1,0:T(4,128)(2,1)S(1)} %all-to-all-done), channel_id=1, source_target_pairs={{0,8},{8,0},{1,9},{9,1},{2,10},{10,2},{3,11},{11,3},{4,12},{12,4},... | collective-permute-start | bytes 1769480 | tf_op jit(solution)/shard_map/ppermute | solution.py:192
  50.6 0.0 copy-done
  50.7 0.0 copy-start.1
  50.7 0.9 %shard_map.48 = (bf16[3,3,64,512]{3,2,1,0:T(8,128)(2,1)S(1)}, f32[192,768]{1,0:T(8,128)S(1)}) custom-call(bf16[2304,128]{1,0:T(8,128)(2,1)S(1)} %bitcast.14, bf16[3,256,512]{2,1,0:T(8,128)(2,1)S(1)} %copy-done, bf16[3,256,512]{2,1,0:T(8,128)(2,1)S(1)} %get-tuple-element.11.refs_1_, bf16[3,256,512]{2,1,0:T(8,128)(2,1)S(1)} %get-tuple-element.12.refs_2_), custom_call_target="tpu_custom_call" | custom-call | flops 1000 | bytes 1000 | tf_op jit(solution)/shard_map/pallas_call | solution.py:63
  51.6 0.0 collective-permute-done.3.refs_4_
  51.6 0.6 collective-permute-done.2
  52.2 0.0 copy-done.1
  52.2 2.0 %shard_map.49 = (bf16[8,8,2,24,128]{4,3,2,1,0:T(8,128)(2,1)S(1)}, bf16[3,16384]{1,0:T(4,128)(2,1)S(1)}) custom-call(s32[1]{0:T(128)} %bitcast.1.core_ref, s32[1]{0:T(128)} %bitcast._.x_ref, bf16[3,3,64,512]{3,2,1,0:T(8,128)(2,1)S(1)} %get-tuple-element.13.mine_ref, f32[192,768]{1,0:T(8,128)S(1)} %get-tuple-element.14.near_ref, ...), custom_call_target="tpu_custom_call" | custom-call | flops 1000 | bytes 1000 | tf_op jit(solution)/shard_map/pallas_call | solution.py:63
  54.3 30.3 %all_to_all.10 = bf16[128,24,128]{2,1,0:T(8,128)(2,1)S(1)} all-to-all(bf16[128,24,128]{2,1,0:T(8,128)(2,1)S(1)} %bitcast.15), channel_id=1, replica_groups=mesh['y2'=2,'y1'=2,'y0'=2,'x'=4,'c'=2,'z2'=2,'z1'=2,'z0'=2] {'y0','y1','..., dimensions={0} | all-to-all | bytes 1572864 | tf_op jit(solution)/shard_map/all_to_all | solution.py:221
  84.5 0.1 reduce_sum.12
  84.7 0.8 shard_map.50
  (3 shorter events, 0.0 us)
Async XLA Ops:
  0.0 26.8 %collective-permute-start.1 = (bf16[3,256,512]{2,1,0:T(8,128)(2,1)}, bf16[3,256,512]{2,1,0:T(8,128)(2,1)S(1)}, u32[]{:S(2)}, u32[]{:S(2)}) collective-permute-start(bf16[3,256,512]{2,1,0:T(8,128)(2,1)} %refs_0_.3), channel_id=1, source_target_pairs={{8,16},{0,56},{24,32},{16,8},{40,48},{32,24},{56,0},{48,40},{9,17}... | collective-permute-start | bytes 2359304 | tf_op jit(solution)/shard_map/ppermute | solution.py:184
  4.5 22.3 %collective-permute-start = (bf16[3,256,512]{2,1,0:T(8,128)(2,1)}, bf16[3,256,512]{2,1,0:T(8,128)(2,1)S(1)}, u32[]{:S(2)}, u32[]{:S(2)}) collective-permute-start(bf16[3,256,512]{2,1,0:T(8,128)(2,1)} %refs_0_.3), channel_id=1, source_target_pairs={{0,16},{8,56},{16,32},{24,8},{32,48},{40,24},{48,0},{56,40},{1,17}... | collective-permute-start | bytes 2359304 | tf_op jit(solution)/shard_map/ppermute | solution.py:183
  13.3 1.0 %copy-start.2 = (s32[4,3]{1,0:T(4,128)S(1)}, s32[4,3]{1,0:T(4,128)}, u32[]{:S(2)}) copy-start(s32[4,3]{1,0:T(4,128)} %kept_ref.1) | copy-start | bytes 148
  15.8 31.1 %all-to-all-start = ((bf16[64,9,4,128]{3,2,1,0:T(4,128)(2,1)}), bf16[64,9,4,128]{3,2,1,0:T(4,128)(2,1)S(1)}, u32[]{:S(2)}, u32[]{:S(2)}) async-start(bf16[64,9,4,128]{3,2,1,0:T(4,128)(2,1)} %bitcast.4), calls=%async_computation | async-start | bytes 1179648 | tf_op jit(solution)/shard_map/all_to_all | solution.py:190
  26.8 23.9 %copy-start = (bf16[3,256,512]{2,1,0:T(8,128)(2,1)S(1)}, bf16[3,256,512]{2,1,0:T(8,128)(2,1)}, u32[]{:S(2)}) copy-start(bf16[3,256,512]{2,1,0:T(8,128)(2,1)} %refs_0_.3) | copy-start | bytes 2359300
  26.8 24.8 %collective-permute-start.3 = (bf16[3,256,512]{2,1,0:T(8,128)(2,1)S(1)}, bf16[3,256,512]{2,1,0:T(8,128)(2,1)}, u32[]{:S(2)}, u32[]{:S(2)}) collective-permute-start(bf16[3,256,512]{2,1,0:T(8,128)(2,1)S(1)} %get-tuple-element.11.refs_1_), channel_id=1, source_target_pairs={{0,16},{8,56},{16,32},{24,8},{32,48},{40,24},{48,0},{56,40},{1,17}... | collective-permute-start | bytes 2359304 | tf_op jit(solution)/shard_map/ppermute | solution.py:186
  46.9 5.4 %collective-permute-start.2 = (bf16[64,9,4,128]{3,2,1,0:T(4,128)(2,1)S(1)}, bf16[64,9,4,128]{3,2,1,0:T(4,128)(2,1)S(1)}, u32[]{:S(2)}, u32[]{:S(2)}) collective-permute-start(bf16[64,9,4,128]{3,2,1,0:T(4,128)(2,1)S(1)} %all-to-all-done), channel_id=1, source_target_pairs={{0,8},{8,0},{1,9},{9,1},{2,10},{10,2},{3,11},{11,3},{4,12},{12,4},... | collective-permute-start | bytes 1769480 | tf_op jit(solution)/shard_map/ppermute | solution.py:192
  50.7 1.6 %copy-start.1 = (bf16[3,16384]{1,0:T(4,128)(2,1)S(1)}, bf16[3,16384]{1,0:T(4,128)(2,1)}, u32[]{:S(2)}) copy-start(bf16[3,16384]{1,0:T(4,128)(2,1)} %refs_3_.1) | copy-start | bytes 294916
